TPU v7x, 32 devices: a whole 2x2x4 slice. The times are simulated.
32 devices in a mesh: rep: 2 (over y), fsdp: 16 (over z, x, core).
Axes of the slice: x: 2, y: 2, z: 4, core: 2. Of those that a mesh axis runs over, the one named last changes fastest.
Arguments:
- tokens: bfloat16 [32, 256, 1536], P(('rep', 'fsdp')), may hold values from -6 to 6
- doc_lengths: int32 [32, 8], P(('rep', 'fsdp')), may hold values from 1 to 128, 256 in all within a row
- pad_counts: int32 [32], P(('rep', 'fsdp')), may hold values from 0 to 63
- norm_in: bfloat16 [1536], P('fsdp'), may hold values from 0.25 to 1.75
- w_qkv: bfloat16 [1536, 4608], P('fsdp'), may hold values from -0.15625 to 0.15625
- kernel: float32 [16, 6, 11], replicated, may hold values from -1.2 to 1.2
- mixing: float32 [16, 2], replicated, may hold values from -4.2 to 4.2
- norm_heads: bfloat16 [1536], P('fsdp'), may hold values from 0.25 to 1.75
- w_out: bfloat16 [1536, 1536], P('fsdp'), may hold values from -0.15625 to 0.15625
- norm_mid: bfloat16 [1536], P('fsdp'), may hold values from 0.25 to 1.75
- w_gate: bfloat16 [1536, 4096], P('fsdp'), may hold values from -0.15625 to 0.15625
- w_up: bfloat16 [1536, 4096], P('fsdp'), may hold values from -0.15625 to 0.15625
- w_down: bfloat16 [4096, 1536], P('fsdp'), may hold values from -0.09375 to 0.09375
- cotangent: bfloat16 [32, 256, 1536], P(('rep', 'fsdp')), may hold values from -6 to 6
Outputs:
- layer_out: float32 [32, 256, 1536], P(('rep', 'fsdp'))
- grad_tokens: float32 [32, 256, 1536], P(('rep', 'fsdp'))
- grad_norm_in: float32 [1536], P('fsdp')
- grad_w_qkv: float32 [1536, 4608], P('fsdp')
- grad_kernel: float32 [16, 6, 11], replicated
- grad_mixing: float32 [16, 2], replicated
- grad_norm_heads: float32 [1536], P('fsdp')
- grad_w_out: float32 [1536, 1536], P('fsdp')
- grad_norm_mid: float32 [1536], P('fsdp')
- grad_w_gate: float32 [1536, 4096], P('fsdp')
- grad_w_up: float32 [1536, 4096], P('fsdp')
- grad_w_down: float32 [4096, 1536], P('fsdp')
Inputs may be any that keep to these rules, and one draw needn't show every extreme that they name: `doc_lengths`: in each row the 8 lengths sum to 256; the longest is 128.
All inputs are finite; a program needn't handle non-finite values.
Results may differ from a plain program's by a relative error of at most 0.019.
The roundings to bfloat16 on the way count: a program that leaves them out, or rounds other values in their place, can miss the bound.
Values may be sent and summed in bfloat16 or wider, within the bound.
A program may use at most 320 MiB of HBM per device.

v0:
```python
import jax
import jax.numpy as jnp
from jax import lax
from jax.sharding import PartitionSpec as P

NEG_FILL = -1e30
HIGH = lax.Precision.HIGHEST


def rms_norm(values_in, scaling):
    return (
        values_in
        * lax.rsqrt(jnp.mean(values_in * values_in, axis=-1, keepdims=True) + 1e-06)
        * scaling
    )


def group_norm(values_in, scaling):
    centred = values_in - jnp.mean(values_in, axis=-1, keepdims=True)
    scaled = centred * lax.rsqrt(jnp.mean(centred * centred, axis=-1, keepdims=True) + 1e-05)
    return scaled.reshape(values_in.shape[0], -1) * scaling


def convolve(scores, kernel):
    length = scores.shape[1]
    taps_query = kernel.shape[1]
    taps_key = kernel.shape[2]
    half_width = taps_key // 2
    padded = jnp.pad(scores, ((0, 0), (taps_query - 1, 0), (half_width, half_width)))
    summed = jnp.zeros_like(scores)
    for shift_q in range(taps_query):
        for shift_k in range(taps_key):
            start_q = taps_query - 1 - shift_q
            window = padded[:, start_q : start_q + length, shift_k : shift_k + length]
            summed = summed + kernel[:, shift_q, shift_k][:, None, None] * window
    return summed


def convolve_back(grad_conv, masked, kernel):
    length = masked.shape[1]
    taps_query = kernel.shape[1]
    taps_key = kernel.shape[2]
    half_width = taps_key // 2
    padded = jnp.pad(masked, ((0, 0), (taps_query - 1, 0), (half_width, half_width)))
    grad_padded = jnp.pad(grad_conv, ((0, 0), (0, taps_query - 1), (half_width, half_width)))
    grad_masked = jnp.zeros_like(masked)
    grad_taps = []
    for shift_q in range(taps_query):
        for shift_k in range(taps_key):
            start_q = taps_query - 1 - shift_q
            window = padded[:, start_q : start_q + length, shift_k : shift_k + length]
            grad_taps.append(jnp.sum(grad_conv * window, axis=(1, 2)))
            start_k = taps_key - 1 - shift_k
            back_window = grad_padded[:, shift_q : shift_q + length, start_k : start_k + length]
            grad_masked = grad_masked + kernel[:, shift_q, shift_k][:, None, None] * back_window
    grad_kern = jnp.stack(grad_taps, axis=1).reshape(kernel.shape)
    return (grad_masked, grad_kern)


def build_mask(doc_lengths, pad_count, length):
    places = jnp.arange(length, dtype=jnp.int32)
    doc_ends = jnp.cumsum(doc_lengths)
    segment = jnp.sum((places[:, None] >= doc_ends[None, :]).astype(jnp.int32), axis=1)
    live_end = length - pad_count
    same_doc = segment[:, None] == segment[None, :]
    causal = places[None, :] <= places[:, None]
    usable = (places[None, :] < live_end) | (places[None, :] == places[:, None])
    return same_doc & causal & usable


def outer_sum(left_rows, right_rows):
    return lax.dot_general(
        left_rows, right_rows, (((0,), (0,)), ((), ())), preferred_element_type=jnp.float32
    )


def back_product(grad_rows, weight_full):
    return lax.dot_general(
        grad_rows, weight_full, (((1,), (1,)), ((), ())), preferred_element_type=jnp.float32
    )


def attention_weights(norm_in, w_qkv, norm_heads, w_out):
    return (
        lax.all_gather(norm_in, "fsdp", axis=0, tiled=True),
        lax.all_gather(w_qkv, "fsdp", axis=0, tiled=True),
        lax.all_gather(norm_heads, "fsdp", axis=0, tiled=True),
        lax.all_gather(w_out, "fsdp", axis=0, tiled=True),
    )


def feed_weights(norm_mid, w_gate, w_up, w_down):
    return (
        lax.all_gather(norm_mid, "fsdp", axis=0, tiled=True),
        lax.all_gather(w_gate, "fsdp", axis=0, tiled=True),
        lax.all_gather(w_up, "fsdp", axis=0, tiled=True),
        lax.all_gather(w_down, "fsdp", axis=0, tiled=True),
    )


def per_device(
    tokens,
    doc_lengths,
    pad_counts,
    norm_in,
    w_qkv,
    kernel,
    mixing,
    norm_heads,
    w_out,
    norm_mid,
    w_gate,
    w_up,
    w_down,
    cotangent,
):
    inputs = tokens[0].astype(jnp.float32)
    length = inputs.shape[0]
    model_width = inputs.shape[1]
    head_count = kernel.shape[0]
    head_size = model_width // head_count
    pair_count = head_count // 2
    score_scale = head_size ** (-0.5)
    allowed = build_mask(doc_lengths[0], pad_counts[0], length)[None]
    kern_pairs = kernel.reshape(pair_count, 2, kernel.shape[1], kernel.shape[2])
    mix_pairs = mixing.reshape(pair_count, 2, 2)
    attn_set = attention_weights(norm_in, w_qkv, norm_heads, w_out)
    normed = rms_norm(inputs, attn_set[0].astype(jnp.float32)).astype(jnp.bfloat16)
    projected = jnp.dot(normed, attn_set[1], preferred_element_type=jnp.float32).astype(
        jnp.bfloat16
    )
    split_qkv = projected.reshape(length, 3, pair_count, 2, head_size).transpose(1, 2, 3, 0, 4)

    def pair_scores(queries, key_rows, kern_pair):
        raw_scores = (
            jnp.einsum("gie,gje->gij", queries, key_rows, preferred_element_type=jnp.float32)
            * score_scale
        )
        masked = jnp.where(allowed, raw_scores, 0.0)
        logits = jnp.where(allowed, convolve(masked, kern_pair), NEG_FILL)
        return (masked, logits)

    def pair_forward(pieces):
        queries, key_rows, value_rows, kern_pair, mix_pair = pieces
        masked, logits = pair_scores(queries, key_rows, kern_pair)
        row_peak = jnp.max(logits, axis=-1, keepdims=True)
        log_total = row_peak + jnp.log(jnp.sum(jnp.exp(logits - row_peak), axis=-1, keepdims=True))
        attn_probs = jnp.exp(logits - log_total)
        mixed_probs = jnp.einsum("og,gij->oij", mix_pair, attn_probs, precision=HIGH)
        output = jnp.einsum(
            "oij,oje->oie", mixed_probs, value_rows.astype(jnp.float32), precision=HIGH
        )
        return (output, log_total)

    attended_pairs, log_totals = lax.map(
        pair_forward, (split_qkv[0], split_qkv[1], split_qkv[2], kern_pairs, mix_pairs)
    )
    attended = attended_pairs.transpose(2, 0, 1, 3).reshape(length, head_count, head_size)
    gated_out = group_norm(attended, attn_set[2].astype(jnp.float32)).astype(jnp.bfloat16)
    residual = inputs + jnp.dot(gated_out, attn_set[3], preferred_element_type=jnp.float32)
    ffn_set = feed_weights(norm_mid, w_gate, w_up, w_down)
    normed_mid = rms_norm(residual, ffn_set[0].astype(jnp.float32)).astype(jnp.bfloat16)
    gate_pre = jnp.dot(normed_mid, ffn_set[1], preferred_element_type=jnp.float32)
    up_pre = jnp.dot(normed_mid, ffn_set[2], preferred_element_type=jnp.float32)
    sigmoid_gate = jax.nn.sigmoid(gate_pre)
    silu_gate = gate_pre * sigmoid_gate
    hidden = (silu_gate * up_pre).astype(jnp.bfloat16)
    layer_out = (residual + jnp.dot(hidden, ffn_set[3], preferred_element_type=jnp.float32))[None]
    ffn_again = feed_weights(norm_mid, w_gate, w_up, w_down)
    grad_y = cotangent[0]
    grad_w_down = outer_sum(hidden, grad_y)
    grad_hidden = back_product(grad_y, ffn_again[3])
    grad_gate = (
        grad_hidden * up_pre * sigmoid_gate * (1.0 + gate_pre * (1.0 - sigmoid_gate))
    ).astype(jnp.bfloat16)
    grad_up = (grad_hidden * silu_gate).astype(jnp.bfloat16)
    grad_w_gate = outer_sum(normed_mid, grad_gate)
    grad_w_up = outer_sum(normed_mid, grad_up)
    grad_mid = back_product(grad_gate, ffn_again[1]) + back_product(grad_up, ffn_again[2])
    mid_pull = jax.vjp(rms_norm, residual, ffn_again[0].astype(jnp.float32))[1]
    grad_residual_norm, grad_norm_mid = mid_pull(grad_mid)
    grad_residual = grad_y.astype(jnp.float32) + grad_residual_norm
    ffn_shards = (
        lax.psum_scatter(grad_norm_mid, "fsdp", scatter_dimension=0, tiled=True),
        lax.psum_scatter(grad_w_gate, "fsdp", scatter_dimension=0, tiled=True),
        lax.psum_scatter(grad_w_up, "fsdp", scatter_dimension=0, tiled=True),
        lax.psum_scatter(grad_w_down, "fsdp", scatter_dimension=0, tiled=True),
    )
    attn_again = attention_weights(norm_in, w_qkv, norm_heads, w_out)
    grad_branch = grad_residual.astype(jnp.bfloat16)
    grad_w_out = outer_sum(gated_out, grad_branch)
    grad_gated = back_product(grad_branch, attn_again[3])
    head_pull = jax.vjp(group_norm, attended, attn_again[2].astype(jnp.float32))[1]
    grad_attended, grad_norm_heads = head_pull(grad_gated)
    grad_att_pairs = (
        grad_attended.astype(jnp.bfloat16)
        .reshape(length, pair_count, 2, head_size)
        .transpose(1, 2, 0, 3)
    )

    def pair_backward(pieces):
        queries, key_rows, value_rows, kern_pair, mix_pair, log_total, grad_output = pieces
        masked, logits = pair_scores(queries, key_rows, kern_pair)
        attn_probs = jnp.exp(logits - log_total)
        mixed_probs = jnp.einsum("og,gij->oij", mix_pair, attn_probs, precision=HIGH)
        grad_wide = grad_output.astype(jnp.float32)
        grad_mixed = jnp.einsum(
            "oie,oje->oij", grad_wide, value_rows.astype(jnp.float32), precision=HIGH
        )
        grad_values = jnp.einsum("oij,oie->oje", mixed_probs, grad_wide, precision=HIGH)
        grad_mix = jnp.einsum("oij,gij->og", grad_mixed, attn_probs, precision=HIGH)
        grad_probs = jnp.einsum("og,oij->gij", mix_pair, grad_mixed, precision=HIGH)
        grad_logits = attn_probs * (
            grad_probs - jnp.sum(attn_probs * grad_probs, axis=-1, keepdims=True)
        )
        grad_conv = jnp.where(allowed, grad_logits, 0.0)
        grad_masked, grad_kern = convolve_back(grad_conv, masked, kern_pair)
        grad_raw = jnp.where(allowed, grad_masked, 0.0)
        grad_query = (
            jnp.einsum("gij,gje->gie", grad_raw, key_rows.astype(jnp.float32), precision=HIGH)
            * score_scale
        )
        grad_key = (
            jnp.einsum("gij,gie->gje", grad_raw, queries.astype(jnp.float32), precision=HIGH)
            * score_scale
        )
        return (
            grad_query.astype(jnp.bfloat16),
            grad_key.astype(jnp.bfloat16),
            grad_values.astype(jnp.bfloat16),
            grad_kern,
            grad_mix,
        )

    grads_query, grads_key, grads_value, grad_kern_pairs, grad_mix_pairs = lax.map(
        pair_backward,
        (
            split_qkv[0],
            split_qkv[1],
            split_qkv[2],
            kern_pairs,
            mix_pairs,
            log_totals,
            grad_att_pairs,
        ),
    )
    grad_qkv = (
        jnp.stack([grads_query, grads_key, grads_value])
        .transpose(3, 0, 1, 2, 4)
        .reshape(length, 3 * model_width)
    )
    grad_w_qkv = outer_sum(normed, grad_qkv)
    grad_normed = back_product(grad_qkv, attn_again[1])
    in_pull = jax.vjp(rms_norm, inputs, attn_again[0].astype(jnp.float32))[1]
    grad_inputs_norm, grad_norm_in = in_pull(grad_normed)
    grad_tokens = (grad_residual + grad_inputs_norm)[None]
    small_sums = lax.psum(
        (grad_kern_pairs.reshape(kernel.shape), grad_mix_pairs.reshape(mixing.shape)),
        ("rep", "fsdp"),
    )
    attn_shards = (
        lax.psum_scatter(grad_norm_in, "fsdp", scatter_dimension=0, tiled=True),
        lax.psum_scatter(grad_w_qkv, "fsdp", scatter_dimension=0, tiled=True),
        lax.psum_scatter(grad_norm_heads, "fsdp", scatter_dimension=0, tiled=True),
        lax.psum_scatter(grad_w_out, "fsdp", scatter_dimension=0, tiled=True),
    )
    summed = (
        lax.psum(ffn_shards[0].astype(jnp.bfloat16), "rep").astype(jnp.float32),
        lax.psum(ffn_shards[1].astype(jnp.bfloat16), "rep").astype(jnp.float32),
        lax.psum(ffn_shards[2].astype(jnp.bfloat16), "rep").astype(jnp.float32),
        lax.psum(ffn_shards[3].astype(jnp.bfloat16), "rep").astype(jnp.float32),
        lax.psum(attn_shards[0].astype(jnp.bfloat16), "rep").astype(jnp.float32),
        lax.psum(attn_shards[1].astype(jnp.bfloat16), "rep").astype(jnp.float32),
        lax.psum(attn_shards[2].astype(jnp.bfloat16), "rep").astype(jnp.float32),
        lax.psum(attn_shards[3].astype(jnp.bfloat16), "rep").astype(jnp.float32),
    )
    return (
        layer_out,
        grad_tokens,
        summed[4],
        summed[5],
        small_sums[0],
        small_sums[1],
        summed[6],
        summed[7],
        summed[0],
        summed[1],
        summed[2],
        summed[3],
    )


def solution(mesh):
    return jax.shard_map(
        per_device,
        mesh=mesh,
        in_specs=(
            P(("rep", "fsdp"), None, None),
            P(("rep", "fsdp"), None),
            P(("rep", "fsdp")),
            P("fsdp"),
            P("fsdp", None),
            P(),
            P(),
            P("fsdp"),
            P("fsdp", None),
            P("fsdp"),
            P("fsdp", None),
            P("fsdp", None),
            P("fsdp", None),
            P(("rep", "fsdp"), None, None),
        ),
        out_specs=(
            P(("rep", "fsdp"), None, None),
            P(("rep", "fsdp"), None, None),
            P("fsdp"),
            P("fsdp", None),
            P(),
            P(),
            P("fsdp"),
            P("fsdp", None),
            P("fsdp"),
            P("fsdp", None),
            P("fsdp", None),
            P("fsdp", None),
        ),
        check_vma=False,
    )
```

profile of v0, /device:TPU:0, one launch (start us, length us, event | category | flops | bytes accessed | tf_op | source)
XLA Modules:
  0.0 1785.2 jit_solution(17890398854368420141)
XLA Ops:
  14.1 65.2 %all-reduce.11 = (bf16[1536]{0:T(1024)(128)(2,1)S(1)}, bf16[1536]{0:T(1024)(128)(2,1)S(1)}, bf16[1536]{0:T(1024)(128)(2,1)S(1)}) all-reduce(bf16[1536]{0:T(1024)(128)(2,1)S(1)} %dynamic-update-slice, bf16[1536]{0:T(1024)(128)(2,1)S(1)} %dynamic-update-slice.1, ...), channel_id=1, replica_groups=mesh['rep'=2,'fsdp'=16] {'fsdp'}, use_global_device_ids=true, to_apply=%add.3 | all-reduce | flops 4608 | bytes 18432
  80.6 43.6 %all-gather.6.cloned.1.call-done = bf16[1536,4608]{1,0:T(8,128)(2,1)} async-done(((bf16[96,4608]{1,0:T(8,128)(2,1)}), bf16[1536,4608]{1,0:T(8,128)(2,1)}) %all-gather.6.cloned.1.call-update) | async-done | bytes 14155792 | tf_op jit(solution)/shard_map/all_gather | solution.py:86
  124.2 10.3 convolution_convert_fusion.1
  141.7 151.6 %while.36 = (s32[]{:T(128)}, f32[8,2,256,96]{2,3,1,0:T(8,128)S(1)}, f32[8,2,256,1]{2,1,3,0:T(2,128)}, f32[8,2,2]{2,1,0:T(2,128)S(1)}, f32[8,2,6,11]{1,3,2,0:T(8,...) while((s32[]{:T(128)}, f32[8,2,256,96]{2,3,1,0:T(8,128)S(1)}, ...), condition=%wide.region_6.7_spmd.clone, body=%wide.region_3.6_spmd.clone.sunk | while | flops 197787136 | bytes 5430225 | solution.py:155
  146.3 9.9 fusion.453
  165.2 9.9 fusion.453
  184.1 9.9 fusion.453
  203.0 9.9 fusion.453
  221.9 9.9 fusion.453
  240.8 9.9 fusion.453
  259.7 9.9 fusion.453
  278.6 9.9 fusion.453
  308.7 9.8 fusion.378
  318.5 62.4 %all-gather.12.cloned.1.call-done = bf16[1536,4096]{1,0:T(8,128)(2,1)} async-done(((bf16[96,4096]{1,0:T(8,128)(2,1)}), bf16[1536,4096]{1,0:T(8,128)(2,1)}) %all-gather.12.cloned.1.call-update) | async-done | bytes 12582928 | tf_op jit(solution)/shard_map/all_gather | solution.py:96
  381.0 9.5 fusion.379
  390.5 91.6 %all-gather.14.cloned.1.call-done = bf16[4096,1536]{1,0:T(8,128)(2,1)} async-done(((bf16[256,1536]{1,0:T(8,128)(2,1)}), bf16[4096,1536]{1,0:T(8,128)(2,1)}) %all-gather.14.cloned.1.call-update) | async-done | bytes 12582928 | tf_op jit(solution)/shard_map/all_gather | solution.py:97
  482.1 10.3 multiply_convert_fusion
  492.4 8.0 fusion.380
  500.5 7.7 multiply_reduce_fusion.66
  514.7 16.8 fusion.381
  531.6 14.7 fusion.382
  546.8 5.4 multiply_reduce_fusion.67
  555.1 13.8 fusion.360
  570.4 432.4 %while.37 = (s32[]{:T(128)}, bf16[8,2,256,96]{2,3,1,0:T(8,128)(2,1)}, bf16[8,2,256,96]{2,3,1,0:T(8,128)(2,1)}, bf16[8,2,256,96]{2,3,1,0:T(8,128)(2,1)}, f32[8,2,...) while((s32[]{:T(128)}, ...), condition=%wide.region_81.82_spmd.clone, body=%wide.region_13.81_spmd.clone.sunk | while | flops 566215232 | bytes 15503493 | solution.py:235
  573.5 8.6 subtract_exponential_fusion.5
  588.3 8.6 fusion.477
  626.4 8.6 subtract_exponential_fusion.5
  641.2 8.6 fusion.477
  679.5 8.6 subtract_exponential_fusion.5
  694.3 8.6 fusion.477
  732.4 8.6 subtract_exponential_fusion.5
  747.2 8.6 fusion.477
  785.4 8.6 subtract_exponential_fusion.5
  800.2 8.6 fusion.477
  838.4 8.6 subtract_exponential_fusion.5
  853.2 8.6 fusion.477
  891.5 8.6 subtract_exponential_fusion.5
  906.3 8.6 fusion.477
  944.5 8.6 subtract_exponential_fusion.5
  959.3 8.6 fusion.477
  1006.2 11.9 fusion.357
  1022.4 97.9 %reduce-scatter.12.cloned.1.call-done = f32[96,4096]{1,0:T(8,128)} async-done(((f32[1536,4096]{1,0:T(8,128)}), f32[96,4096]{1,0:T(8,128)}) %reduce-scatter.12.cloned.1.call-update) | async-done | bytes 1572880 | tf_op jit(solution)/shard_map/reduce_scatter | solution.py:186
  1122.8 245.4 %reduce-scatter.14.cloned.1.call-done = f32[256,1536]{1,0:T(8,128)} async-done(((f32[4096,1536]{1,0:T(8,128)}), f32[256,1536]{1,0:T(8,128)}) %reduce-scatter.14.cloned.1.call-update) | async-done | bytes 1572880 | tf_op jit(solution)/shard_map/reduce_scatter | solution.py:187
  1370.6 270.6 %reduce-scatter.6.cloned.1.call-done = f32[96,4608]{1,0:T(8,128)} async-done(((f32[1536,4608]{1,0:T(8,128)}), f32[96,4608]{1,0:T(8,128)}) %reduce-scatter.6.cloned.1.call-update) | async-done | bytes 1769488 | tf_op jit(solution)/shard_map/reduce_scatter | solution.py:263
  1644.3 12.0 fusion.344
  1656.4 58.4 %all-reduce.10 = (bf16[1536]{0:T(1024)(128)(2,1)S(1)}, bf16[1536]{0:T(1024)(128)(2,1)S(1)}, bf16[1536]{0:T(1024)(128)(2,1)S(1)}) all-reduce(f32[1536]{0:T(1024)S(1)} %get-tuple-element.572, f32[1536]{0:T(1024)S(1)} %get-tuple-element.783, f32[1536]{0:T(1024)S(1)} %copy-done.30), channel_id=2, replica_groups=mesh['rep'=2,'fsdp'=16] {'fsdp'}, use_global_device_ids=true, to_apply=%region_84.85.clone | all-reduce | flops 4608 | bytes 27648
  1720.6 37.7 %all-reduce.9 = (f32[16,6,11]{2,0,1:T(8,128)S(1)}, f32[16,2]{0,1:T(2,128)}) all-reduce(f32[16,6,11]{2,0,1:T(8,128)S(1)} %bitcast.741, f32[16,2]{0,1:T(2,128)S(1)} %copy.247), channel_id=1, replica_groups=mesh['rep'=2,'fsdp'=16] {'rep','fsdp'}, use_global_device_ids=true, to_apply=%region_88.89 | all-reduce | flops 1088 | bytes 8704 | tf_op jit(solution)/shard_map/psum | solution.py:257
  1763.2 7.9 fusion.336
  (980 shorter events, 429.8 us)
Async XLA Ops:
  7.2 3.5 copy-start.33
  7.2 3.6 copy-start.25
  7.2 117.0 %all-gather.6.cloned.1.call-start = ((), (), s32[]{:S(2)}) async-start(), calls=%async_computation.5 | async-start | bytes 15040512 | tf_op jit(solution)/shard_map/all_gather | solution.py:86
  7.9 4.2 copy-start.32
  7.9 5.4 copy-start.34
  8.0 5.6 copy-start.35
  8.0 5.9 copy-start.36
  8.0 294.8 %all-gather.8.cloned.1.call-start = ((), (), s32[]{:S(2)}) async-start(), calls=%async_computation.6 | async-start | bytes 5013504 | tf_op jit(solution)/shard_map/all_gather | solution.py:88
  8.7 70.6 %copy-start.6 = (bf16[1,256,1536]{2,1,0:T(8,128)(2,1)S(1)}, bf16[1,256,1536]{2,1,0:T(8,128)(2,1)}, u32[]{:S(2)}) copy-start(bf16[1,256,1536]{2,1,0:T(8,128)(2,1)} %param.18) | copy-start | bytes 2359300
  8.7 300.0 %all-gather.10.cloned.1.call-start = ((), (), s32[]{:S(2)}) async-start(), calls=%async_computation.7 | async-start | bytes 13369344 | tf_op jit(solution)/shard_map/all_gather | solution.py:95
  9.5 70.2 %copy-start.37 = (s32[1,8]{1,0:T(1,128)S(1)}, s32[1,8]{1,0:T(1,128)}, u32[]{:S(2)}) copy-start(s32[1,8]{1,0:T(1,128)} %param.19) | copy-start | bytes 100
  9.5 371.5 %all-gather.12.cloned.1.call-start = ((), (), s32[]{:S(2)}) async-start(), calls=%async_computation.8 | async-start | bytes 13369344 | tf_op jit(solution)/shard_map/all_gather | solution.py:96
  10.1 472.0 %all-gather.14.cloned.1.call-start = ((), (), s32[]{:S(2)}) async-start(), calls=%async_computation.9 | async-start | bytes 13369344 | tf_op jit(solution)/shard_map/all_gather | solution.py:97
  10.6 1007.5 %reduce-scatter.8.cloned.1.call-start = ((), (), s32[]{:S(2)}) async-start(), calls=%async_computation.11 | async-start | bytes 10027008 | tf_op jit(solution)/shard_map/reduce_scatter | solution.py:265
  79.4 55.1 %copy-start.21 = (f32[1536]{0:T(1024)}, f32[1536]{0:T(1024)S(1)}, u32[]{:S(2)}) copy-start(f32[1536]{0:T(1024)S(1)} %convert_element_type.144) | copy-start | bytes 18436
  79.6 54.9 %copy-start.28 = (f32[256]{0:T(256)}, f32[256]{0:T(256)S(1)}, u32[]{:S(2)}) copy-start(f32[256]{0:T(256)S(1)} %fusion.345) | copy-start | bytes 3076
  79.6 54.9 %copy-start.26 = (f32[256]{0:T(256)}, f32[256]{0:T(256)S(1)}, u32[]{:S(2)}) copy-start(f32[256]{0:T(256)S(1)} %fusion.372) | copy-start | bytes 3076
  293.9 0.9 copy-start.8
  302.7 4.6 copy-start.2
  307.4 1.1 copy-start.9
  308.7 72.3 %copy-start.4 = (bf16[256,1536]{1,0:T(8,128)(2,1)}, bf16[256,1536]{1,0:T(8,128)(2,1)S(1)}, u32[]{:S(2)}) copy-start(bf16[256,1536]{1,0:T(8,128)(2,1)S(1)} %multiply_convert_fusion.3) | copy-start | bytes 2359300
  318.5 163.5 %copy-start.13 = (bf16[1,256,1536]{2,1,0:T(8,128)(2,1)S(1)}, bf16[1,256,1536]{2,1,0:T(8,128)(2,1)}, u32[]{:S(2)}) copy-start(bf16[1,256,1536]{2,1,0:T(8,128)(2,1)} %param.31) | copy-start | bytes 2359300
  492.4 8.0 copy-start.16
  492.4 8.1 copy-start.15
  492.4 8.1 copy-start.10
  500.5 7.7 copy-start.14
  508.2 1.4 copy-start.3
  509.6 37.2 %copy-start = (f32[256,1536]{1,0:T(8,128)}, f32[256,1536]{1,0:T(8,128)S(1)}, u32[]{:S(2)}) copy-start(f32[256,1536]{1,0:T(8,128)S(1)} %fusion.349) | copy-start | bytes 4718596
  514.7 505.4 %reduce-scatter.10.cloned.1.call-start = ((), (), s32[]{:S(2)}) async-start(), calls=%async_computation.12 | async-start | bytes 26738688 | tf_op jit(solution)/shard_map/reduce_scatter | solution.py:185
  531.5 588.8 %reduce-scatter.12.cloned.1.call-start = ((), (), s32[]{:S(2)}) async-start(), calls=%async_computation.13 | async-start | bytes 26738688 | tf_op jit(solution)/shard_map/reduce_scatter | solution.py:186
  546.3 821.8 %reduce-scatter.14.cloned.1.call-start = ((), (), s32[]{:S(2)}) async-start(), calls=%async_computation.14 | async-start | bytes 26738688 | tf_op jit(solution)/shard_map/reduce_scatter | solution.py:187
  568.9 1072.2 %reduce-scatter.6.cloned.1.call-start = ((), (), s32[]{:S(2)}) async-start(), calls=%async_computation.10 | async-start | bytes 30081024 | tf_op jit(solution)/shard_map/reduce_scatter | solution.py:263
  569.0 1.4 copy-start.24
  569.0 1.4 copy-start.31
  1002.8 3.4 copy-start.7
  1002.8 3.4 copy-start.22
  1002.8 3.3 copy-start.27
  1004.8 1.4 copy-start.5
  1018.1 752.9 %all-reduce.16.cloned.1.call-start = ((), (), s32[]{:S(2)}) async-start(), calls=%async_computation.15 | async-start | bytes 7077888 | tf_op jit(solution)/shard_map/psum | solution.py:273
  1644.3 12.1 copy-start.30
  1644.3 115.7 %copy-start.29 = (f32[256]{0:T(256)S(1)}, f32[256]{0:T(256)}, u32[]{:S(2)}) copy-start(f32[256]{0:T(256)} %copy-done.28) | copy-start | bytes 3076
  1644.3 115.7 %copy-start.1 = (f32[256,1536]{1,0:T(8,128)S(1)}, f32[256,1536]{1,0:T(8,128)}, u32[]{:S(2)}) copy-start(f32[256,1536]{1,0:T(8,128)} %copy-done) | copy-start | bytes 4718596
  1760.0 3.1 copy-start.11
  1760.1 3.1 copy-start.12
  1771.0 2.6 copy-start.20
  1771.0 3.5 copy-start.19
  1773.7 2.2 copy-start.18
  1775.8 1.3 copy-start.17
  (1 other events, 0.5 us)
Sparse Core Ops, SparseCore 0:
  10.3 113.8 all-gather.5
  126.5 51.5 all-gather.7
  180.4 99.4 all-gather.9
  282.0 98.9 all-gather.11
  383.1 98.9 all-gather.13
  514.8 109.4 reduce-scatter.7
  629.0 243.7 reduce-scatter.9
  877.4 242.8 reduce-scatter.11
  1125.0 243.0 reduce-scatter.13
  1372.8 268.3 reduce-scatter.5
  1644.5 94.9 all-reduce.15
where the time goes:
time: 1800 us; the launch traced here: 1790 us
  waiting for transfers between devices  815 us (45%)
  other arithmetic  340 us (19%)
  matrix products  324 us (18%)
  blocking collectives  166 us (9%)
  local copies, waits for them, and re-layouts  112 us (6%)
    reduce_scatter x1, waiting for transfers between devices, per_device(): lax.psum_scatter(grad_w_qkv, 'fsdp', scatter_dimension=0, tiled=True)  271 us
    reduce_scatter x1, waiting for transfers between devices, per_device(): lax.psum_scatter(grad_w_down, 'fsdp', scatter_dimension=0, tiled=True)  245 us
    unnamed x2, blocking collectives  124 us
    reduce_scatter x1, waiting for transfers between devices, per_device(): lax.psum_scatter(grad_w_up, 'fsdp', scatter_dimension=0, tiled=True)  97.9 us
    all_gather x1, waiting for transfers between devices, feed_weights(): lax.all_gather(w_down, 'fsdp', axis=0, tiled=True)  91.6 us
    reduce_max x8, other arithmetic, pair_forward(): row_peak = jnp.max(logits, axis=-1, keepdims=True)  79.4 us
    exp x8, other arithmetic, pair_backward(): attn_probs = jnp.exp(logits - log_total)  69.2 us
    select_n x8, other arithmetic, pair_backward(): grad_raw = jnp.where(allowed, grad_masked, 0.0)  68.7 us
  transfers between devices with their start and end apart: 11, of which 6 were waited for; matrix products, arithmetic and copies ran while one was open for 41% of the time, Pallas kernels for 0%

commit v1 on v0

--- a/solution.py
+++ b/solution.py
@@ -1,10 +1,325 @@
+import functools
+
 import jax
 import jax.numpy as jnp
 from jax import lax
+from jax.experimental import pallas as pl
+from jax.experimental.pallas import tpu as pltpu
 from jax.sharding import PartitionSpec as P
 
+F32 = jnp.float32
+BF16 = jnp.bfloat16
 NEG_FILL = -1e30
-HIGH = lax.Precision.HIGHEST
+MESH = pl.DeviceIdType.MESH
+PLANE = 4
+GROUP = 8
+SIDE = 256
+SLOTS = 4
+QKV = 640
+
+
+class Place:
+    def __init__(self, planes):
+        self.planes = planes
+        self.y = lax.axis_index("rep")
+        self.f = lax.axis_index("fsdp")
+        self.g = lax.div(self.f, PLANE)
+        self.s = lax.rem(self.f, PLANE)
+        self.x = lax.div(self.s, 2)
+        self.c = lax.rem(self.s, 2)
+        self.slot = self.y * PLANE + self.s
+        self.pair = self.y * 4 + self.c * 2 + self.x
+
+    def dev(self, y, x, c):
+        return (y, self.g * PLANE + x * 2 + c)
+
+    def sib(self):
+        return self.dev(self.y, self.x, 1 - self.c)
+
+    def xn(self):
+        return self.dev(self.y, 1 - self.x, self.c)
+
+    def yn(self):
+        return self.dev(1 - self.y, self.x, self.c)
+
+    def plane_dev(self, g):
+        return (self.y, g * PLANE + self.s)
+
+    def row(self, dy, dx, dc):
+        y = self.y + dy - 2 * dy * self.y
+        x = self.x + dx - 2 * dx * self.x
+        c = self.c + dc - 2 * dc * self.c
+        return y * 4 + x * 2 + c
+
+    def greet(self):
+        sem = pltpu.get_barrier_semaphore()
+        n = self.planes * PLANE
+        for d in range(1, n):
+            pl.semaphore_signal(sem, inc=1, device_id=(self.y, lax.rem(self.f + d, n)), device_id_type=MESH)
+        for s in range(PLANE):
+            pl.semaphore_signal(sem, inc=1, device_id=(1 - self.y, self.g * PLANE + s), device_id_type=MESH)
+        pl.semaphore_wait(sem, n - 1 + PLANE)
+
+
+def remote(src, dst, send, recv, dev):
+    return pltpu.make_async_remote_copy(
+        src_ref=src, dst_ref=dst, send_sem=send, recv_sem=recv, device_id=dev, device_id_type=MESH
+    )
+
+
+class Gather:
+    SENDS = 14
+    RECVS = 14
+
+    def __init__(self, me, own, buf, send, recv, local):
+        self.me, self.own, self.buf = me, own, buf
+        self.send, self.recv, self.local = send, recv, local
+        self.half = own.shape[0] // 2
+        self.sent = []
+
+    def _own(self, h):
+        return self.own.at[pl.ds(h * self.half, self.half)]
+
+    def _blk(self, row, h):
+        return self.buf.at[row, pl.ds(h * self.half, self.half)]
+
+    def _go(self, src, row, h, kind, dev):
+        cp = remote(src, self._blk(row, h), self.send.at[len(self.sent)], self.recv.at[kind * 2 + h], dev)
+        cp.start()
+        self.sent.append(cp)
+
+    def _await(self, row, h, kind):
+        b = self._blk(row, h)
+        remote(b, b, self.send.at[0], self.recv.at[kind * 2 + h], self.me.sib()).wait_recv()
+
+    def start(self):
+        me = self.me
+        self.rows = [me.row(0, 0, 1), me.row(0, 1, 0), me.row(1, 0, 0), me.row(1, 1, 0), me.row(0, 1, 1), me.row(1, 0, 1), me.row(1, 1, 1)]
+        self.here = pltpu.make_async_copy(self.own, self.buf.at[me.slot], self.local)
+        self.here.start()
+        self._go(self._own(0), me.slot, 0, 1, me.xn())
+        self._go(self._own(1), me.slot, 1, 2, me.yn())
+        self._go(self._own(0), me.slot, 0, 0, me.sib())
+        self._go(self._own(1), me.slot, 1, 0, me.sib())
+        self._go(self._own(1), me.slot, 1, 1, me.xn())
+        self._go(self._own(0), me.slot, 0, 2, me.yn())
+
+    def relay(self):
+        me, rows = self.me, self.rows
+        self._await(rows[1], 0, 1)
+        self._go(self._blk(rows[1], 0), rows[1], 0, 3, me.yn())
+        self._go(self._blk(rows[1], 0), rows[1], 0, 4, me.sib())
+        self._await(rows[2], 1, 2)
+        self._go(self._blk(rows[2], 1), rows[2], 1, 3, me.xn())
+        self._go(self._blk(rows[2], 1), rows[2], 1, 5, me.sib())
+
+    def share(self):
+        me, rows = self.me, self.rows
+        self._await(rows[1], 1, 1)
+        self._go(self._blk(rows[1], 1), rows[1], 1, 4, me.sib())
+        self._await(rows[2], 0, 2)
+        self._go(self._blk(rows[2], 0), rows[2], 0, 5, me.sib())
+
+    def last(self):
+        me, rows = self.me, self.rows
+        for h in (0, 1):
+            self._await(rows[3], h, 3)
+            self._go(self._blk(rows[3], h), rows[3], h, 6, me.sib())
+
+    def finish(self):
+        for kind in (0, 4, 5, 6):
+            for h in (0, 1):
+                self._await(self.rows[kind], h, kind)
+        for cp in self.sent:
+            cp.wait_send()
+        self.here.wait()
+
+
+class Scatter:
+    SENDS = 10
+    RECVS = 10
+
+    @staticmethod
+    def scratch(rows, width):
+        return [
+            pltpu.VMEM((2, rows, width), BF16),
+            pltpu.VMEM((4, rows, width), BF16),
+            pltpu.VMEM((2, rows // 2, width), BF16),
+            pltpu.VMEM((2, rows, width), BF16),
+            pltpu.SemaphoreType.DMA((Scatter.SENDS,)),
+            pltpu.SemaphoreType.DMA((Scatter.RECVS,)),
+        ]
+
+    def __init__(self, me, out, red, diag, near, send, recv):
+        self.me, self.out, self.red, self.diag, self.near = me, out, red, diag, near
+        self.send, self.recv = send, recv
+        self.half = diag.shape[1]
+
+    def _sib(self, k):
+        return remote(self.out.at[lax.rem(k, 2)], self.red.at[k], self.send.at[k], self.recv.at[k], self.me.sib())
+
+    def put_sib(self, k, value):
+        @pl.when(k >= 2)
+        def _():
+            self._sib(k - 2).wait_send()
+
+        self.out[lax.rem(k, 2)] = value.astype(BF16)
+        self._sib(k).start()
+
+    def put_self(self, k, value):
+        self._sib(k).wait_recv()
+        self.red[k] = (value + self.red[k].astype(F32)).astype(BF16)
+
+    def _copy(self, name):
+        h, me = self.half, self.me
+        lo, hi = pl.ds(0, h), pl.ds(h, h)
+        src, dst, i, dev = {
+            "da": (self.red.at[0, lo], self.diag.at[0], 4, me.xn()),
+            "db": (self.red.at[0, hi], self.diag.at[1], 5, me.yn()),
+            "xa": (self.red.at[1, lo], self.near.at[0, lo], 6, me.xn()),
+            "xb": (self.red.at[1, hi], self.near.at[0, hi], 7, me.xn()),
+            "ya": (self.red.at[2, lo], self.near.at[1, lo], 8, me.yn()),
+            "yb": (self.red.at[2, hi], self.near.at[1, hi], 9, me.yn()),
+        }[name]
+        return remote(src, dst, self.send.at[i], self.recv.at[i], dev)
+
+    def push(self, i):
+        @pl.when(i == 1)
+        def _():
+            self._copy("da").start()
+            self._copy("db").start()
+
+        @pl.when(i == 3)
+        def _():
+            self._copy("xa").start()
+
+        @pl.when(i == 5)
+        def _():
+            self._copy("yb").start()
+
+    def turn(self):
+        h = self.half
+        self._copy("db").wait_recv()
+        self.red[1, h:] = (self.red[1, h:].astype(F32) + self.diag[1].astype(F32)).astype(BF16)
+        self._copy("xb").start()
+        self._copy("da").wait_recv()
+        self.red[2, :h] = (self.red[2, :h].astype(F32) + self.diag[0].astype(F32)).astype(BF16)
+        self._copy("ya").start()
+
+    def arrive(self):
+        for name in ("xa", "xb", "ya", "yb"):
+            self._copy(name).wait_recv()
+
+    def total(self, at):
+        return self.red[3, at].astype(F32) + self.near[0, at].astype(F32) + self.near[1, at].astype(F32)
+
+    def finish(self):
+        for k in (2, 3):
+            self._sib(k).wait_send()
+        for name in ("da", "db", "xa", "xb", "ya", "yb"):
+            self._copy(name).wait_send()
+
+
+class Chain:
+    def __init__(self, me, blocks, send, recv):
+        self.me, self.blocks, self.send, self.recv = me, blocks, send, recv
+
+    def _copy(self, b, way, hop):
+        to = self.me.g + 1 if way == 0 else self.me.g - 1
+        return remote(self.blocks(b), self.blocks(b), self.send.at[way, hop], self.recv.at[b], self.me.plane_dev(to))
+
+    def _each(self, hop, act):
+        g, z = self.me.g, self.me.planes
+        for way, b, have, more in ((0, g - hop, g - hop >= 0, g + 1 < z), (1, g + hop, g + hop < z, g >= 1)):
+            act(way, b, have, more)
+
+    def hop(self, hop):
+        def act(way, b, have, more):
+            @pl.when(have)
+            def _():
+                if hop > 0:
+                    self._copy(b, way, hop).wait_recv()
+
+                @pl.when(more)
+                def _():
+                    self._copy(b, way, hop).start()
+
+        self._each(hop, act)
+
+    def finish(self):
+        for hop in range(self.me.planes):
+
+            def act(way, b, have, more):
+                @pl.when(jnp.logical_and(have, more))
+                def _():
+                    self._copy(b, way, hop).wait_send()
+
+            self._each(hop, act)
+
+
+def order(me, i):
+    k = lax.div(i, 2)
+    dx = 1 - lax.div(k, 2)
+    dy = 1 - lax.rem(k, 2)
+    dc = 1 - lax.rem(i, 2)
+    return me.row(dy, dx, dc), k
+
+
+def strips(length, body, strip=64):
+    def one(i, carry):
+        body(pl.ds(pl.multiple_of(i * strip, strip), strip))
+        return carry
+
+    lax.fori_loop(0, length // strip, one, 0)
+
+
+def lanes(rows, width):
+    return lax.broadcasted_iota(jnp.int32, (rows, width), 1)
+
+
+def nt(a, b):
+    return lax.dot_general(a, b, (((1,), (1,)), ((), ())), preferred_element_type=F32)
+
+
+def tn(a, b):
+    return lax.dot_general(a, b, (((0,), (0,)), ((), ())), preferred_element_type=F32)
+
+
+def nn(a, b):
+    return jnp.dot(a, b, preferred_element_type=F32)
+
+
+def head_lanes(rows, dh):
+    at = lanes(rows, SIDE)
+    return at < dh, (at >= dh) & (at < 2 * dh)
+
+
+def allowed_mask(length, ends):
+    i = lax.broadcasted_iota(jnp.int32, (length, length), 0)
+    j = lax.broadcasted_iota(jnp.int32, (length, length), 1)
+    return (i >= j) & (i.astype(F32) < ends)
+
+
+def mix_lanes(mix_ref, pair, g, dh):
+    at = lanes(1, SIDE)
+    m0, m1 = mix_ref[2 * pair, g], mix_ref[2 * pair + 1, g]
+    return jnp.where(at < dh, m0, jnp.where(at < 2 * dh, m1, 0.0))
+
+
+def head_stats(value, dh, h0, h1):
+    m0 = jnp.sum(jnp.where(h0, value, 0.0), axis=-1, keepdims=True) / dh
+    m1 = jnp.sum(jnp.where(h1, value, 0.0), axis=-1, keepdims=True) / dh
+    return jnp.where(h0, m0, jnp.where(h1, m1, 0.0))
+
+
+def band(kern_ref, head, a, taps_q, taps_k, length, flip):
+    r = lax.broadcasted_iota(jnp.int32, (length, length), 0)
+    c = lax.broadcasted_iota(jnp.int32, (length, length), 1)
+    diff = (c - r) if flip else (r - c)
+    acc = jnp.zeros((length, length), F32)
+    for b in range(taps_k):
+        acc = jnp.where(diff == b - taps_k // 2, kern_ref[(head * taps_q + a) * taps_k + b], acc)
+    return acc
 
 
 def rms_norm(values_in, scaling):
@@ -146,9 +461,9 @@
         row_peak = jnp.max(logits, axis=-1, keepdims=True)
         log_total = row_peak + jnp.log(jnp.sum(jnp.exp(logits - row_peak), axis=-1, keepdims=True))
         attn_probs = jnp.exp(logits - log_total)
-        mixed_probs = jnp.einsum("og,gij->oij", mix_pair, attn_probs, precision=HIGH)
+        mixed_probs = jnp.einsum("og,gij->oij", mix_pair, attn_probs, precision=lax.Precision.HIGHEST)
         output = jnp.einsum(
-            "oij,oje->oie", mixed_probs, value_rows.astype(jnp.float32), precision=HIGH
+            "oij,oje->oie", mixed_probs, value_rows.astype(jnp.float32), precision=lax.Precision.HIGHEST
         )
         return (output, log_total)
 
@@ -202,14 +517,14 @@
         queries, key_rows, value_rows, kern_pair, mix_pair, log_total, grad_output = pieces
         masked, logits = pair_scores(queries, key_rows, kern_pair)
         attn_probs = jnp.exp(logits - log_total)
-        mixed_probs = jnp.einsum("og,gij->oij", mix_pair, attn_probs, precision=HIGH)
+        mixed_probs = jnp.einsum("og,gij->oij", mix_pair, attn_probs, precision=lax.Precision.HIGHEST)
         grad_wide = grad_output.astype(jnp.float32)
         grad_mixed = jnp.einsum(
-            "oie,oje->oij", grad_wide, value_rows.astype(jnp.float32), precision=HIGH
+            "oie,oje->oij", grad_wide, value_rows.astype(jnp.float32), precision=lax.Precision.HIGHEST
         )
-        grad_values = jnp.einsum("oij,oie->oje", mixed_probs, grad_wide, precision=HIGH)
-        grad_mix = jnp.einsum("oij,gij->og", grad_mixed, attn_probs, precision=HIGH)
-        grad_probs = jnp.einsum("og,oij->gij", mix_pair, grad_mixed, precision=HIGH)
+        grad_values = jnp.einsum("oij,oie->oje", mixed_probs, grad_wide, precision=lax.Precision.HIGHEST)
+        grad_mix = jnp.einsum("oij,gij->og", grad_mixed, attn_probs, precision=lax.Precision.HIGHEST)
+        grad_probs = jnp.einsum("og,oij->gij", mix_pair, grad_mixed, precision=lax.Precision.HIGHEST)
         grad_logits = attn_probs * (
             grad_probs - jnp.sum(attn_probs * grad_probs, axis=-1, keepdims=True)
         )
@@ -217,11 +532,11 @@
         grad_masked, grad_kern = convolve_back(grad_conv, masked, kern_pair)
         grad_raw = jnp.where(allowed, grad_masked, 0.0)
         grad_query = (
-            jnp.einsum("gij,gje->gie", grad_raw, key_rows.astype(jnp.float32), precision=HIGH)
+            jnp.einsum("gij,gje->gie", grad_raw, key_rows.astype(jnp.float32), precision=lax.Precision.HIGHEST)
             * score_scale
         )
         grad_key = (
-            jnp.einsum("gij,gie->gje", grad_raw, queries.astype(jnp.float32), precision=HIGH)
+            jnp.einsum("gij,gie->gje", grad_raw, queries.astype(jnp.float32), precision=lax.Precision.HIGHEST)
             * score_scale
         )
         return (
@@ -290,39 +605,946 @@
     )
 
 
+def forward_kernel(cfg, *refs):
+    (tok, ct, w_a, w_b, w_d, w_o, meta, kern, mix,
+     tok_all, ct_all, a_all, b_all, d_all, o_all, nrm_all, qkv_all, p_all, m_all, gated_all, mid_all, resid, gains, ends,
+     x_v, wa_v, wo_v, t_v, cat_v, shift_v, qkv_v, p_v, m_v, gated_v, meta_v, mid_v, tok_v,
+     out_v, red, diag, near, rs_send, rs_recv,
+     g_send, g_recv, g_loc, a_send, a_recv, ch_send, ch_recv, o_send, o_recv, meta_send, meta_recv, loc, row_in, row_out) = refs
+    planes, dh, taps_q, taps_k = cfg["planes"], cfg["dh"], cfg["kq"], cfg["kk"]
+    length, width = tok.shape
+    per_pair = o_all.shape[0]
+    scale = dh ** (-0.5)
+    me = Place(planes)
+    me.greet()
+
+    def first(src, dst_all, base):
+        cps = []
+        for d in range(1, PLANE):
+            s = lax.rem(me.s + d, PLANE)
+            cp = remote(src.at[s], dst_all.at[me.f], a_send.at[base + d], a_recv.at[base + d], (me.y, me.g * PLANE + s))
+            cp.start()
+            cps.append(cp)
+        own = pltpu.make_async_copy(src.at[me.s], dst_all.at[me.f], a_send.at[base])
+        own.start()
+        return cps, own
+
+    def first_wait(src, dst_all, base, own):
+        for d in range(1, PLANE):
+            s = lax.rem(me.s - d + PLANE, PLANE)
+            blk = dst_all.at[me.g * PLANE + s]
+            remote(blk, blk, a_send.at[base + d], a_recv.at[base + d], me.sib()).wait_recv()
+        own.wait()
+
+    meta_sent = []
+    for d in range(1, GROUP):
+        to = lax.rem(me.slot + d, GROUP)
+        cp = remote(
+            meta, meta_v.at[me.slot], meta_send.at[d], meta_recv.at[d],
+            (lax.div(to, PLANE), me.g * PLANE + lax.rem(to, PLANE)),
+        )
+        cp.start()
+        meta_sent.append(cp)
+    meta_here = pltpu.make_async_copy(meta, meta_v.at[me.slot], meta_send.at[0])
+    meta_here.start()
+    sent_a, own_a = first(w_a, a_all, 0)
+    tokens = Gather(me, tok, tok_all, g_send.at[0], g_recv.at[0], g_loc.at[0])
+    tokens.start()
+    tok_in = pltpu.make_async_copy(tok, tok_v, loc.at[0])
+    tok_in.start()
+
+    blocks4 = lambda ref: (lambda b: ref.at[pl.ds(b * PLANE, PLANE)])
+    chain_a = Chain(me, blocks4(a_all), ch_send.at[0], ch_recv.at[0])
+    chain_b = Chain(me, blocks4(b_all), ch_send.at[1], ch_recv.at[1])
+    chain_d = Chain(me, lambda b: d_all.at[b], ch_send.at[2], ch_recv.at[2])
+
+    for g in range(2):
+        for a in range(taps_q):
+            t = band(kern, 2 * me.pair + g, a, taps_q, taps_k, length, False)
+            hi = t.astype(BF16)
+            t_v[g, 0, a * length : (a + 1) * length] = hi
+            t_v[g, 1, a * length : (a + 1) * length] = (t - hi.astype(F32)).astype(BF16)
+    shift_v[0:8] = jnp.zeros((8, length), F32)
+    wo_v[...] = jnp.zeros(wo_v.shape, BF16)
+
+    first_wait(w_a, a_all, 0, own_a)
+    chain_a.hop(0)
+
+    src_pair = lax.div(me.f, per_pair)
+    src_y, src_s = lax.div(src_pair, 4), lax.rem(src_pair, 2) * 2 + lax.rem(lax.div(src_pair, 2), 2)
+    src_j = lax.rem(me.f, per_pair)
+
+    def o_copy(g):
+        return remote(w_o, o_all.at[src_j], o_send.at[g], o_recv.at[src_j], (me.y, g * PLANE + src_s))
+
+    o_here = pltpu.make_async_copy(w_o, o_all.at[src_j], o_send.at[planes])
+
+    def o_each(act, act_here):
+        for g in range(planes):
+            mine = g * PLANE + src_s == me.f
+
+            if act is not None:
+
+                @pl.when((src_y == me.y) & jnp.logical_not(mine))
+                def _():
+                    act(o_copy(g))
+
+        if act_here is not None:
+
+            @pl.when((src_y == me.y) & (src_s == me.s))
+            def _():
+                act_here(o_here)
+
+    o_each(lambda cp: cp.start(), lambda cp: cp.start())
+
+    tokens.relay()
+    for hop in range(1, planes - 1):
+        chain_a.hop(hop)
+    tokens.share()
+    tokens.last()
+    sent_b, own_b = first(w_b, b_all, PLANE)
+    tokens.finish()
+    cots = Gather(me, ct, ct_all, g_send.at[1], g_recv.at[1], g_loc.at[1])
+    cots.start()
+    for r in range(GROUP):
+        pltpu.make_async_copy(tok_all.at[r], x_v.at[r], row_in.at[r]).start()
+    chain_a.hop(planes - 1)
+
+    wa_in = pltpu.make_async_copy(a_all, wa_v, loc.at[1])
+    wa_in.start()
+    for j in range(per_pair):
+        from_f = me.pair * per_pair + j
+
+        @pl.when(from_f != me.f)
+        def _():
+            remote(w_o, o_all.at[j], o_send.at[0], o_recv.at[j], me.sib()).wait_recv()
+
+    o_each(None, lambda cp: cp.wait())
+    wo_in = pltpu.make_async_copy(o_all, wo_v.at[pl.ds(0, per_pair)], loc.at[2])
+    wo_in.start()
+    pltpu.make_async_copy(w_d, d_all.at[me.g], loc.at[3]).start()
+    pltpu.make_async_copy(w_d, d_all.at[me.g], loc.at[3]).wait()
+    first_wait(w_b, b_all, PLANE, own_b)
+    wa_in.wait()
+    chain_d.hop(0)
+    chain_b.hop(0)
+    wo_in.wait()
+    for d in range(1, GROUP):
+        fr = lax.rem(me.slot - d + GROUP, GROUP)
+        remote(meta, meta_v.at[fr], meta_send.at[d], meta_recv.at[d], me.sib()).wait_recv()
+    meta_here.wait()
+    ends[...] = meta_v[...]
+
+    rows_o = per_pair * w_o.shape[0]
+    weights_a = wa_v[...].reshape(width, QKV)
+    gain_rows = jnp.transpose(weights_a[:, 384:512].astype(F32))
+    gains[...] = jnp.zeros(gains.shape, F32)
+    gains[0:1] = gain_rows[64:65]
+    gains[1:2] = gain_rows[65:66]
+    heads_col = wo_v[:, :, width:].reshape(wo_v.shape[0] * wo_v.shape[1], 128).astype(F32)
+    gains[2:3] = jnp.concatenate(
+        [jnp.transpose(heads_col[0:SIDE])[0:1], jnp.zeros((1, width - SIDE), F32)], axis=1
+    )
+
+    h0, h1 = head_lanes(length, dh)
+    scatter = Scatter(me, out_v, red, diag, near, rs_send, rs_recv)
+
+    def one(i, carry):
+        row, k = order(me, i)
+        pltpu.make_async_copy(tok_all.at[row], x_v.at[row], row_in.at[row]).wait()
+
+        def norm(at):
+            x = x_v[row, at].astype(F32)
+            s = lax.rsqrt(jnp.mean(x * x, axis=-1, keepdims=True) + 1e-6)
+            x_v[row, at] = (x * s * gains[0:1]).astype(BF16)
+
+        strips(length, norm)
+        pltpu.make_async_copy(x_v.at[row], nrm_all.at[row], row_out.at[0, row]).start()
+        acc = nn(x_v[row], wa_v[...].reshape(width, QKV))
+        at = lanes(length, 128)
+        q = jnp.where(h0 | h1, acc[:, 0:SIDE], 0.0)
+        kk = jnp.where(h0 | h1, acc[:, SIDE : 2 * SIDE], 0.0)
+        tail = jnp.where(at < 64, pltpu.roll(acc[:, 128:256], 64, 1), 0.0)
+        v = jnp.concatenate([acc[:, 2 * SIDE : QKV], tail], axis=1)
+        q, kk, v = q.astype(BF16), kk.astype(BF16), v.astype(BF16)
+        qkv_v[row, :, 0:SIDE] = q
+        qkv_v[row, :, SIDE : 2 * SIDE] = kk
+        qkv_v[row, :, 2 * SIDE : 3 * SIDE] = v
+        pltpu.make_async_copy(qkv_v.at[row], qkv_all.at[row], row_out.at[1, row]).start()
+        ok = allowed_mask(length, meta_v[row, 0:1, :])
+        attended = jnp.zeros((length, SIDE), F32)
+        for g in range(2):
+            kg = jnp.where(h0 if g == 0 else h1, kk.astype(F32), 0.0).astype(BF16)
+            raw = nt(q, kg) * scale
+            masked = jnp.where(ok, raw, 0.0)
+            m_v[row, g] = masked.astype(BF16)
+            shift_v[8 : 8 + length] = masked
+            for a in range(taps_q):
+                sh = shift_v[8 - a : 8 - a + length]
+                hi = sh.astype(BF16)
+                cat_v[0, :, a * length : (a + 1) * length] = hi
+                cat_v[1, :, a * length : (a + 1) * length] = (sh - hi.astype(F32)).astype(BF16)
+            conv = nn(cat_v[0], t_v[g, 0]) + nn(cat_v[1], t_v[g, 0]) + nn(cat_v[0], t_v[g, 1])
+            logits = jnp.where(ok, conv, NEG_FILL)
+            e = jnp.exp(logits - jnp.max(logits, axis=-1, keepdims=True))
+            probs = e / jnp.sum(e, axis=-1, keepdims=True)
+            high = probs.astype(BF16)
+            low = (probs - high.astype(F32)).astype(BF16)
+            p_v[row, g, 0] = high
+            p_v[row, g, 1] = low
+            attended = attended + (nn(high, v) + nn(low, v)) * mix_lanes(mix, me.pair, g, dh)
+        pltpu.make_async_copy(m_v.at[row], m_all.at[row], row_out.at[2, row]).start()
+        pltpu.make_async_copy(p_v.at[row], p_all.at[row], row_out.at[3, row]).start()
+        centred = attended - head_stats(attended, dh, h0, h1)
+        centred = jnp.where(h0 | h1, centred, 0.0)
+        scaled = centred * lax.rsqrt(head_stats(centred * centred, dh, h0, h1) + 1e-5)
+        gated = (scaled * gains[2:3, 0:SIDE]).astype(BF16)
+        gated_v[row] = gated
+        pltpu.make_async_copy(gated_v.at[row], gated_all.at[row], row_out.at[4, row]).start()
+        wo = wo_v[:, :, 0:width].reshape(wo_v.shape[0] * wo_v.shape[1], width)
+        part = nn(gated, wo[0:SIDE])
+
+        @pl.when(lax.rem(i, 2) == 0)
+        def _():
+            scatter.put_sib(k, part)
+
+        @pl.when(lax.rem(i, 2) == 1)
+        def _():
+            scatter.put_self(k, part)
+
+        scatter.push(i)
+        return carry
+
+    lax.fori_loop(0, GROUP, one, 0)
+    cots.relay()
+    scatter.turn()
+    cots.share()
+    cots.last()
+    cots.finish()
+    tok_in.wait()
+    scatter.arrive()
+
+    def middle(at):
+        res = tok_v[at].astype(F32) + scatter.total(at)
+        resid[at] = res
+        s = lax.rsqrt(jnp.mean(res * res, axis=-1, keepdims=True) + 1e-6)
+        mid_v[at] = (res * s * gains[1:2]).astype(BF16)
+
+    strips(length, middle)
+    mids = Gather(me, mid_v, mid_all, g_send.at[2], g_recv.at[2], g_loc.at[2])
+    mids.start()
+    chain_d.hop(1)
+    chain_b.hop(1)
+    mids.relay()
+    mids.share()
+    mids.last()
+    for hop in range(2, planes):
+        chain_d.hop(hop)
+        chain_b.hop(hop)
+    mids.finish()
+    scatter.finish()
+    for ch in (chain_a, chain_b, chain_d):
+        ch.finish()
+    o_each(lambda cp: cp.wait_send(), None)
+    for cp in meta_sent + sent_a + sent_b:
+        cp.wait_send()
+    for r in range(GROUP):
+        pltpu.make_async_copy(x_v.at[r], nrm_all.at[r], row_out.at[0, r]).wait()
+        pltpu.make_async_copy(qkv_v.at[r], qkv_all.at[r], row_out.at[1, r]).wait()
+        pltpu.make_async_copy(m_v.at[r], m_all.at[r], row_out.at[2, r]).wait()
+        pltpu.make_async_copy(p_v.at[r], p_all.at[r], row_out.at[3, r]).wait()
+        pltpu.make_async_copy(gated_v.at[r], gated_all.at[r], row_out.at[4, r]).wait()
+
+
+def forward_call(cfg, tok, ct, w_a, w_b, w_d, w_o, meta, kern, mix):
+    length, width = tok.shape
+    planes, ff, r = cfg["planes"], cfg["ff"], w_a.shape[1]
+    n = planes * PLANE
+    chunk = w_d.shape[0]
+    per_pair = n // GROUP
+    taps = cfg["kq"] * length
+    pad_rows = -(-SIDE // w_o.shape[0])
+    hbm, vmem, smem = pl.BlockSpec(memory_space=pl.ANY), pl.BlockSpec(memory_space=pltpu.VMEM), pl.BlockSpec(memory_space=pltpu.SMEM)
+    sds = jax.ShapeDtypeStruct
+    rows = (GROUP, length)
+    dma = pltpu.SemaphoreType.DMA
+    return pl.pallas_call(
+        functools.partial(forward_kernel, cfg),
+        out_shape=(
+            sds(rows + (width,), BF16), sds(rows + (width,), BF16),
+            sds((n, r, QKV), BF16), sds((n, r, 2 * ff), BF16), sds((planes, chunk, width), BF16),
+            sds((per_pair,) + w_o.shape, BF16), sds(rows + (width,), BF16), sds(rows + (3 * SIDE,), BF16),
+            sds((GROUP, 2, 2, length, length), BF16), sds((GROUP, 2, length, length), BF16), sds(rows + (SIDE,), BF16),
+            sds(rows + (width,), BF16), sds((length, width), F32), sds((8, width), F32), sds((GROUP, 8, length), F32),
+        ),
+        in_specs=[hbm] * 7 + [smem] * 2,
+        out_specs=(hbm,) * 12 + (vmem,) * 3,
+        scratch_shapes=[
+            pltpu.VMEM(rows + (width,), BF16), pltpu.VMEM((n, r, QKV), BF16), pltpu.VMEM((pad_rows,) + w_o.shape, BF16),
+            pltpu.VMEM((2, 2, taps, length), BF16), pltpu.VMEM((2, length, taps), BF16), pltpu.VMEM((length + 8, length), F32),
+            pltpu.VMEM(rows + (3 * SIDE,), BF16), pltpu.VMEM((GROUP, 2, 2, length, length), BF16),
+            pltpu.VMEM((GROUP, 2, length, length), BF16), pltpu.VMEM(rows + (SIDE,), BF16),
+            pltpu.VMEM((GROUP, 8, length), F32), pltpu.VMEM((length, width), BF16), pltpu.VMEM((length, width), BF16),
+            *Scatter.scratch(length, width),
+            dma((3, Gather.SENDS)), dma((3, Gather.RECVS)), dma((3,)), dma((2 * PLANE,)), dma((2 * PLANE,)),
+            dma((3, 2, planes)), dma((3, planes)), dma((planes + 1,)), dma((per_pair,)), dma((GROUP,)), dma((GROUP,)),
+            dma((4,)), dma((GROUP,)), dma((5, GROUP)),
+        ],
+        compiler_params=pltpu.CompilerParams(collective_id=1, has_side_effects=True, vmem_limit_bytes=50 * 2**20),
+        name="attention_forward",
+    )(tok, ct, w_a, w_b, w_d, w_o, meta, kern, mix)
+
+
+def feed_kernel(cfg, *refs):
+    (mid_all, ct_all, w_b, w_d, resid, gains,
+     layer_out, g_res, branch_all, dw_b, dw_d, g_mid_gain,
+     mid_v, ct_v, wb_v, wd_v, hid_v, gu_v, tile_v,
+     o_out, o_red, o_diag, o_near, o_send, o_recv,
+     m_out, m_red, m_diag, m_near, m_send, m_recv,
+     g_send, g_recv, g_loc, loc, row_in, out_sem) = refs
+    length, width = resid.shape
+    ff = cfg["ff"]
+    me = Place(cfg["planes"])
+    wb_in = pltpu.make_async_copy(w_b, wb_v, loc.at[0])
+    wb_in.start()
+    wd_in = pltpu.make_async_copy(w_d, wd_v, loc.at[1])
+    wd_in.start()
+
+    def row_copies(row):
+        return (
+            pltpu.make_async_copy(mid_all.at[row], mid_v.at[row], row_in.at[0, row]),
+            pltpu.make_async_copy(ct_all.at[row], ct_v.at[row], row_in.at[1, row]),
+        )
+
+    for i in range(GROUP):
+        for cp in row_copies(order(me, i)[0]):
+            cp.start()
+    me.greet()
+    sum_out = Scatter(me, o_out, o_red, o_diag, o_near, o_send, o_recv)
+    sum_mid = Scatter(me, m_out, m_red, m_diag, m_near, m_send, m_recv)
+    wb_in.wait()
+    wd_in.wait()
+
+    def one(i, carry):
+        row, k = order(me, i)
+        for cp in row_copies(row):
+            cp.wait()
+        wb = wb_v[...].reshape(width, 2 * ff)
+        wd = wd_v[...].reshape(ff, width)
+        pre = nn(mid_v[row], wb)
+        gate, up = pre[:, :ff], pre[:, ff:]
+        g_hidden = nt(ct_v[row], wd)
+        sig = jax.nn.sigmoid(gate)
+        silu = gate * sig
+        hidden = (silu * up).astype(BF16)
+        hid_v[row] = hidden
+        g_gate = (g_hidden * up * sig * (1.0 + gate * (1.0 - sig))).astype(BF16)
+        g_up = (g_hidden * silu).astype(BF16)
+        gu_v[row, :, :ff] = g_gate
+        gu_v[row, :, ff:] = g_up
+        mid_part = nt(gu_v[row], wb)
+        out_part = nn(hidden, wd)
+
+        @pl.when(lax.rem(i, 2) == 0)
+        def _():
+            sum_mid.put_sib(k, mid_part)
+            sum_out.put_sib(k, out_part)
+
+        @pl.when(lax.rem(i, 2) == 1)
+        def _():
+            sum_mid.put_self(k, mid_part)
+            sum_out.put_self(k, out_part)
+
+        sum_mid.push(i)
+        return carry
+
+    lax.fori_loop(0, GROUP, one, 0)
+    sum_mid.turn()
+
+    tokens = GROUP * length
+    tile = SIDE
+
+    steps_down, steps_up = ff // tile, width // tile
+
+    def tile_out(i, down):
+        slot = lax.rem(i, 2)
+        if down:
+            src, dst = tile_v.at[slot], dw_d.at[pl.ds(pl.multiple_of(i * tile, tile), tile)]
+        else:
+            at = pl.ds(pl.multiple_of((i - steps_down) * tile, tile), tile)
+            src, dst = tile_v.at[slot, :, pl.ds(0, 2 * ff)], dw_b.at[at]
+        return pltpu.make_async_copy(src, dst, out_sem.at[slot])
+
+    def down(i, carry):
+        at = pl.ds(pl.multiple_of(i * tile, tile), tile)
+        tile_v[lax.rem(i, 2)] = tn(hid_v[:, :, at].reshape(tokens, tile), ct_v[...].reshape(tokens, width)).astype(BF16)
+        tile_out(i, True).start()
+        return carry
+
+    lax.fori_loop(0, steps_down, down, 0)
+    for i in range(steps_down):
+        tile_out(i, True).wait()
+
+    g_mid_gain[...] = jnp.zeros(g_mid_gain.shape, F32)
+    sum_mid.arrive()
+
+    def middle(at):
+        g_mid = sum_mid.total(at)
+        res = resid[at]
+        s = lax.rsqrt(jnp.mean(res * res, axis=-1, keepdims=True) + 1e-6)
+        g_mid_gain[0:1] = g_mid_gain[0:1] + jnp.sum(g_mid * res * s, axis=0, keepdims=True)
+        pulled = g_mid * gains[1:2]
+        back = ct_v[me.slot, at].astype(F32) + s * pulled
+        back = back - res * (s * s * s * jnp.mean(pulled * res, axis=-1, keepdims=True))
+        g_res[at] = back
+        ct_v[me.slot, at] = back.astype(BF16)
+
+    strips(length, middle)
+    branch = Gather(me, ct_v.at[me.slot], branch_all, g_send, g_recv, g_loc.at[0])
+    branch.start()
+    for i in (1, 3, 5):
+        sum_out.push(i)
+
+    def gate_up(i, carry):
+        @pl.when(i >= steps_down + 2)
+        def _():
+            tile_out(i - 2, False).wait()
+
+        at = pl.ds(pl.multiple_of((i - steps_down) * tile, tile), tile)
+        value = tn(mid_v[:, :, at].reshape(tokens, tile), gu_v[...].reshape(tokens, 2 * ff))
+        tile_v[lax.rem(i, 2), :, 0 : 2 * ff] = value.astype(BF16)
+        tile_out(i, False).start()
+        return carry
+
+    end = steps_down + steps_up
+    lax.fori_loop(steps_down, steps_down + steps_up // 2, gate_up, 0)
+    branch.relay()
+    lax.fori_loop(steps_down + steps_up // 2, end, gate_up, 0)
+    branch.share()
+    sum_out.turn()
+    branch.last()
+    sum_out.arrive()
+
+    def result(at):
+        layer_out[at] = resid[at] + sum_out.total(at)
+
+    strips(length, result)
+    branch.finish()
+    sum_mid.finish()
+    sum_out.finish()
+    tile_out(end - 2, False).wait()
+    tile_out(end - 1, False).wait()
+
+
+def feed_call(cfg, mid_all, ct_all, w_b, w_d, resid, gains):
+    length, width = resid.shape
+    ff = cfg["ff"]
+    hbm, vmem = pl.BlockSpec(memory_space=pl.ANY), pl.BlockSpec(memory_space=pltpu.VMEM)
+    sds = jax.ShapeDtypeStruct
+    dma = pltpu.SemaphoreType.DMA
+    rows = (GROUP, length)
+    return pl.pallas_call(
+        functools.partial(feed_kernel, cfg),
+        out_shape=(
+            sds((length, width), F32), sds((length, width), F32), sds(rows + (width,), BF16),
+            sds((width, 2 * ff), BF16), sds((ff, width), BF16), sds((8, width), F32),
+        ),
+        in_specs=[hbm] * 4 + [vmem] * 2,
+        out_specs=(vmem, vmem, hbm, hbm, hbm, vmem),
+        scratch_shapes=[
+            pltpu.VMEM(rows + (width,), BF16), pltpu.VMEM(rows + (width,), BF16),
+            pltpu.VMEM(w_b.shape, BF16), pltpu.VMEM(w_d.shape, BF16),
+            pltpu.VMEM(rows + (ff,), BF16), pltpu.VMEM(rows + (2 * ff,), BF16),
+            pltpu.VMEM((2, SIDE, width), BF16),
+            *Scatter.scratch(length, width), *Scatter.scratch(length, width),
+            dma((Gather.SENDS,)), dma((Gather.RECVS,)), dma((1,)), dma((2,)), dma((2, GROUP)), dma((2,)),
+        ],
+        compiler_params=pltpu.CompilerParams(collective_id=2, has_side_effects=True, vmem_limit_bytes=50 * 2**20),
+        name="feed_forward",
+    )(mid_all, ct_all, w_b, w_d, resid, gains)
+
+
+def backward_kernel(cfg, *refs):
+    (branch_all, o_all, a_all, nrm_all, qkv_all, p_all, m_all, gated_all, dw_b, dw_d, tok, g_res, gains, ends, g_mid_gain, kern, mix,
+     g_tokens, out_a, out_b, out_d, out_o, out_small,
+     gb_v, wo_v, wa_v, nrm_v, qkv_v, p_v, m_v, gated_v, t_v, cat_v, shift_v, corr_v, gq_v, da_v, do_v, tok_v, rows_v, line_v,
+     zb_v, zd_v, za_v, zo_v, sb_v, sd_v, sa_v, so_v, own_b, own_d, small_v, small_in,
+     s_out, s_red, s_diag, s_near, rs_send, rs_recv,
+     z_send, z_recv, t_send, t_recv, loc, row_in) = refs
+    planes, dh, taps_q, taps_k = cfg["planes"], cfg["dh"], cfg["kq"], cfg["kk"]
+    length, width = tok.shape
+    scale = dh ** (-0.5)
+    me = Place(planes)
+    per_pair = o_all.shape[0]
+    r = a_all.shape[1]
+    loads = [
+        pltpu.make_async_copy(src, dst, loc.at[i])
+        for i, (src, dst) in enumerate(
+            [(a_all, wa_v), (o_all, wo_v.at[pl.ds(0, per_pair)]), (tok, tok_v), (gated_all, gated_v)]
+            + [(dw_b.at[pl.ds(me.g * PLANE, PLANE)], own_b), (dw_d.at[me.g], own_d)]
+        )
+    ]
+
+    span = PLANE * r
+
+    def nrm_copy(j):
+        at = pl.ds(j * span, span)
+        return pltpu.make_async_copy(nrm_all.at[:, :, at], nrm_v.at[j % 2], loc.at[6 + j % 2])
+
+    def row_copies(i):
+        row = order(me, i)[0]
+        at = lax.rem(i, SLOTS)
+        cps = [pltpu.make_async_copy(branch_all.at[row], gb_v.at[row], row_in.at[0, i])]
+        for j, (src, dst) in enumerate(((qkv_all, qkv_v), (p_all, p_v), (m_all, m_v))):
+            cps.append(pltpu.make_async_copy(src.at[row], dst.at[at], row_in.at[j + 1, i]))
+        return cps
+
+    wo_v[...] = jnp.zeros(wo_v.shape, BF16)
+    loads[1].start()
+    loads[0].start()
+    for i in range(SLOTS):
+        for cp in row_copies(i):
+            cp.start()
+    for cp in loads[2:]:
+        cp.start()
+    for j in range(2):
+        nrm_copy(j).start()
+    me.greet()
+
+    def z_copies(kind, src_of, landing):
+        cps = []
+        for d in range(1, planes):
+            to = lax.rem(me.g + d, planes)
+            cps.append(remote(src_of(to), landing.at[d - 1], z_send.at[kind, d - 1], z_recv.at[kind, d - 1], me.plane_dev(to)))
+        return cps
+
+    blocks4 = lambda ref: (lambda b: ref.at[pl.ds(b * PLANE, PLANE)])
+    send_d = z_copies(0, lambda b: dw_d.at[b], zd_v)
+    send_b = z_copies(1, blocks4(dw_b), zb_v)
+    send_a = z_copies(2, blocks4(da_v), za_v)
+    send_o = z_copies(3, lambda b: do_v.at[b], zo_v)
+    send_s = z_copies(4, lambda b: small_v, small_in)
+    for cp in send_d + send_b:
+        cp.start()
+
+    for g in range(2):
+        for a in range(taps_q):
+            t_v[g, a * length : (a + 1) * length] = band(kern, 2 * me.pair + g, a, taps_q, taps_k, length, True).astype(BF16)
+    shift_v[length:] = jnp.zeros((8, length), F32)
+    corr_v[...] = jnp.zeros(corr_v.shape, F32)
+    rows_v[...] = jnp.zeros(rows_v.shape, F32)
+    small_v[...] = jnp.zeros(small_v.shape, F32)
+    h0, h1 = head_lanes(length, dh)
+    scatter = Scatter(me, s_out, s_red, s_diag, s_near, rs_send, rs_recv)
+    loads[0].wait()
+    loads[1].wait()
+
+    def one(i, carry):
+        row, k = order(me, i)
+        at = lax.rem(i, SLOTS)
+        for cp in row_copies(i):
+            cp.wait()
+        wo = wo_v[:, :, 0:width].reshape(wo_v.shape[0] * wo_v.shape[1], width)[0:SIDE]
+        q, kk, v = qkv_v[at, :, 0:SIDE], qkv_v[at, :, SIDE : 2 * SIDE], qkv_v[at, :, 2 * SIDE : 3 * SIDE]
+        parts = [nn(p_v[at, g, 0], v) + nn(p_v[at, g, 1], v) for g in range(2)]
+        probs = [p_v[at, g, 0].astype(F32) + p_v[at, g, 1].astype(F32) for g in range(2)]
+        lane_mix = [mix_lanes(mix, me.pair, g, dh) for g in range(2)]
+        attended = parts[0] * lane_mix[0] + parts[1] * lane_mix[1]
+        centred = jnp.where(h0 | h1, attended - head_stats(attended, dh, h0, h1), 0.0)
+        inv = lax.rsqrt(head_stats(centred * centred, dh, h0, h1) + 1e-5)
+        normal = centred * inv
+        g_gated = nt(gb_v[row], wo)
+        rows_v[0:1] = rows_v[0:1] + jnp.sum(g_gated * normal, axis=0, keepdims=True)
+        u = g_gated * gains[2:3, 0:SIDE]
+        g_att = inv * (u - head_stats(u, dh, h0, h1) - normal * head_stats(u * normal, dh, h0, h1))
+        g_exact = jnp.where(h0 | h1, g_att, 0.0)
+        g_att = g_exact.astype(BF16).astype(F32)
+        ok = allowed_mask(length, ends[row, 0:1, :])
+        g_q = jnp.zeros((length, SIDE), F32)
+        g_k = jnp.zeros((length, SIDE), F32)
+        g_v = jnp.zeros((length, SIDE), F32)
+        for o in range(2):
+            mixed = mix[2 * me.pair + o, 0] * probs[0] + mix[2 * me.pair + o, 1] * probs[1]
+            g_v = g_v + tn(mixed.astype(BF16), jnp.where(h0 if o == 0 else h1, g_att, 0.0).astype(BF16))
+        for g in range(2):
+            mine = h0 if g == 0 else h1
+            rows_v[1 + g : 2 + g] = rows_v[1 + g : 2 + g] + jnp.sum(g_exact * parts[g], axis=0, keepdims=True)
+            g_out = (g_att * lane_mix[g]).astype(BF16)
+            g_probs = nt(g_out, v)
+            g_conv = probs[g] * (g_probs - jnp.sum(probs[g] * g_probs, axis=-1, keepdims=True))
+            shift_v[0:length] = g_conv
+            for a in range(taps_q):
+                cat_v[:, a * length : (a + 1) * length] = shift_v[a : a + length].astype(BF16)
+            corr_v[g] = corr_v[g] + tn(m_v[at, g], cat_v[...])
+            g_raw = jnp.where(ok, nn(cat_v[...], t_v[g]), 0.0).astype(BF16)
+            g_q = g_q + nn(g_raw, jnp.where(mine, kk.astype(F32), 0.0).astype(BF16))
+            g_k = g_k + tn(g_raw, jnp.where(mine, q.astype(F32), 0.0).astype(BF16))
+        g_q, g_k = g_q * scale, g_k * scale
+        mid_tile = g_q[:, 128:256] + pltpu.roll(g_v[:, 128:256], 64, 1)
+        packed = jnp.concatenate([g_q[:, 0:128], mid_tile, g_k, g_v[:, 0:128]], axis=1).astype(BF16)
+        gq_v[row] = packed
+        part = nt(packed, wa_v[...].reshape(width, QKV))
+
+        @pl.when(lax.rem(i, 2) == 0)
+        def _():
+            scatter.put_sib(k, part)
+
+        @pl.when(lax.rem(i, 2) == 1)
+        def _():
+            scatter.put_self(k, part)
+
+        scatter.push(i)
+
+        @pl.when(i + SLOTS < GROUP)
+        def _():
+            for cp in row_copies(i + SLOTS):
+                cp.start()
+
+        return carry
+
+    lax.fori_loop(0, GROUP, one, 0)
+    scatter.turn()
+
+    for cp in loads[2:]:
+        cp.wait()
+    tokens = GROUP * length
+    for j in range(planes):
+        nrm_copy(j).wait()
+        value = tn(nrm_v[j % 2].reshape(tokens, span), gq_v[...].reshape(tokens, QKV))
+        da_v[j * PLANE : (j + 1) * PLANE] = value.astype(BF16).reshape(PLANE, r, QKV)
+        if j + 2 < planes:
+            nrm_copy(j + 2).start()
+    for cp in send_a:
+        cp.start()
+    value = tn(gated_v[...].reshape(tokens, SIDE), gb_v[...].reshape(tokens, width))
+    do_v[...] = value[0 : 2 * dh].astype(BF16).reshape(do_v.shape)
+    for cp in send_o:
+        cp.start()
+
+    def taps(at, carry):
+        g, a = lax.div(at, taps_q), lax.rem(at, taps_q)
+        lanes_at = pl.ds(pl.multiple_of(a * length, length), length)
+        e = corr_v[g, :, lanes_at]
+        diff = lax.broadcasted_iota(jnp.int32, (length, length), 0) - lax.broadcasted_iota(jnp.int32, (length, length), 1)
+        for b in range(taps_k):
+            line = jnp.sum(jnp.where(diff == b - taps_k // 2, e, 0.0), axis=0, keepdims=True)
+            small_v[at, b : b + 1] = line[:, 0:128] + line[:, 128:256]
+        return carry
+
+    lax.fori_loop(0, 2 * taps_q, taps, 0)
+    base = 2 * taps_q
+    at = lanes(1, SIDE)
+    for o in range(2):
+        for g in range(2):
+            line = jnp.where((at >= o * dh) & (at < (o + 1) * dh), rows_v[1 + g : 2 + g], 0.0)
+            small_v[base, 2 * o + g : 2 * o + g + 1] = line[:, 0:128] + line[:, 128:256]
+    for j in range(2):
+        small_v[base, 4 + j : 5 + j] = rows_v[0:1, j * 128 : (j + 1) * 128]
+
+    scatter.arrive()
+
+    def middle(at):
+        g_normed = scatter.total(at)
+        tok32 = tok_v[at].astype(F32)
+        s = lax.rsqrt(jnp.mean(tok32 * tok32, axis=-1, keepdims=True) + 1e-6)
+        line_v[0:1] = line_v[0:1] + jnp.sum(g_normed * tok32 * s, axis=0, keepdims=True)
+        pulled = g_normed * gains[0:1]
+        back = g_res[at] + s * pulled
+        g_tokens[at] = back - tok32 * (s * s * s * jnp.mean(pulled * tok32, axis=-1, keepdims=True))
+
+    line_v[...] = jnp.zeros(line_v.shape, F32)
+    strips(length, middle)
+    line = line_v[0:1]
+    for j in range(width // 128):
+        small_v[base + 1, j : j + 1] = line[:, j * 128 : (j + 1) * 128]
+        small_v[base + 2, j : j + 1] = g_mid_gain[0:1, j * 128 : (j + 1) * 128]
+    for cp in send_s:
+        cp.start()
+
+    def to_slot(d):
+        to = lax.rem(me.slot + d, GROUP)
+        return lax.div(to, PLANE), lax.rem(to, PLANE)
+
+    def group_copies(kind, src_of, landing):
+        cps = []
+        for d in range(1, GROUP):
+            y, sl = to_slot(d)
+            cps.append(remote(src_of(sl), landing.at[me.slot], t_send.at[kind, d], t_recv.at[kind, d], (y, me.g * PLANE + sl)))
+        cps.append(pltpu.make_async_copy(src_of(me.s), landing.at[me.slot], t_send.at[kind, 0]))
+        return cps
+
+    def group_wait(kind, cps, landing):
+        for d in range(1, GROUP):
+            fr = lax.rem(me.slot - d + GROUP, GROUP)
+            remote(landing.at[fr], landing.at[fr], t_send.at[kind, d], t_recv.at[kind, d], me.sib()).wait_recv()
+        for cp in cps[:-1]:
+            cp.wait_send()
+        cps[-1].wait()
+
+    for cp in send_s:
+        cp.wait_recv()
+    for cp in send_s:
+        cp.wait_send()
+    small_v[...] = small_v[...] + sum(small_in[d] for d in range(planes - 1))
+    small_cps = group_copies(2, lambda sl: small_v, out_small)
+    for cp in small_cps:
+        cp.start()
+
+    def sums(landing, own):
+        total = own.astype(F32)
+        for d in range(planes - 1):
+            total = total + landing[d].astype(F32)
+        return total.astype(BF16)
+
+    for cp in send_d:
+        cp.wait_recv()
+    sd_v[...] = sums(zd_v, own_d[...])
+    d_cp = remote(sd_v, out_d.at[me.y], t_send.at[3, 0], t_recv.at[3, 0], me.yn())
+    d_cp.start()
+    d_here = pltpu.make_async_copy(sd_v, out_d.at[me.y], t_send.at[3, 1])
+    d_here.start()
+    for cp in send_b:
+        cp.wait_recv()
+    sb_v[...] = sums(zb_v, own_b[...])
+    b_cps = group_copies(0, lambda sl: sb_v.at[sl], out_b)
+    for cp in b_cps:
+        cp.start()
+    for cp in send_o:
+        cp.wait_recv()
+    so_v[...] = sums(zo_v, do_v[me.g])
+    o_to = me.pair * per_pair + lax.div(me.g, 2)
+    o_half = lax.rem(me.g, 2)
+
+    def o_copy(y):
+        return remote(so_v, out_o.at[o_half], t_send.at[4, y], t_recv.at[4, o_half], (y, o_to))
+
+    o_here = pltpu.make_async_copy(so_v, out_o.at[o_half], t_send.at[4, 2])
+
+    def o_each(act, act_here):
+        for y in range(2):
+            mine = (y == me.y) & (o_to == me.f)
+
+            @pl.when(jnp.logical_not(mine))
+            def _():
+                act(o_copy(y))
+
+            @pl.when(mine)
+            def _():
+                act_here(o_here)
+
+    o_each(lambda cp: cp.start(), lambda cp: cp.start())
+    for cp in send_a:
+        cp.wait_recv()
+    sa_v[...] = sums(za_v, da_v[pl.ds(me.g * PLANE, PLANE)])
+    a_cps = group_copies(1, lambda sl: sa_v.at[sl], out_a)
+    for cp in a_cps:
+        cp.start()
+
+    group_wait(2, small_cps, out_small)
+    d_cp.wait_send()
+    remote(out_d.at[1 - me.y], out_d.at[1 - me.y], t_send.at[3, 0], t_recv.at[3, 0], me.yn()).wait_recv()
+    d_here.wait()
+    group_wait(0, b_cps, out_b)
+    src_pair = lax.div(me.f, per_pair)
+    src_y, src_s = lax.div(src_pair, 4), lax.rem(src_pair, 2) * 2 + lax.rem(lax.div(src_pair, 2), 2)
+    for h in range(2):
+        src_f = (2 * lax.rem(me.f, per_pair) + h) * PLANE + src_s
+
+        @pl.when(jnp.logical_not((src_y == me.y) & (src_f == me.f)))
+        def _():
+            remote(out_o.at[h], out_o.at[h], t_send.at[4, 0], t_recv.at[4, h], me.sib()).wait_recv()
+
+    o_each(lambda cp: cp.wait_send(), lambda cp: cp.wait())
+    group_wait(1, a_cps, out_a)
+    for cp in send_d + send_b + send_a + send_o:
+        cp.wait_send()
+    scatter.finish()
+
+
+def backward_call(cfg, branch_all, o_all, a_all, nrm_all, qkv_all, p_all, m_all, gated_all, dw_b, dw_d, tok, g_res, gains, ends, g_mid_gain, kern, mix):
+    length, width = tok.shape
+    planes, ff = cfg["planes"], cfg["ff"]
+    n, r = a_all.shape[:2]
+    chunk = ff // planes
+    taps = cfg["kq"] * length
+    pad_rows = -(-SIDE // o_all.shape[1])
+    piece = 2 * cfg["dh"] // planes
+    small = (2 * cfg["kq"] + 3, 16, 128)
+    hbm, vmem, smem = pl.BlockSpec(memory_space=pl.ANY), pl.BlockSpec(memory_space=pltpu.VMEM), pl.BlockSpec(memory_space=pltpu.SMEM)
+    sds = jax.ShapeDtypeStruct
+    dma = pltpu.SemaphoreType.DMA
+    rows = (GROUP, length)
+    v16 = lambda *shape: pltpu.VMEM(shape, BF16)
+    v32 = lambda *shape: pltpu.VMEM(shape, F32)
+    return pl.pallas_call(
+        functools.partial(backward_kernel, cfg),
+        out_shape=(
+            sds((length, width), F32), sds((GROUP, r, QKV), BF16), sds((GROUP, r, 2 * ff), BF16),
+            sds((2, chunk, width), BF16), sds((2, piece, width), BF16), sds((GROUP,) + small, F32),
+        ),
+        in_specs=[hbm] * 11 + [vmem] * 4 + [smem] * 2,
+        out_specs=(vmem,) + (hbm,) * 5,
+        scratch_shapes=[
+            v16(*rows, width), v16(pad_rows, *o_all.shape[1:]), v16(n, r, QKV), v16(2, *rows, PLANE * r), v16(SLOTS, length, 3 * SIDE),
+            v16(SLOTS, 2, 2, length, length), v16(SLOTS, 2, length, length), v16(*rows, SIDE),
+            v16(2, taps, length), v16(length, taps), v32(length + 8, length), v32(2, length, taps), v16(*rows, QKV),
+            v16(n, r, QKV), v16(planes, piece, width), v16(length, width), v32(8, SIDE), v32(8, width),
+            v16(planes - 1, PLANE, r, 2 * ff), v16(planes - 1, chunk, width), v16(planes - 1, PLANE, r, QKV), v16(planes - 1, piece, width),
+            v16(PLANE, r, 2 * ff), v16(chunk, width), v16(PLANE, r, QKV), v16(piece, width), v16(PLANE, r, 2 * ff), v16(chunk, width),
+            v32(*small), v32(planes - 1, *small),
+            *Scatter.scratch(length, width),
+            dma((5, planes - 1)), dma((5, planes - 1)), dma((5, GROUP)), dma((5, GROUP)), dma((8,)), dma((4, GROUP)),
+        ],
+        compiler_params=pltpu.CompilerParams(collective_id=3, has_side_effects=True, vmem_limit_bytes=54 * 2**20),
+        name="attention_backward",
+    )(branch_all, o_all, a_all, nrm_all, qkv_all, p_all, m_all, gated_all, dw_b, dw_d, tok, g_res, gains, ends, g_mid_gain, kern, mix)
+
+
+def pair_order(blocks):
+    rest = blocks.shape[1:]
+    return jnp.swapaxes(blocks.reshape((2, 2, 2) + rest), 1, 2).reshape((GROUP,) + rest)
+
+
+def fits(mesh, tokens, kernel, w_gate):
+    n = mesh.shape["fsdp"]
+    width, length, heads, ff = tokens.shape[2], tokens.shape[1], kernel.shape[0], w_gate.shape[1]
+    return (
+        mesh.shape["rep"] == 2
+        and n % GROUP == 0
+        and heads == 2 * GROUP
+        and width == heads * 96
+        and (width // n) % 32 == 0
+        and ff % (2 * n * 128) == 0
+        and length == SIDE
+    )
+
+
+def per_device_group(
+    planes,
+    tokens,
+    doc_lengths,
+    pad_counts,
+    norm_in,
+    w_qkv,
+    kernel,
+    mixing,
+    norm_heads,
+    w_out,
+    norm_mid,
+    w_gate,
+    w_up,
+    w_down,
+    cotangent,
+):
+    length, width = tokens.shape[1:]
+    heads, kq, kk = kernel.shape
+    dh = width // heads
+    n = planes * PLANE
+    r = width // n
+    chunk = w_down.shape[0] // 2
+    ff = planes * chunk
+    cfg = dict(planes=planes, dh=dh, kq=kq, kk=kk, ff=ff)
+    y = lax.axis_index("rep")
+    f = lax.axis_index("fsdp")
+
+    with jax.named_scope("slices_to_send"):
+        by_pair = lax.dynamic_index_in_dim(w_qkv.reshape(r, 3, 2, 2, 2, 2 * dh), y, 2, keepdims=False)
+        by_pair = by_pair.transpose(3, 2, 0, 1, 4).reshape(PLANE, r, 3, 2 * dh)
+        gains_at = jnp.stack([norm_in, norm_mid], axis=1)
+        gains_at = jnp.broadcast_to(jnp.pad(gains_at, ((0, 0), (0, 62)))[None], (PLANE, r, 64))
+        w_a = jnp.concatenate(
+            [by_pair[:, :, 0], by_pair[:, :, 2, 128:], by_pair[:, :, 1], gains_at, by_pair[:, :, 2, :128]], axis=-1
+        )
+
+        def columns(w):
+            w = lax.dynamic_index_in_dim(w.reshape(r, planes, PLANE, 2, chunk), y, 3, keepdims=False)
+            return w.transpose(2, 0, 1, 3).reshape(PLANE, r, ff)
+
+        w_b = jnp.concatenate([columns(w_gate), columns(w_up)], axis=-1)
+        w_d = lax.dynamic_index_in_dim(w_down.reshape(2, chunk, width), y, 0, keepdims=False)
+        w_o = jnp.concatenate([w_out, jnp.pad(norm_heads[:, None], ((0, 0), (0, 127)))], axis=1)
+        places = jnp.arange(length, dtype=jnp.int32)
+        doc_ends = jnp.cumsum(doc_lengths[0])
+        own_end = jnp.min(jnp.where(doc_ends[None, :] > places[:, None], doc_ends[None, :], length), axis=1)
+        ends = jnp.where(places < length - pad_counts[0], own_end, places + 1).astype(F32)
+        meta = jnp.broadcast_to(ends[None], (8, length))
+    tok, ct = tokens[0], cotangent[0]
+    kern_flat = kernel.reshape(-1)
+
+    (_, ct_all, a_all, b_all, d_all, o_all, nrm_all, qkv_all, p_all, m_all, gated_all, mid_all, resid, gains, ends_all) = (
+        forward_call(cfg, tok, ct, w_a, w_b, w_d, w_o, meta, kern_flat, mixing)
+    )
+    layer_out, g_res, branch_all, dw_b, dw_d, g_mid_gain = feed_call(
+        cfg, mid_all, ct_all, b_all, d_all, resid, gains
+    )
+    g_tokens, out_a, out_b, out_d, out_o, small = backward_call(
+        cfg, branch_all, o_all, a_all, nrm_all, qkv_all, p_all, m_all, gated_all, dw_b.reshape(n, r, 2 * ff),
+        dw_d.reshape(planes, chunk, width), tok, g_res, gains, ends_all, g_mid_gain, kern_flat, mixing,
+    )
+
+    with jax.named_scope("results"):
+        q = out_a[:, :, 0 : 2 * dh]
+        k = out_a[:, :, SIDE : SIDE + 2 * dh]
+        v = jnp.concatenate([out_a[:, :, 2 * SIDE :], out_a[:, :, 2 * dh : SIDE]], axis=-1)
+        g_qkv = jnp.stack([pair_order(part) for part in (q, k, v)]).transpose(2, 0, 1, 3)
+        g_qkv = g_qkv.reshape(r, 3 * width).astype(F32)
+
+        def whole(part):
+            part = part.reshape(2, PLANE, r, planes, chunk).transpose(2, 3, 1, 0, 4)
+            return part.reshape(r, n * 2 * chunk).astype(F32)
+
+        g_gate, g_up = whole(out_b[:, :, :ff]), whole(out_b[:, :, ff:])
+        g_down = out_d.reshape(2 * chunk, width).astype(F32)
+        g_out = out_o.reshape(r, width).astype(F32)
+        g_kernel = pair_order(small[:, : 2 * kq, :kk].sum(-1)).reshape(heads, kq, kk)
+        base = 2 * kq
+        g_mixing = pair_order(small[:, base, 0:4].sum(-1)).reshape(heads, 2)
+
+        def own(line):
+            return lax.dynamic_slice_in_dim(line, f * r, r)
+
+        g_heads = own(pair_order(small[:, base, 4:6].reshape(GROUP, 256)[:, : 2 * dh]).reshape(width))
+        lines = small[:, base + 1 :, : width // 128].sum(0).reshape(2, width)
+        g_in, g_mid = own(lines[0]), own(lines[1])
+    return (layer_out[None], g_tokens[None], g_in, g_qkv, g_kernel, g_mixing, g_heads, g_out, g_mid, g_gate, g_up, g_down)
+
+
 def solution(mesh):
-    return jax.shard_map(
-        per_device,
-        mesh=mesh,
-        in_specs=(
-            P(("rep", "fsdp"), None, None),
-            P(("rep", "fsdp"), None),
-            P(("rep", "fsdp")),
-            P("fsdp"),
-            P("fsdp", None),
-            P(),
-            P(),
-            P("fsdp"),
-            P("fsdp", None),
-            P("fsdp"),
-            P("fsdp", None),
-            P("fsdp", None),
-            P("fsdp", None),
-            P(("rep", "fsdp"), None, None),
-        ),
-        out_specs=(
-            P(("rep", "fsdp"), None, None),
-            P(("rep", "fsdp"), None, None),
-            P("fsdp"),
-            P("fsdp", None),
-            P(),
-            P(),
-            P("fsdp"),
-            P("fsdp", None),
-            P("fsdp"),
-            P("fsdp", None),
-            P("fsdp", None),
-            P("fsdp", None),
-        ),
-        check_vma=False,
-    )
+    in_specs = (
+        P(("rep", "fsdp"), None, None),
+        P(("rep", "fsdp"), None),
+        P(("rep", "fsdp")),
+        P("fsdp"),
+        P("fsdp", None),
+        P(),
+        P(),
+        P("fsdp"),
+        P("fsdp", None),
+        P("fsdp"),
+        P("fsdp", None),
+        P("fsdp", None),
+        P("fsdp", None),
+        P(("rep", "fsdp"), None, None),
+    )
+    out_specs = (
+        P(("rep", "fsdp"), None, None),
+        P(("rep", "fsdp"), None, None),
+        P("fsdp"),
+        P("fsdp", None),
+        P(),
+        P(),
+        P("fsdp"),
+        P("fsdp", None),
+        P("fsdp"),
+        P("fsdp", None),
+        P("fsdp", None),
+        P("fsdp", None),
+    )
+
+    def layer(*args):
+        body = per_device
+        if fits(mesh, args[0], args[5], args[10]):
+            body = functools.partial(per_device_group, mesh.shape["fsdp"] // PLANE)
+        return jax.shard_map(body, mesh=mesh, in_specs=in_specs, out_specs=out_specs, check_vma=False)(*args)
+
+    return layer

time: 1800 us -> 596 us (0.33)
  waiting for transfers between devices: 815 us -> 0 us
  Pallas kernels: 0 us -> 518 us
  other arithmetic: 340 us -> 11.6 us
  matrix products: 324 us -> 0 us
  blocking collectives: 166 us -> 0 us
  local copies, waits for them, and re-layouts: 112 us -> 55 us
    reduce_scatter x5 -> x0, waiting for transfers between devices: 614 us -> none  [the longest x1 271 us: per_device(): lax.psum_scatter(grad_w_qkv, 'fsdp', scatter_dimension=0, tiled=True)]
    pallas_call x0 -> x3, Pallas kernels: none -> 518 us  [the longest x1 226 us: backward_call(): pl.pallas_call(functools.partial(backward_kernel, cfg), out_shape=(sds((l...]
    dot_general x103 -> x0, matrix products: 324 us -> none  [the longest x5 62.3 us: outer_sum(): lax.dot_general(left_rows, right_rows, (((0,), (0,)), ((), ())), preferre...]
    all_gather x5 -> x0, waiting for transfers between devices: 198 us -> none  [the longest x1 91.6 us: feed_weights(): lax.all_gather(w_down, 'fsdp', axis=0, tiled=True)]
    unnamed x2 -> x0, blocking collectives: 124 us -> none
    reduce_max x8 -> x0, other arithmetic: 79.4 us -> none  [pair_forward(): row_peak = jnp.max(logits, axis=-1, keepdims=True)]
    exp x16 -> x0, other arithmetic: 70.3 us -> none  [the longest x8 69.2 us: pair_backward(): attn_probs = jnp.exp(logits - log_total)]
    select_n x8 -> x0, other arithmetic: 68.7 us -> none  [pair_backward(): grad_raw = jnp.where(allowed, grad_masked, 0.0)]
  transfers between devices with their start and end apart: 11 -> 0, of which waited for: 6 -> 0; matrix products, arithmetic and copies ran while one was open for 41% -> 0% of each run, Pallas kernels for 0% -> 0%
where the time goes in v1:
time: 596 us; the launch traced here: 587 us
  Pallas kernels  518 us (87%)
  local copies, waits for them, and re-layouts  55 us (9%)
  other arithmetic  11.6 us (2%)
    pallas_call x1, Pallas kernels, backward_call(): pl.pallas_call(functools.partial(backward_kernel, cfg), out_shape=(sds((l...  226 us
    pallas_call x1, Pallas kernels, forward_call(): pl.pallas_call(functools.partial(forward_kernel, cfg), out_shape=(sds(row...  195 us
    pallas_call x1, Pallas kernels, feed_call(): pl.pallas_call(functools.partial(feed_kernel, cfg), out_shape=(sds((lengt...  96.7 us
    convert_element_type x6, local copies, waits for them, and re-layouts, whole(): return part.reshape(r, n * 2 * chunk).astype(F32)  19.6 us

profile of v1, /device:TPU:0, one launch (start us, length us, event | category | flops | bytes accessed | tf_op | source)
XLA Modules:
  0.0 586.6 jit_solution(4219188822449989357)
XLA Ops:
  1.4 0.4 copy-done
  1.8 0.8 reduce-window.8
  2.7 0.7 pad_maximum_fusion.2
  3.4 0.8 copy.98.refs_8_.refs_16_
  4.3 0.8 copy.96
  5.1 0.9 copy.97
  6.2 0.7 broadcast_in_dim.20
  6.8 1.0 fusion.1.refs_5_
  7.9 0.6 reshape.155
  8.4 3.3 reshape.157
  11.7 2.8 constant_dynamic-slice_fusion
  15.2 1.0 pad_maximum_fusion.refs_3_
  16.2 3.7 reshape.153
  19.9 0.4 constant_dynamic-slice_fusion.2
  20.5 0.7 slice_bitcast_fusion.3
  21.1 0.7 slice_bitcast_fusion.2
  21.8 1.1 concatenate.12.refs_2_
  23.0 195.4 %attention_forward.1 = (bf16[8,256,1536]{2,1,0:T(8,128)(2,1)}, bf16[8,256,1536]{2,1,0:T(8,128)(2,1)}, bf16[16,96,640]{2,1,0:T(8,128)(2,1)}, bf16[16,96,1024]{2,1...) custom-call(bf16[256,1536]{1,0:T(8,128)(2,1)S(1)} %bitcast.82, ...), custom_call_target="tpu_custom_call" | custom-call | tf_op jit(solution)/shard_map/attention_forward/pallas_call | solution.py:871
  218.4 0.8 copy-done.5
  219.3 96.7 %feed_forward.1 = (f32[256,1536]{1,0:T(8,128)S(1)}, f32[256,1536]{1,0:T(8,128)S(1)}, bf16[8,256,1536]{2,1,0:T(8,128)(2,1)}, bf16[1536,1024]{1,0:T(8,128)(2,1)}, ...) custom-call(bf16[8,256,1536]{2,1,0:T(8,128)(2,1)} %get-tuple-element.38.refs_0_, ...), custom_call_target="tpu_custom_call" | custom-call | tf_op jit(solution)/shard_map/feed_forward/pallas_call | solution.py:1046
  316.0 1.1 copy-done.3
  317.2 0.6 copy-done.10
  317.8 225.8 %attention_backward.1 = (f32[256,1536]{1,0:T(8,128)}, bf16[8,96,640]{2,1,0:T(8,128)(2,1)}, bf16[8,96,1024]{2,1,0:T(8,128)(2,1)}, bf16[2,128,1536]{2,1,0:T(8,128)...) custom-call(bf16[8,256,1536]{2,1,0:T(8,128)(2,1)} %get-tuple-element.45.refs_0_, ...), custom_call_target="tpu_custom_call" | custom-call | tf_op jit(solution)/shard_map/attention_backward/pallas_call | solution.py:1379
  543.6 0.9 slice_reduce_fusion.2
  544.7 0.6 copy.111
  545.3 0.8 slice_bitcast_fusion.6
  546.2 0.6 dynamic_slice.29
  546.8 0.9 slice_reduce_fusion.1
  547.7 1.4 slice_reduce_fusion
  549.2 0.6 dynamic_slice.30
  549.8 0.6 dynamic_slice.28
  550.6 0.7 copy.110
  551.8 0.8 copy-done.17
  552.5 0.9 bitcast_convert_fusion.1
  553.8 2.8 copy.103
  556.5 3.1 reshape.177
  559.6 1.4 bitcast_convert_fusion
  561.0 0.6 copy-done.12
  561.6 2.1 slice_convert_fusion
  563.7 2.7 reshape.183
  566.4 3.8 copy.109
  570.1 3.3 reshape.180
  573.5 2.7 reshape.182
  576.2 3.8 copy.108
  579.9 3.3 reshape.179
  583.3 1.1 copy.123
  584.4 0.8 copy-done.11
  585.2 1.1 copy.124
  (60 shorter events, 2.5 us)
Async XLA Ops:
  0.6 1.2 copy-start
  0.7 7.2 %copy-start.14 = (bf16[96,4096]{1,0:T(8,128)(2,1)S(1)}, bf16[96,4096]{1,0:T(8,128)(2,1)}, u32[]{:S(2)}) copy-start(bf16[96,4096]{1,0:T(8,128)(2,1)} %param.24) | copy-start | bytes 2359300
  4.2 18.8 %copy-start.8 = (f32[16,2]{1,0:T(8,128)}, f32[16,2]{1,0:T(8,128)S(1)}, u32[]{:S(2)}) copy-start(f32[16,2]{1,0:T(8,128)S(1)} %copy.98.refs_8_.refs_16_) | copy-start | bytes 388
  6.2 16.8 %copy-start.7 = (f32[1056]{0:T(1024)}, f32[1056]{0:T(1024)S(1)}, u32[]{:S(2)}) copy-start(f32[1056]{0:T(1024)S(1)} %reshape.162.refs_7_.refs_15_) | copy-start | bytes 12676
  19.9 1.9 copy-start.16
  20.4 2.6 copy-start.2
  20.4 2.6 copy-start.4
  218.4 0.8 copy-start.5
  219.3 96.7 %copy-start.6 = (f32[8,1536]{1,0:T(8,128)}, f32[8,1536]{1,0:T(8,128)S(1)}, u32[]{:S(2)}) copy-start(f32[8,1536]{1,0:T(8,128)S(1)} %get-tuple-element.43.refs_5_.refs_12_) | copy-start | bytes 147460
  219.3 96.8 %copy-start.9 = (f32[8,8,256]{2,1,0:T(8,128)}, f32[8,8,256]{2,1,0:T(8,128)S(1)}, u32[]{:S(2)}) copy-start(f32[8,8,256]{2,1,0:T(8,128)S(1)} %get-tuple-element.56.refs_13_) | copy-start | bytes 196612
  316.0 1.1 copy-start.3
  317.2 0.6 copy-start.10
  543.6 7.7 %copy-start.13 = (bf16[8,96,640]{2,1,0:T(8,128)(2,1)S(1)}, bf16[8,96,640]{2,1,0:T(8,128)(2,1)}, u32[]{:S(2)}) copy-start(bf16[8,96,640]{2,1,0:T(8,128)(2,1)} %get-tuple-element.60) | copy-start | bytes 2949124
  551.6 1.0 copy-start.17
  556.5 3.1 copy-start.15
  559.6 2.0 copy-start.12
  583.3 2.0 copy-start.11
  583.3 3.1 copy-start.1

commit v2 on v1

--- a/solution.py
+++ b/solution.py
@@ -14,7 +14,8 @@
 PLANE = 4
 GROUP = 8
 SIDE = 256
-SLOTS = 4
+LAG = 3
+SLOTS = 2
 QKV = 640
 
 
@@ -28,19 +29,14 @@
         self.x = lax.div(self.s, 2)
         self.c = lax.rem(self.s, 2)
         self.slot = self.y * PLANE + self.s
-        self.pair = self.y * 4 + self.c * 2 + self.x
+        self.home = self.y + self.c * (planes - 1 - 2 * self.y)
+        self.pair = 2 * self.home + self.x
+        self.sib = self.dev(self.y, self.x, 1 - self.c)
+        self.xn = self.dev(self.y, 1 - self.x, self.c)
+        self.yn = self.dev(1 - self.y, self.x, self.c)
 
     def dev(self, y, x, c):
         return (y, self.g * PLANE + x * 2 + c)
-
-    def sib(self):
-        return self.dev(self.y, self.x, 1 - self.c)
-
-    def xn(self):
-        return self.dev(self.y, 1 - self.x, self.c)
-
-    def yn(self):
-        return self.dev(1 - self.y, self.x, self.c)
 
     def plane_dev(self, g):
         return (self.y, g * PLANE + self.s)
@@ -61,6 +57,11 @@
         pl.semaphore_wait(sem, n - 1 + PLANE)
 
 
+def meet(me, sem):
+    pl.semaphore_signal(sem, inc=1, device_id=me.sib, device_id_type=MESH)
+    pl.semaphore_wait(sem, 1)
+
+
 def remote(src, dst, send, recv, dev):
     return pltpu.make_async_remote_copy(
         src_ref=src, dst_ref=dst, send_sem=send, recv_sem=recv, device_id=dev, device_id_type=MESH
@@ -83,55 +84,59 @@
     def _blk(self, row, h):
         return self.buf.at[row, pl.ds(h * self.half, self.half)]
 
-    def _go(self, src, row, h, kind, dev):
-        cp = remote(src, self._blk(row, h), self.send.at[len(self.sent)], self.recv.at[kind * 2 + h], dev)
-        cp.start()
-        self.sent.append(cp)
+    def _copy(self, i):
+        own, row, h, kind, dev = self.sent[i]
+        src = self._own(h) if own else self._blk(row, h)
+        return remote(src, self._blk(row, h), self.send.at[i], self.recv.at[kind * 2 + h], dev)
+
+    def _go(self, own, row, h, kind, dev):
+        self.sent.append((own, row, h, kind, dev))
+        self._copy(len(self.sent) - 1).start()
 
     def _await(self, row, h, kind):
         b = self._blk(row, h)
-        remote(b, b, self.send.at[0], self.recv.at[kind * 2 + h], self.me.sib()).wait_recv()
+        remote(b, b, self.send.at[0], self.recv.at[kind * 2 + h], self.me.sib).wait_recv()
 
     def start(self):
         me = self.me
         self.rows = [me.row(0, 0, 1), me.row(0, 1, 0), me.row(1, 0, 0), me.row(1, 1, 0), me.row(0, 1, 1), me.row(1, 0, 1), me.row(1, 1, 1)]
         self.here = pltpu.make_async_copy(self.own, self.buf.at[me.slot], self.local)
         self.here.start()
-        self._go(self._own(0), me.slot, 0, 1, me.xn())
-        self._go(self._own(1), me.slot, 1, 2, me.yn())
-        self._go(self._own(0), me.slot, 0, 0, me.sib())
-        self._go(self._own(1), me.slot, 1, 0, me.sib())
-        self._go(self._own(1), me.slot, 1, 1, me.xn())
-        self._go(self._own(0), me.slot, 0, 2, me.yn())
+        self._go(True, me.slot, 0, 1, me.xn)
+        self._go(True, me.slot, 1, 2, me.yn)
+        self._go(True, me.slot, 0, 0, me.sib)
+        self._go(True, me.slot, 1, 0, me.sib)
+        self._go(True, me.slot, 1, 1, me.xn)
+        self._go(True, me.slot, 0, 2, me.yn)
 
     def relay(self):
         me, rows = self.me, self.rows
         self._await(rows[1], 0, 1)
-        self._go(self._blk(rows[1], 0), rows[1], 0, 3, me.yn())
-        self._go(self._blk(rows[1], 0), rows[1], 0, 4, me.sib())
+        self._go(False, rows[1], 0, 3, me.yn)
+        self._go(False, rows[1], 0, 4, me.sib)
         self._await(rows[2], 1, 2)
-        self._go(self._blk(rows[2], 1), rows[2], 1, 3, me.xn())
-        self._go(self._blk(rows[2], 1), rows[2], 1, 5, me.sib())
+        self._go(False, rows[2], 1, 3, me.xn)
+        self._go(False, rows[2], 1, 5, me.sib)
 
     def share(self):
         me, rows = self.me, self.rows
         self._await(rows[1], 1, 1)
-        self._go(self._blk(rows[1], 1), rows[1], 1, 4, me.sib())
+        self._go(False, rows[1], 1, 4, me.sib)
         self._await(rows[2], 0, 2)
-        self._go(self._blk(rows[2], 0), rows[2], 0, 5, me.sib())
+        self._go(False, rows[2], 0, 5, me.sib)
 
     def last(self):
         me, rows = self.me, self.rows
         for h in (0, 1):
             self._await(rows[3], h, 3)
-            self._go(self._blk(rows[3], h), rows[3], h, 6, me.sib())
+            self._go(False, rows[3], h, 6, me.sib)
 
     def finish(self):
         for kind in (0, 4, 5, 6):
             for h in (0, 1):
                 self._await(self.rows[kind], h, kind)
-        for cp in self.sent:
-            cp.wait_send()
+        for i in range(len(self.sent)):
+            self._copy(i).wait_send()
         self.here.wait()
 
 
@@ -140,23 +145,22 @@
     RECVS = 10
 
     @staticmethod
-    def scratch(rows, width):
-        return [
-            pltpu.VMEM((2, rows, width), BF16),
-            pltpu.VMEM((4, rows, width), BF16),
-            pltpu.VMEM((2, rows // 2, width), BF16),
-            pltpu.VMEM((2, rows, width), BF16),
-            pltpu.SemaphoreType.DMA((Scatter.SENDS,)),
-            pltpu.SemaphoreType.DMA((Scatter.RECVS,)),
-        ]
+    def scratch(rows, width, cores=True, chips=True):
+        bufs = []
+        if cores:
+            bufs.append(pltpu.VMEM((2, rows, width), BF16))
+        bufs.append(pltpu.VMEM((4, rows, width), BF16))
+        if chips:
+            bufs += [pltpu.VMEM((2, rows // 2, width), BF16), pltpu.VMEM((2, rows, width), BF16)]
+        return bufs + [pltpu.SemaphoreType.DMA((Scatter.SENDS,)), pltpu.SemaphoreType.DMA((Scatter.RECVS,))]
 
     def __init__(self, me, out, red, diag, near, send, recv):
         self.me, self.out, self.red, self.diag, self.near = me, out, red, diag, near
         self.send, self.recv = send, recv
-        self.half = diag.shape[1]
+        self.half = red.shape[1] // 2
 
     def _sib(self, k):
-        return remote(self.out.at[lax.rem(k, 2)], self.red.at[k], self.send.at[k], self.recv.at[k], self.me.sib())
+        return remote(self.out.at[lax.rem(k, 2)], self.red.at[k], self.send.at[k], self.recv.at[k], self.me.sib)
 
     def put_sib(self, k, value):
         @pl.when(k >= 2)
@@ -174,12 +178,12 @@
         h, me = self.half, self.me
         lo, hi = pl.ds(0, h), pl.ds(h, h)
         src, dst, i, dev = {
-            "da": (self.red.at[0, lo], self.diag.at[0], 4, me.xn()),
-            "db": (self.red.at[0, hi], self.diag.at[1], 5, me.yn()),
-            "xa": (self.red.at[1, lo], self.near.at[0, lo], 6, me.xn()),
-            "xb": (self.red.at[1, hi], self.near.at[0, hi], 7, me.xn()),
-            "ya": (self.red.at[2, lo], self.near.at[1, lo], 8, me.yn()),
-            "yb": (self.red.at[2, hi], self.near.at[1, hi], 9, me.yn()),
+            "da": (self.red.at[0, lo], self.diag.at[0], 4, me.xn),
+            "db": (self.red.at[0, hi], self.diag.at[1], 5, me.yn),
+            "xa": (self.red.at[1, lo], self.near.at[0, lo], 6, me.xn),
+            "xb": (self.red.at[1, hi], self.near.at[0, hi], 7, me.xn),
+            "ya": (self.red.at[2, lo], self.near.at[1, lo], 8, me.yn),
+            "yb": (self.red.at[2, hi], self.near.at[1, hi], 9, me.yn),
         }[name]
         return remote(src, dst, self.send.at[i], self.recv.at[i], dev)
 
@@ -196,6 +200,10 @@
         @pl.when(i == 5)
         def _():
             self._copy("yb").start()
+            self.turn()
+
+    def ahead(self):
+        self._copy("yb").start()
 
     def turn(self):
         h = self.half
@@ -213,48 +221,145 @@
     def total(self, at):
         return self.red[3, at].astype(F32) + self.near[0, at].astype(F32) + self.near[1, at].astype(F32)
 
-    def finish(self):
+    def finish_cores(self):
         for k in (2, 3):
             self._sib(k).wait_send()
+
+    def finish_chips(self):
         for name in ("da", "db", "xa", "xb", "ya", "yb"):
             self._copy(name).wait_send()
 
 
-class Chain:
+class Spread:
     def __init__(self, me, blocks, send, recv):
         self.me, self.blocks, self.send, self.recv = me, blocks, send, recv
 
-    def _copy(self, b, way, hop):
-        to = self.me.g + 1 if way == 0 else self.me.g - 1
-        return remote(self.blocks(b), self.blocks(b), self.send.at[way, hop], self.recv.at[b], self.me.plane_dev(to))
-
-    def _each(self, hop, act):
-        g, z = self.me.g, self.me.planes
-        for way, b, have, more in ((0, g - hop, g - hop >= 0, g + 1 < z), (1, g + hop, g + hop < z, g >= 1)):
-            act(way, b, have, more)
-
-    def hop(self, hop):
-        def act(way, b, have, more):
-            @pl.when(have)
+    def _copy(self, b, t, i):
+        return remote(self.blocks(b), self.blocks(b), self.send.at[i], self.recv.at[b], self.me.plane_dev(t))
+
+    def _sends(self, b):
+        last = self.me.planes - 1
+        if b in (0, last):
+            return [(b, 1 if b == 0 else last - 1, 0)] + [(b, t, 1) for t in sorted(range(last + 1), key=lambda t: abs(t - b))[2:]]
+        other, end = (2, 0) if b == 1 else (1, 3)
+        return [(b, b - 1, 0), (b, b + 1, 0), (other, end, 1)]
+
+    def _each(self, act, steps):
+        for g in range(self.me.planes):
+
+            @pl.when(self.me.g == g)
             def _():
-                if hop > 0:
-                    self._copy(b, way, hop).wait_recv()
-
-                @pl.when(more)
-                def _():
-                    self._copy(b, way, hop).start()
-
-        self._each(hop, act)
+                for i, (b, t, step) in enumerate(self._sends(g)):
+                    if step in steps:
+                        act(self._copy(b, t, i))
+
+    def near(self):
+        self._each(lambda cp: cp.start(), (0,))
+
+    def settle(self):
+        inner = (self.me.g == 0) | (self.me.g == 2)
+
+        @pl.when(inner)
+        def _():
+            self._copy(1, 0, 0).wait_recv()
+
+        @pl.when(jnp.logical_not(inner))
+        def _():
+            self._copy(2, 0, 0).wait_recv()
+
+    def rest(self):
+        self._each(lambda cp: cp.start(), (1,))
+
+    def arrive(self):
+        for g in range(self.me.planes):
+
+            @pl.when(self.me.g == g)
+            def _():
+                for b in range(self.me.planes):
+                    if b not in (g, 1 if g in (0, 2) else 2):
+                        self._copy(b, b, 0).wait_recv()
 
     def finish(self):
-        for hop in range(self.me.planes):
-
-            def act(way, b, have, more):
-                @pl.when(jnp.logical_and(have, more))
-                def _():
-                    self._copy(b, way, hop).wait_send()
-
-            self._each(hop, act)
+        self._each(lambda cp: cp.wait_send(), (0, 1))
+
+
+class Collect:
+    def __init__(self, me, blocks, landing, via, send, recv):
+        self.me, self.blocks, self.landing, self.via, self.send, self.recv = me, blocks, landing, via, send, recv
+        self.by = {(0, 3): 1, (3, 0): 2} if me.planes == 4 else {}
+
+    def _copy(self, b, t, src, i):
+        at = (b - t) % self.me.planes - 1
+        return remote(src, self.landing.at[at], self.send.at[i], self.recv.at[at], self.me.plane_dev(t))
+
+    def _plan(self, b):
+        combined = [t for (s, t), by in self.by.items() if by == b]
+        direct = [t for t in range(self.me.planes) if t != b and t not in combined]
+        direct.sort(key=lambda t: -abs(t - b))
+        return [(t, (b, t) in self.by, i) for i, t in enumerate(direct)]
+
+    def _each(self, b, act):
+        @pl.when(self.me.g == b)
+        def _():
+            for t, through, i in self._plan(b):
+                if through:
+                    z = self.me.planes
+                    by = self.by[(b, t)]
+                    act(remote(self.blocks(t), self.via, self.send.at[i], self.recv.at[z - 1], self.me.plane_dev(by)))
+                else:
+                    act(self._copy(b, t, self.blocks(t), i))
+
+    def start(self):
+        for b in range(self.me.planes):
+            self._each(b, lambda cp: cp.start())
+
+    def _combined(self, b, t):
+        return self._copy(b, t, self.via, self.me.planes - 2)
+
+    def combine(self, own):
+        for (s, t), by in self.by.items():
+
+            @pl.when(self.me.g == by)
+            def _():
+                z = self.me.planes
+                remote(self.via, self.via, self.send.at[0], self.recv.at[z - 1], self.me.plane_dev(by)).wait_recv()
+                for q in range(self.via.shape[0]):
+                    self.via[q] = (self.via[q].astype(F32) + own(t)[q].astype(F32)).astype(BF16)
+                self._combined(by, t).start()
+
+    def clear(self):
+        for s, t in self.by:
+
+            @pl.when(self.me.g == t)
+            def _():
+                at = (s - t) % self.me.planes - 1
+                self.landing[at] = jnp.zeros(self.landing.shape[1:], BF16)
+
+    def total(self, out, own):
+        z = self.me.planes
+        for t in range(z):
+
+            @pl.when(self.me.g == t)
+            def _():
+                for b in range(z):
+                    if b != t and (b, t) not in self.by:
+                        at = (b - t) % z - 1
+                        self._copy(b, t, self.landing.at[at], 0).wait_recv()
+
+        for q in range(out.shape[0]):
+            value = own[q].astype(F32)
+            for at in range(z - 1):
+                value = value + self.landing[at, q].astype(F32)
+            out[q] = value.astype(BF16)
+
+    def finish(self):
+        for b in range(self.me.planes):
+            self._each(b, lambda cp: cp.wait_send())
+        for (s, t), by in self.by.items():
+
+            @pl.when(self.me.g == by)
+            def _():
+                self._combined(by, t).wait_send()
 
 
 def order(me, i):
@@ -606,16 +711,70 @@
 
 
 def forward_kernel(cfg, *refs):
-    (tok, ct, w_a, w_b, w_d, w_o, meta, kern, mix,
+    (tok, ct, w_qkv, w_gate, w_up, w_down, w_o, gain_cols, docs, pads, kern, mix,
      tok_all, ct_all, a_all, b_all, d_all, o_all, nrm_all, qkv_all, p_all, m_all, gated_all, mid_all, resid, gains, ends,
+     wq_v, w_a, w_b, meta,
      x_v, wa_v, wo_v, t_v, cat_v, shift_v, qkv_v, p_v, m_v, gated_v, meta_v, mid_v, tok_v,
      out_v, red, diag, near, rs_send, rs_recv,
-     g_send, g_recv, g_loc, a_send, a_recv, ch_send, ch_recv, o_send, o_recv, meta_send, meta_recv, loc, row_in, row_out) = refs
+     g_send, g_recv, g_loc, a_send, a_recv, ch_send, ch_recv, o_send, o_recv, meta_send, meta_recv, meet_sems, loc, pack, row_in, row_out) = refs
     planes, dh, taps_q, taps_k = cfg["planes"], cfg["dh"], cfg["kq"], cfg["kk"]
     length, width = tok.shape
     per_pair = o_all.shape[0]
     scale = dh ** (-0.5)
+    ff, chunk = cfg["ff"], cfg["ff"] // planes
     me = Place(planes)
+
+    wq_in = pltpu.make_async_copy(w_qkv, wq_v, loc.at[1])
+    wq_in.start()
+    tok_in = pltpu.make_async_copy(tok, tok_v, loc.at[0])
+    tok_in.start()
+    down_in = pltpu.make_async_copy(w_down.at[pl.ds(me.y * chunk, chunk)], d_all.at[me.g], loc.at[3])
+    down_in.start()
+
+    def columns(j, s, z):
+        at = pl.multiple_of(z * (2 * PLANE * chunk) + s * (2 * chunk) + me.y * chunk, 128)
+        src = (w_gate, w_up)[j].at[:, pl.ds(at, chunk)]
+        return pltpu.make_async_copy(src, w_b.at[s, :, pl.ds(j * ff + z * chunk, chunk)], pack.at[j, s, z])
+
+    for j in range(2):
+        for s in range(PLANE):
+            for z in range(planes):
+                columns(j, s, z).start()
+
+    places = lanes(8, length).astype(F32)
+    last = length * 1.0
+    reach = [docs[0, 0]]
+    for k in range(1, docs.shape[1]):
+        reach.append(reach[-1] + docs[0, k])
+    own_end = jnp.full((8, length), last, F32)
+    for end in reversed(reach):
+        own_end = jnp.where(places < end.astype(F32), end.astype(F32), own_end)
+    meta[...] = jnp.where(places < last - pads[0].astype(F32), own_end, places + 1.0)
+
+    wq_in.wait()
+    low = lanes(w_qkv.shape[0], 128) < 64
+    for s in range(PLANE):
+        base = (me.y if s % 2 == 0 else planes - 1 - me.y) * (4 * dh)
+
+        def part(j):
+            blk = wq_v[:, pl.ds(pl.multiple_of(j * width + base, 128), 4 * dh)].astype(F32)
+            t0, t1, t2 = blk[:, 0:128], blk[:, 128:256], blk[:, 256:384]
+            if s // 2 == 0:
+                return t0, t1
+            t1, t2 = pltpu.roll(t1, 64, 1), pltpu.roll(t2, 64, 1)
+            return jnp.where(low, t1, t2), t2
+
+        (q0, q1), (k0, k1), (v0, v1) = part(0), part(1), part(2)
+        tiles = (
+            q0,
+            jnp.where(low, q1, pltpu.roll(v1, 64, 1)),
+            k0,
+            jnp.where(low, k1, pltpu.roll(gain_cols[...], 64, 1)),
+            v0,
+        )
+        for i, t in enumerate(tiles):
+            w_a[s, :, i * 128 : (i + 1) * 128] = t.astype(BF16)
+
     me.greet()
 
     def first(src, dst_all, base):
@@ -633,7 +792,7 @@
         for d in range(1, PLANE):
             s = lax.rem(me.s - d + PLANE, PLANE)
             blk = dst_all.at[me.g * PLANE + s]
-            remote(blk, blk, a_send.at[base + d], a_recv.at[base + d], me.sib()).wait_recv()
+            remote(blk, blk, a_send.at[base + d], a_recv.at[base + d], me.sib).wait_recv()
         own.wait()
 
     meta_sent = []
@@ -650,106 +809,112 @@
     sent_a, own_a = first(w_a, a_all, 0)
     tokens = Gather(me, tok, tok_all, g_send.at[0], g_recv.at[0], g_loc.at[0])
     tokens.start()
-    tok_in = pltpu.make_async_copy(tok, tok_v, loc.at[0])
-    tok_in.start()
+
+    o_y = jnp.where((me.g == 1) | (me.g == 2), 1, 0)
+    o_c = jnp.where(me.g >= 2, 1, 0)
+    o_here = pltpu.make_async_copy(w_o, o_all.at[me.c], o_send.at[0])
+    o_sib = remote(w_o, o_all.at[me.c], o_send.at[0], o_recv.at[0], me.sib)
+
+    @pl.when((o_y == me.y) & (o_c == me.c))
+    def _():
+        o_here.start()
+
+    @pl.when((o_y == me.y) & (o_c != me.c))
+    def _():
+        o_sib.start()
+
+    def o_next(way):
+        return remote(o_all, o_all, o_send.at[1 + way], o_recv.at[1], me.plane_dev(me.g + 1 - 2 * way))
+
+    def o_each(act):
+        @pl.when((me.g >= me.home) & (me.g + 1 < planes))
+        def _():
+            act(o_next(0))
+
+        @pl.when((me.g <= me.home) & (me.g >= 1))
+        def _():
+            act(o_next(1))
+
+    apart = jnp.where(me.g > me.home, me.g - me.home, me.home - me.g)
+    inner = (me.g == 1) | (me.g == 2)
+
+    def o_from_home():
+        o_here.wait()
+        remote(o_all.at[1 - me.c], o_all.at[1 - me.c], o_send.at[0], o_recv.at[0], me.sib).wait_recv()
+        o_each(lambda cp: cp.start())
+
+    def o_pass_on():
+        o_next(0).wait_recv()
+        o_each(lambda cp: cp.start())
 
     blocks4 = lambda ref: (lambda b: ref.at[pl.ds(b * PLANE, PLANE)])
-    chain_a = Chain(me, blocks4(a_all), ch_send.at[0], ch_recv.at[0])
-    chain_b = Chain(me, blocks4(b_all), ch_send.at[1], ch_recv.at[1])
-    chain_d = Chain(me, lambda b: d_all.at[b], ch_send.at[2], ch_recv.at[2])
+    spread_a = Spread(me, blocks4(a_all), ch_send.at[0], ch_recv.at[0])
+    spread_b = Spread(me, blocks4(b_all), ch_send.at[1], ch_recv.at[1])
+    spread_d = Spread(me, lambda b: d_all.at[b], ch_send.at[2], ch_recv.at[2])
 
     for g in range(2):
         for a in range(taps_q):
             t = band(kern, 2 * me.pair + g, a, taps_q, taps_k, length, False)
-            hi = t.astype(BF16)
-            t_v[g, 0, a * length : (a + 1) * length] = hi
-            t_v[g, 1, a * length : (a + 1) * length] = (t - hi.astype(F32)).astype(BF16)
-    shift_v[0:8] = jnp.zeros((8, length), F32)
+            high = t.astype(BF16)
+            at = slice(a * length, (a + 1) * length)
+            t_v[g, 0:length, at] = high
+            t_v[g, length : 2 * length, at] = high
+            t_v[g, 2 * length :, at] = (t - high.astype(F32)).astype(BF16)
+    shift_v[0:8] = jnp.zeros((8, taps_q * length), F32)
     wo_v[...] = jnp.zeros(wo_v.shape, BF16)
 
+    pl.when((apart == 0) & jnp.logical_not(inner))(o_from_home)
     first_wait(w_a, a_all, 0, own_a)
-    chain_a.hop(0)
-
-    src_pair = lax.div(me.f, per_pair)
-    src_y, src_s = lax.div(src_pair, 4), lax.rem(src_pair, 2) * 2 + lax.rem(lax.div(src_pair, 2), 2)
-    src_j = lax.rem(me.f, per_pair)
-
-    def o_copy(g):
-        return remote(w_o, o_all.at[src_j], o_send.at[g], o_recv.at[src_j], (me.y, g * PLANE + src_s))
-
-    o_here = pltpu.make_async_copy(w_o, o_all.at[src_j], o_send.at[planes])
-
-    def o_each(act, act_here):
-        for g in range(planes):
-            mine = g * PLANE + src_s == me.f
-
-            if act is not None:
-
-                @pl.when((src_y == me.y) & jnp.logical_not(mine))
-                def _():
-                    act(o_copy(g))
-
-        if act_here is not None:
-
-            @pl.when((src_y == me.y) & (src_s == me.s))
-            def _():
-                act_here(o_here)
-
-    o_each(lambda cp: cp.start(), lambda cp: cp.start())
+    spread_a.near()
+    pl.when((apart == 0) & inner)(o_from_home)
+    pl.when((apart == 1) & inner & (me.y == 0))(o_pass_on)
 
     tokens.relay()
-    for hop in range(1, planes - 1):
-        chain_a.hop(hop)
+    for j in range(2):
+        for s in range(PLANE):
+            for z in range(planes):
+                columns(j, s, z).wait()
+    sent_b, own_b = first(w_b, b_all, PLANE)
+    cots = Gather(me, ct, ct_all, g_send.at[1], g_recv.at[1], g_loc.at[1])
+    cots.start()
+    spread_a.settle()
+    meet(me, meet_sems.at[0])
+    spread_a.rest()
+
+    down_in.wait()
+
     tokens.share()
     tokens.last()
-    sent_b, own_b = first(w_b, b_all, PLANE)
     tokens.finish()
-    cots = Gather(me, ct, ct_all, g_send.at[1], g_recv.at[1], g_loc.at[1])
-    cots.start()
-    for r in range(GROUP):
-        pltpu.make_async_copy(tok_all.at[r], x_v.at[r], row_in.at[r]).start()
-    chain_a.hop(planes - 1)
-
+    for row in range(GROUP):
+        pltpu.make_async_copy(tok_all.at[row], x_v.at[row], row_in.at[row]).start()
+    first_wait(w_b, b_all, PLANE, own_b)
+
+    spread_a.arrive()
     wa_in = pltpu.make_async_copy(a_all, wa_v, loc.at[1])
     wa_in.start()
-    for j in range(per_pair):
-        from_f = me.pair * per_pair + j
-
-        @pl.when(from_f != me.f)
-        def _():
-            remote(w_o, o_all.at[j], o_send.at[0], o_recv.at[j], me.sib()).wait_recv()
-
-    o_each(None, lambda cp: cp.wait())
-    wo_in = pltpu.make_async_copy(o_all, wo_v.at[pl.ds(0, per_pair)], loc.at[2])
-    wo_in.start()
-    pltpu.make_async_copy(w_d, d_all.at[me.g], loc.at[3]).start()
-    pltpu.make_async_copy(w_d, d_all.at[me.g], loc.at[3]).wait()
-    first_wait(w_b, b_all, PLANE, own_b)
+    pl.when((apart > 0) & inner & ((apart == 2) | (me.y == 1)))(o_pass_on)
+    spread_d.near()
+    spread_b.near()
     wa_in.wait()
-    chain_d.hop(0)
-    chain_b.hop(0)
-    wo_in.wait()
     for d in range(1, GROUP):
         fr = lax.rem(me.slot - d + GROUP, GROUP)
-        remote(meta, meta_v.at[fr], meta_send.at[d], meta_recv.at[d], me.sib()).wait_recv()
+        remote(meta, meta_v.at[fr], meta_send.at[d], meta_recv.at[d], me.sib).wait_recv()
     meta_here.wait()
     ends[...] = meta_v[...]
 
-    rows_o = per_pair * w_o.shape[0]
-    weights_a = wa_v[...].reshape(width, QKV)
-    gain_rows = jnp.transpose(weights_a[:, 384:512].astype(F32))
+    gain_rows = jnp.transpose(wa_v[:, :, 384:512].reshape(width, 128).astype(F32))
     gains[...] = jnp.zeros(gains.shape, F32)
     gains[0:1] = gain_rows[64:65]
     gains[1:2] = gain_rows[65:66]
-    heads_col = wo_v[:, :, width:].reshape(wo_v.shape[0] * wo_v.shape[1], 128).astype(F32)
-    gains[2:3] = jnp.concatenate(
-        [jnp.transpose(heads_col[0:SIDE])[0:1], jnp.zeros((1, width - SIDE), F32)], axis=1
-    )
+    heads_at = wa_v[pl.ds(me.pair * per_pair, per_pair), :, 384:512].reshape(2 * dh, 128).astype(F32)
+    heads_at = jnp.concatenate([heads_at, jnp.zeros((SIDE - 2 * dh, 128), F32)], axis=0)
+    gains[2:3, 0:SIDE] = jnp.transpose(heads_at)[66:67]
 
     h0, h1 = head_lanes(length, dh)
     scatter = Scatter(me, out_v, red, diag, near, rs_send, rs_recv)
 
-    def one(i, carry):
+    def attention(i):
         row, k = order(me, i)
         pltpu.make_async_copy(tok_all.at[row], x_v.at[row], row_in.at[row]).wait()
 
@@ -778,13 +943,14 @@
             raw = nt(q, kg) * scale
             masked = jnp.where(ok, raw, 0.0)
             m_v[row, g] = masked.astype(BF16)
-            shift_v[8 : 8 + length] = masked
-            for a in range(taps_q):
-                sh = shift_v[8 - a : 8 - a + length]
-                hi = sh.astype(BF16)
-                cat_v[0, :, a * length : (a + 1) * length] = hi
-                cat_v[1, :, a * length : (a + 1) * length] = (sh - hi.astype(F32)).astype(BF16)
-            conv = nn(cat_v[0], t_v[g, 0]) + nn(cat_v[1], t_v[g, 0]) + nn(cat_v[0], t_v[g, 1])
+            high = masked.astype(BF16)
+            cat_v[:, 0:length] = high
+            cat_v[:, length : 2 * length] = (masked - high.astype(F32)).astype(BF16)
+            cat_v[:, 2 * length :] = high
+            shift_v[8 : 8 + length] = nn(cat_v[...], t_v[g])
+            conv = shift_v[8 : 8 + length, 0:length]
+            for a in range(1, taps_q):
+                conv = conv + shift_v[8 - a : 8 - a + length, a * length : (a + 1) * length]
             logits = jnp.where(ok, conv, NEG_FILL)
             e = jnp.exp(logits - jnp.max(logits, axis=-1, keepdims=True))
             probs = e / jnp.sum(e, axis=-1, keepdims=True)
@@ -801,8 +967,14 @@
         gated = (scaled * gains[2:3, 0:SIDE]).astype(BF16)
         gated_v[row] = gated
         pltpu.make_async_copy(gated_v.at[row], gated_all.at[row], row_out.at[4, row]).start()
-        wo = wo_v[:, :, 0:width].reshape(wo_v.shape[0] * wo_v.shape[1], width)
-        part = nn(gated, wo[0:SIDE])
+        wo = wo_v[...].reshape(wo_v.shape[0] * wo_v.shape[1], width)
+
+    wo_in = pltpu.make_async_copy(o_all, wo_v.at[pl.ds(0, per_pair)], loc.at[2])
+
+    def project(i):
+        row, k = order(me, i)
+        wo = wo_v[...].reshape(wo_v.shape[0] * wo_v.shape[1], width)
+        part = nn(gated_v[row], wo[0:SIDE])
 
         @pl.when(lax.rem(i, 2) == 0)
         def _():
@@ -813,14 +985,50 @@
             scatter.put_self(k, part)
 
         scatter.push(i)
+
+    def one(i, carry):
+        attention(i)
+
+        @pl.when(i == LAG)
+        def _():
+            wo_in.wait()
+
+            def late(j, carry):
+                project(j)
+                return carry
+
+            lax.fori_loop(0, LAG, late, 0)
+
+        @pl.when(i >= LAG)
+        def _():
+            project(i)
+
+        @pl.when(i == 1)
+        def _():
+            cots.relay()
+
+            @pl.when((apart > 0) & jnp.logical_not(inner))
+            def _():
+                o_next(0).wait_recv()
+
+            wo_in.start()
+
+        @pl.when(i == 4)
+        def _():
+            spread_d.settle()
+            spread_b.settle()
+            meet(me, meet_sems.at[1])
+            spread_d.rest()
+            spread_b.rest()
+
+        @pl.when(i == 5)
+        def _():
+            cots.share()
+            cots.last()
+
         return carry
 
     lax.fori_loop(0, GROUP, one, 0)
-    cots.relay()
-    scatter.turn()
-    cots.share()
-    cots.last()
-    cots.finish()
     tok_in.wait()
     scatter.arrive()
 
@@ -833,19 +1041,23 @@
     strips(length, middle)
     mids = Gather(me, mid_v, mid_all, g_send.at[2], g_recv.at[2], g_loc.at[2])
     mids.start()
-    chain_d.hop(1)
-    chain_b.hop(1)
     mids.relay()
     mids.share()
     mids.last()
-    for hop in range(2, planes):
-        chain_d.hop(hop)
-        chain_b.hop(hop)
     mids.finish()
-    scatter.finish()
-    for ch in (chain_a, chain_b, chain_d):
-        ch.finish()
-    o_each(lambda cp: cp.wait_send(), None)
+    cots.finish()
+    spread_d.arrive()
+    spread_b.arrive()
+    scatter.finish_cores()
+    scatter.finish_chips()
+    for sp in (spread_a, spread_b, spread_d):
+        sp.finish()
+    o_each(lambda cp: cp.wait_send())
+
+    @pl.when((o_y == me.y) & (o_c != me.c))
+    def _():
+        o_sib.wait_send()
+
     for cp in meta_sent + sent_a + sent_b:
         cp.wait_send()
     for r in range(GROUP):
@@ -856,11 +1068,11 @@
         pltpu.make_async_copy(gated_v.at[r], gated_all.at[r], row_out.at[4, r]).wait()
 
 
-def forward_call(cfg, tok, ct, w_a, w_b, w_d, w_o, meta, kern, mix):
+def forward_call(cfg, tok, ct, w_qkv, w_gate, w_up, w_down, w_o, gain_cols, docs, pads, kern, mix):
     length, width = tok.shape
-    planes, ff, r = cfg["planes"], cfg["ff"], w_a.shape[1]
+    planes, ff, r = cfg["planes"], cfg["ff"], w_qkv.shape[0]
     n = planes * PLANE
-    chunk = w_d.shape[0]
+    chunk = ff // planes
     per_pair = n // GROUP
     taps = cfg["kq"] * length
     pad_rows = -(-SIDE // w_o.shape[0])
@@ -868,6 +1080,8 @@
     sds = jax.ShapeDtypeStruct
     rows = (GROUP, length)
     dma = pltpu.SemaphoreType.DMA
+    v16 = lambda *shape: pltpu.VMEM(shape, BF16)
+    v32 = lambda *shape: pltpu.VMEM(shape, F32)
     return pl.pallas_call(
         functools.partial(forward_kernel, cfg),
         out_shape=(
@@ -877,31 +1091,31 @@
             sds((GROUP, 2, 2, length, length), BF16), sds((GROUP, 2, length, length), BF16), sds(rows + (SIDE,), BF16),
             sds(rows + (width,), BF16), sds((length, width), F32), sds((8, width), F32), sds((GROUP, 8, length), F32),
         ),
-        in_specs=[hbm] * 7 + [smem] * 2,
+        in_specs=[hbm] * 7 + [vmem] + [smem] * 4,
         out_specs=(hbm,) * 12 + (vmem,) * 3,
         scratch_shapes=[
-            pltpu.VMEM(rows + (width,), BF16), pltpu.VMEM((n, r, QKV), BF16), pltpu.VMEM((pad_rows,) + w_o.shape, BF16),
-            pltpu.VMEM((2, 2, taps, length), BF16), pltpu.VMEM((2, length, taps), BF16), pltpu.VMEM((length + 8, length), F32),
-            pltpu.VMEM(rows + (3 * SIDE,), BF16), pltpu.VMEM((GROUP, 2, 2, length, length), BF16),
-            pltpu.VMEM((GROUP, 2, length, length), BF16), pltpu.VMEM(rows + (SIDE,), BF16),
-            pltpu.VMEM((GROUP, 8, length), F32), pltpu.VMEM((length, width), BF16), pltpu.VMEM((length, width), BF16),
+            v16(*w_qkv.shape), v16(PLANE, r, QKV), v16(PLANE, r, 2 * ff), v32(8, length),
+            v16(*rows, width), v16(n, r, QKV), v16(pad_rows, *w_o.shape),
+            v16(2, 3 * length, taps), v16(length, 3 * length), v32(length + 8, taps),
+            v16(*rows, 3 * SIDE), v16(GROUP, 2, 2, length, length), v16(GROUP, 2, length, length), v16(*rows, SIDE),
+            v32(GROUP, 8, length), v16(length, width), v16(length, width),
             *Scatter.scratch(length, width),
             dma((3, Gather.SENDS)), dma((3, Gather.RECVS)), dma((3,)), dma((2 * PLANE,)), dma((2 * PLANE,)),
-            dma((3, 2, planes)), dma((3, planes)), dma((planes + 1,)), dma((per_pair,)), dma((GROUP,)), dma((GROUP,)),
-            dma((4,)), dma((GROUP,)), dma((5, GROUP)),
+            dma((3, planes)), dma((3, planes)), dma((3,)), dma((2,)), dma((GROUP,)), dma((GROUP,)), pltpu.SemaphoreType.REGULAR((2,)),
+            dma((4,)), dma((2, PLANE, planes)), dma((GROUP,)), dma((5, GROUP)),
         ],
-        compiler_params=pltpu.CompilerParams(collective_id=1, has_side_effects=True, vmem_limit_bytes=50 * 2**20),
+        compiler_params=pltpu.CompilerParams(collective_id=1, has_side_effects=True, vmem_limit_bytes=52 * 2**20),
         name="attention_forward",
-    )(tok, ct, w_a, w_b, w_d, w_o, meta, kern, mix)
+    )(tok, ct, w_qkv, w_gate, w_up, w_down, w_o, gain_cols, docs, pads, kern, mix)
 
 
 def feed_kernel(cfg, *refs):
     (mid_all, ct_all, w_b, w_d, resid, gains,
-     layer_out, g_res, branch_all, dw_b, dw_d, g_mid_gain,
-     mid_v, ct_v, wb_v, wd_v, hid_v, gu_v, tile_v,
-     o_out, o_red, o_diag, o_near, o_send, o_recv,
+     g_res, branch_all, dw_b, sum_d, sum_first, out_red, g_mid_gain,
+     mid_v, ct_v, wb_v, wd_v, hid_v, gu_v, tile_v, dd_v, zd_v, via_v, sd_v, first_v, zf_v, via_f, sf_v,
+     o_out, o_red, o_send, o_recv,
      m_out, m_red, m_diag, m_near, m_send, m_recv,
-     g_send, g_recv, g_loc, loc, row_in, out_sem) = refs
+     g_send, g_recv, g_loc, z_send, z_recv, loc, row_in, out_sem) = refs
     length, width = resid.shape
     ff = cfg["ff"]
     me = Place(cfg["planes"])
@@ -920,7 +1134,11 @@
         for cp in row_copies(order(me, i)[0]):
             cp.start()
     me.greet()
-    sum_out = Scatter(me, o_out, o_red, o_diag, o_near, o_send, o_recv)
+    sum_out = Scatter(me, o_out, o_red, None, None, o_send, o_recv)
+    down_sum = Collect(me, lambda b: dd_v.at[pl.ds(b, 1)], zd_v, via_v, z_send.at[0], z_recv.at[0])
+    down_sum.clear()
+    first_sum = Collect(me, lambda b: first_v.at[pl.ds(b, 1)], zf_v, via_f, z_send.at[1], z_recv.at[1])
+    first_sum.clear()
     sum_mid = Scatter(me, m_out, m_red, m_diag, m_near, m_send, m_recv)
     wb_in.wait()
     wd_in.wait()
@@ -959,31 +1177,19 @@
         return carry
 
     lax.fori_loop(0, GROUP, one, 0)
-    sum_mid.turn()
 
     tokens = GROUP * length
     tile = SIDE
 
-    steps_down, steps_up = ff // tile, width // tile
-
-    def tile_out(i, down):
-        slot = lax.rem(i, 2)
-        if down:
-            src, dst = tile_v.at[slot], dw_d.at[pl.ds(pl.multiple_of(i * tile, tile), tile)]
-        else:
-            at = pl.ds(pl.multiple_of((i - steps_down) * tile, tile), tile)
-            src, dst = tile_v.at[slot, :, pl.ds(0, 2 * ff)], dw_b.at[at]
-        return pltpu.make_async_copy(src, dst, out_sem.at[slot])
-
     def down(i, carry):
         at = pl.ds(pl.multiple_of(i * tile, tile), tile)
-        tile_v[lax.rem(i, 2)] = tn(hid_v[:, :, at].reshape(tokens, tile), ct_v[...].reshape(tokens, width)).astype(BF16)
-        tile_out(i, True).start()
+        value = tn(hid_v[:, :, at].reshape(tokens, tile), ct_v[...].reshape(tokens, width)).astype(BF16)
+        per = tile // dd_v.shape[1]
+        dd_v[pl.ds(i * per, per)] = value.reshape((per,) + dd_v.shape[1:])
         return carry
 
-    lax.fori_loop(0, steps_down, down, 0)
-    for i in range(steps_down):
-        tile_out(i, True).wait()
+    lax.fori_loop(0, ff // tile, down, 0)
+    down_sum.start()
 
     g_mid_gain[...] = jnp.zeros(g_mid_gain.shape, F32)
     sum_mid.arrive()
@@ -1002,38 +1208,58 @@
     strips(length, middle)
     branch = Gather(me, ct_v.at[me.slot], branch_all, g_send, g_recv, g_loc.at[0])
     branch.start()
-    for i in (1, 3, 5):
-        sum_out.push(i)
+    red_out = pltpu.make_async_copy(o_red, out_red, out_sem.at[2])
+    red_out.start()
+
+    steps = width // tile
+
+    def tile_out(i):
+        slot = lax.rem(i, 2)
+        at = pl.ds(pl.multiple_of(i * tile, tile), tile)
+        return pltpu.make_async_copy(tile_v.at[slot], dw_b.at[at], out_sem.at[slot])
 
     def gate_up(i, carry):
-        @pl.when(i >= steps_down + 2)
-        def _():
-            tile_out(i - 2, False).wait()
-
-        at = pl.ds(pl.multiple_of((i - steps_down) * tile, tile), tile)
-        value = tn(mid_v[:, :, at].reshape(tokens, tile), gu_v[...].reshape(tokens, 2 * ff))
-        tile_v[lax.rem(i, 2), :, 0 : 2 * ff] = value.astype(BF16)
-        tile_out(i, False).start()
+        @pl.when(i >= 2)
+        def _():
+            tile_out(i - 2).wait()
+
+        at = pl.ds(pl.multiple_of(i * tile, tile), tile)
+        value = tn(mid_v[:, :, at].reshape(tokens, tile), gu_v[...].reshape(tokens, 2 * ff)).astype(BF16)
+        tile_v[lax.rem(i, 2)] = value
+        tile_out(i).start()
+        for z in range(first_v.shape[0]):
+            lo = z * PLANE * first_v.shape[1]
+
+            @pl.when(i == lo // tile)
+            def _():
+                first_v[z] = value[lo % tile : lo % tile + first_v.shape[1]]
+
         return carry
 
-    end = steps_down + steps_up
-    lax.fori_loop(steps_down, steps_down + steps_up // 2, gate_up, 0)
+    lax.fori_loop(0, steps, gate_up, 0)
+    first_sum.start()
+    down_sum.combine(lambda t: dd_v.at[pl.ds(t, 1)])
     branch.relay()
-    lax.fori_loop(steps_down + steps_up // 2, end, gate_up, 0)
     branch.share()
-    sum_out.turn()
+    first_sum.combine(lambda t: first_v.at[pl.ds(t, 1)])
     branch.last()
-    sum_out.arrive()
-
-    def result(at):
-        layer_out[at] = resid[at] + sum_out.total(at)
-
-    strips(length, result)
+    down_sum.total(sd_v, dd_v.at[pl.ds(me.g, 1)])
+    sd_out = pltpu.make_async_copy(sd_v.at[0], sum_d, out_sem.at[3])
+    sd_out.start()
+    first_sum.total(sf_v, first_v.at[pl.ds(me.g, 1)])
+    sf_out = pltpu.make_async_copy(sf_v.at[0], sum_first, out_sem.at[4])
+    sf_out.start()
     branch.finish()
-    sum_mid.finish()
-    sum_out.finish()
-    tile_out(end - 2, False).wait()
-    tile_out(end - 1, False).wait()
+    sum_mid.finish_cores()
+    sum_mid.finish_chips()
+    sum_out.finish_cores()
+    down_sum.finish()
+    first_sum.finish()
+    tile_out(steps - 2).wait()
+    tile_out(steps - 1).wait()
+    red_out.wait()
+    sd_out.wait()
+    sf_out.wait()
 
 
 def feed_call(cfg, mid_all, ct_all, w_b, w_d, resid, gains):
@@ -1043,45 +1269,53 @@
     sds = jax.ShapeDtypeStruct
     dma = pltpu.SemaphoreType.DMA
     rows = (GROUP, length)
+    chunk = ff // cfg["planes"]
+    others = cfg["planes"] - 1
+    r = w_b.shape[1]
+    v16 = lambda *shape: pltpu.VMEM(shape, BF16)
     return pl.pallas_call(
         functools.partial(feed_kernel, cfg),
         out_shape=(
-            sds((length, width), F32), sds((length, width), F32), sds(rows + (width,), BF16),
-            sds((width, 2 * ff), BF16), sds((ff, width), BF16), sds((8, width), F32),
+            sds((length, width), F32), sds(rows + (width,), BF16),
+            sds((width, 2 * ff), BF16), sds((chunk, width), BF16), sds((r, 2 * ff), BF16), sds((4, length, width), BF16), sds((8, width), F32),
         ),
         in_specs=[hbm] * 4 + [vmem] * 2,
-        out_specs=(vmem, vmem, hbm, hbm, hbm, vmem),
+        out_specs=(vmem, hbm, hbm, hbm, hbm, hbm, vmem),
         scratch_shapes=[
-            pltpu.VMEM(rows + (width,), BF16), pltpu.VMEM(rows + (width,), BF16),
-            pltpu.VMEM(w_b.shape, BF16), pltpu.VMEM(w_d.shape, BF16),
-            pltpu.VMEM(rows + (ff,), BF16), pltpu.VMEM(rows + (2 * ff,), BF16),
-            pltpu.VMEM((2, SIDE, width), BF16),
-            *Scatter.scratch(length, width), *Scatter.scratch(length, width),
-            dma((Gather.SENDS,)), dma((Gather.RECVS,)), dma((1,)), dma((2,)), dma((2, GROUP)), dma((2,)),
+            v16(*rows, width), v16(*rows, width), v16(*w_b.shape), v16(*w_d.shape), v16(*rows, ff), v16(*rows, 2 * ff),
+            v16(2, SIDE, 2 * ff), v16(others + 1, chunk, width), v16(others, 1, chunk, width), v16(1, chunk, width), v16(1, chunk, width),
+            v16(others + 1, r, 2 * ff), v16(others, 1, r, 2 * ff), v16(1, r, 2 * ff), v16(1, r, 2 * ff),
+            *Scatter.scratch(length, width, chips=False), *Scatter.scratch(length, width),
+            dma((Gather.SENDS,)), dma((Gather.RECVS,)), dma((1,)), dma((2, others + 1)), dma((2, others + 1)),
+            dma((2,)), dma((2, GROUP)), dma((5,)),
         ],
-        compiler_params=pltpu.CompilerParams(collective_id=2, has_side_effects=True, vmem_limit_bytes=50 * 2**20),
+        compiler_params=pltpu.CompilerParams(collective_id=2, has_side_effects=True, vmem_limit_bytes=52 * 2**20),
         name="feed_forward",
     )(mid_all, ct_all, w_b, w_d, resid, gains)
 
 
 def backward_kernel(cfg, *refs):
-    (branch_all, o_all, a_all, nrm_all, qkv_all, p_all, m_all, gated_all, dw_b, dw_d, tok, g_res, gains, ends, g_mid_gain, kern, mix,
-     g_tokens, out_a, out_b, out_d, out_o, out_small,
-     gb_v, wo_v, wa_v, nrm_v, qkv_v, p_v, m_v, gated_v, t_v, cat_v, shift_v, corr_v, gq_v, da_v, do_v, tok_v, rows_v, line_v,
-     zb_v, zd_v, za_v, zo_v, sb_v, sd_v, sa_v, so_v, own_b, own_d, small_v, small_in,
+    (branch_all, o_all, a_all, nrm_all, qkv_all, p_all, m_all, gated_all, dw_b, sum_d, sum_first, out_red, tok,
+     resid, g_res, gains, ends, g_mid_gain, kern, mix,
+     g_tokens, layer_out, out_a, out_b, out_d, out_o, out_small,
+     gb_v, wo_v, wa_v, nrm_v, qkv_v, p_v, m_v, t_v, cat_v, shift_v, corr_v, gq_v, da_v, do_v, tok_v, rows_v, line_v, taps_v,
+     zb_v, za_v, zo_v, via_b, via_a, via_o, sb_v, sa_v, so_v, far_b, strip_v, small_v, small_in,
      s_out, s_red, s_diag, s_near, rs_send, rs_recv,
-     z_send, z_recv, t_send, t_recv, loc, row_in) = refs
+     l_red, l_diag, l_near, l_send, l_recv,
+     z_send, z_recv, small_send, small_recv, t_send, t_recv, loc, row_in) = refs
     planes, dh, taps_q, taps_k = cfg["planes"], cfg["dh"], cfg["kq"], cfg["kk"]
     length, width = tok.shape
     scale = dh ** (-0.5)
     me = Place(planes)
     per_pair = o_all.shape[0]
     r = a_all.shape[1]
+    far = jnp.where(me.g == 1, planes - 1, 0)
     loads = [
         pltpu.make_async_copy(src, dst, loc.at[i])
         for i, (src, dst) in enumerate(
-            [(a_all, wa_v), (o_all, wo_v.at[pl.ds(0, per_pair)]), (tok, tok_v), (gated_all, gated_v)]
-            + [(dw_b.at[pl.ds(me.g * PLANE, PLANE)], own_b), (dw_d.at[me.g], own_d)]
+            [(a_all, wa_v), (o_all, wo_v.at[pl.ds(0, per_pair)]), (tok, tok_v)]
+            + [(dw_b.at[pl.ds(me.g * PLANE + 1, PLANE - 1)], sb_v.at[pl.ds(1, PLANE - 1)]), (sum_first, sb_v.at[0])]
+            + [(dw_b.at[pl.ds(far * PLANE + 1, PLANE - 1)], far_b), (out_red, l_red)]
         )
     ]
 
@@ -1089,7 +1323,7 @@
 
     def nrm_copy(j):
         at = pl.ds(j * span, span)
-        return pltpu.make_async_copy(nrm_all.at[:, :, at], nrm_v.at[j % 2], loc.at[6 + j % 2])
+        return pltpu.make_async_copy(nrm_all.at[:, :, at], nrm_v.at[j % 2], loc.at[7 + j % 2])
 
     def row_copies(i):
         row = order(me, i)[0]
@@ -1111,21 +1345,21 @@
         nrm_copy(j).start()
     me.greet()
 
-    def z_copies(kind, src_of, landing):
-        cps = []
-        for d in range(1, planes):
-            to = lax.rem(me.g + d, planes)
-            cps.append(remote(src_of(to), landing.at[d - 1], z_send.at[kind, d - 1], z_recv.at[kind, d - 1], me.plane_dev(to)))
-        return cps
-
     blocks4 = lambda ref: (lambda b: ref.at[pl.ds(b * PLANE, PLANE)])
-    send_d = z_copies(0, lambda b: dw_d.at[b], zd_v)
-    send_b = z_copies(1, blocks4(dw_b), zb_v)
-    send_a = z_copies(2, blocks4(da_v), za_v)
-    send_o = z_copies(3, lambda b: do_v.at[b], zo_v)
-    send_s = z_copies(4, lambda b: small_v, small_in)
-    for cp in send_d + send_b:
-        cp.start()
+    sum_b = Collect(me, lambda b: dw_b.at[pl.ds(b * PLANE + 1, PLANE - 1)], zb_v, via_b, z_send.at[0], z_recv.at[0])
+    sum_a = Collect(me, blocks4(da_v), za_v, via_a, z_send.at[1], z_recv.at[1])
+    sum_o = Collect(me, lambda b: do_v.at[pl.ds(b, 1)], zo_v, via_o, z_send.at[2], z_recv.at[2])
+    send_s = []
+    for d in range(1, planes):
+        to = lax.rem(me.g + d, planes)
+        send_s.append(remote(small_v, small_in.at[d - 1], small_send.at[d - 1], small_recv.at[d - 1], me.plane_dev(to)))
+    sum_b.start()
+    for group in (sum_b, sum_a, sum_o):
+        group.clear()
+    d_cp = remote(sum_d, out_d.at[me.y], t_send.at[3, 0], t_recv.at[3, 0], me.yn)
+    d_cp.start()
+    d_here = pltpu.make_async_copy(sum_d, out_d.at[me.y], t_send.at[3, 1])
+    d_here.start()
 
     for g in range(2):
         for a in range(taps_q):
@@ -1136,15 +1370,17 @@
     small_v[...] = jnp.zeros(small_v.shape, F32)
     h0, h1 = head_lanes(length, dh)
     scatter = Scatter(me, s_out, s_red, s_diag, s_near, rs_send, rs_recv)
+    layer = Scatter(me, None, l_red, l_diag, l_near, l_send, l_recv)
     loads[0].wait()
     loads[1].wait()
+    loads[5].wait()
 
     def one(i, carry):
         row, k = order(me, i)
         at = lax.rem(i, SLOTS)
         for cp in row_copies(i):
             cp.wait()
-        wo = wo_v[:, :, 0:width].reshape(wo_v.shape[0] * wo_v.shape[1], width)[0:SIDE]
+        wo = wo_v[...].reshape(wo_v.shape[0] * wo_v.shape[1], width)[0:SIDE]
         q, kk, v = qkv_v[at, :, 0:SIDE], qkv_v[at, :, SIDE : 2 * SIDE], qkv_v[at, :, 2 * SIDE : 3 * SIDE]
         parts = [nn(p_v[at, g, 0], v) + nn(p_v[at, g, 1], v) for g in range(2)]
         probs = [p_v[at, g, 0].astype(F32) + p_v[at, g, 1].astype(F32) for g in range(2)]
@@ -1200,13 +1436,24 @@
             for cp in row_copies(i + SLOTS):
                 cp.start()
 
+        @pl.when(i == 5)
+        def _():
+            sum_b.combine(lambda t: far_b)
+
         return carry
 
     lax.fori_loop(0, GROUP, one, 0)
-    scatter.turn()
-
-    for cp in loads[2:]:
-        cp.wait()
+    for i in (2, 3, 4, 6):
+        loads[i].wait()
+    for i in (1, 3):
+        layer.push(i)
+    layer.ahead()
+    gated_in = [
+        pltpu.make_async_copy(gated_all.at[i], p_v.at[i // 4, i // 2 % 2, i % 2], row_in.at[0, i]) for i in range(GROUP)
+    ]
+    for cp in gated_in:
+        cp.start()
+
     tokens = GROUP * length
     for j in range(planes):
         nrm_copy(j).wait()
@@ -1214,13 +1461,13 @@
         da_v[j * PLANE : (j + 1) * PLANE] = value.astype(BF16).reshape(PLANE, r, QKV)
         if j + 2 < planes:
             nrm_copy(j + 2).start()
-    for cp in send_a:
-        cp.start()
-    value = tn(gated_v[...].reshape(tokens, SIDE), gb_v[...].reshape(tokens, width))
+    sum_a.start()
+    for cp in gated_in:
+        cp.wait()
+    value = tn(p_v[...].reshape(tokens, SIDE), gb_v[...].reshape(tokens, width))
     do_v[...] = value[0 : 2 * dh].astype(BF16).reshape(do_v.shape)
-    for cp in send_o:
-        cp.start()
-
+
+    sum_o.start()
     def taps(at, carry):
         g, a = lax.div(at, taps_q), lax.rem(at, taps_q)
         lanes_at = pl.ds(pl.multiple_of(a * length, length), length)
@@ -1228,11 +1475,14 @@
         diff = lax.broadcasted_iota(jnp.int32, (length, length), 0) - lax.broadcasted_iota(jnp.int32, (length, length), 1)
         for b in range(taps_k):
             line = jnp.sum(jnp.where(diff == b - taps_k // 2, e, 0.0), axis=0, keepdims=True)
-            small_v[at, b : b + 1] = line[:, 0:128] + line[:, 128:256]
+            taps_v[b : b + 1] = line[:, 0:128] + line[:, 128:256]
+        each = jnp.sum(taps_v[...], axis=-1, keepdims=True)
+        small_v[0] = jnp.where(lanes(16, 128) == at, each, small_v[0])
         return carry
 
+    taps_v[...] = jnp.zeros(taps_v.shape, F32)
     lax.fori_loop(0, 2 * taps_q, taps, 0)
-    base = 2 * taps_q
+    base = 1
     at = lanes(1, SIDE)
     for o in range(2):
         for g in range(2):
@@ -1271,97 +1521,95 @@
             y, sl = to_slot(d)
             cps.append(remote(src_of(sl), landing.at[me.slot], t_send.at[kind, d], t_recv.at[kind, d], (y, me.g * PLANE + sl)))
         cps.append(pltpu.make_async_copy(src_of(me.s), landing.at[me.slot], t_send.at[kind, 0]))
+        for cp in cps:
+            cp.start()
         return cps
 
     def group_wait(kind, cps, landing):
         for d in range(1, GROUP):
             fr = lax.rem(me.slot - d + GROUP, GROUP)
-            remote(landing.at[fr], landing.at[fr], t_send.at[kind, d], t_recv.at[kind, d], me.sib()).wait_recv()
+            remote(landing.at[fr], landing.at[fr], t_send.at[kind, d], t_recv.at[kind, d], me.sib).wait_recv()
         for cp in cps[:-1]:
             cp.wait_send()
         cps[-1].wait()
 
+    layer.turn()
+    sum_b.total(sb_v.at[pl.ds(1, PLANE - 1)], sb_v.at[pl.ds(1, PLANE - 1)])
+    b_cps = group_copies(0, lambda sl: sb_v.at[sl], out_b)
+
+    sum_a.combine(lambda t: da_v.at[pl.ds(t * PLANE, PLANE)])
+
+    sum_o.combine(lambda t: do_v.at[pl.ds(t, 1)])
+    sum_a.total(sa_v, da_v.at[pl.ds(me.g * PLANE, PLANE)])
+    a_cps = group_copies(1, lambda sl: sa_v.at[sl], out_a)
+
+    sum_o.total(so_v, do_v.at[pl.ds(me.g, 1)])
+    o_to = me.pair * per_pair + lax.div(me.g, 2)
+    o_half = lax.rem(me.g, 2)
+
+    def o_copy(y):
+        return remote(so_v.at[0], out_o.at[o_half], t_send.at[4, y], t_recv.at[4, o_half], (y, o_to))
+
+    o_here = pltpu.make_async_copy(so_v.at[0], out_o.at[o_half], t_send.at[4, 2])
+
+    def o_each(act, act_here):
+        for y in range(2):
+            mine = (y == me.y) & (o_to == me.f)
+
+            @pl.when(jnp.logical_not(mine))
+            def _():
+                act(o_copy(y))
+
+            @pl.when(mine)
+            def _():
+                act_here(o_here)
+
+    o_each(lambda cp: cp.start(), lambda cp: cp.start())
     for cp in send_s:
         cp.wait_recv()
     for cp in send_s:
         cp.wait_send()
     small_v[...] = small_v[...] + sum(small_in[d] for d in range(planes - 1))
     small_cps = group_copies(2, lambda sl: small_v, out_small)
-    for cp in small_cps:
+
+    layer.arrive()
+
+    def result(at):
+        cp = pltpu.make_async_copy(resid.at[at], strip_v, loc.at[0])
         cp.start()
-
-    def sums(landing, own):
-        total = own.astype(F32)
-        for d in range(planes - 1):
-            total = total + landing[d].astype(F32)
-        return total.astype(BF16)
-
-    for cp in send_d:
-        cp.wait_recv()
-    sd_v[...] = sums(zd_v, own_d[...])
-    d_cp = remote(sd_v, out_d.at[me.y], t_send.at[3, 0], t_recv.at[3, 0], me.yn())
-    d_cp.start()
-    d_here = pltpu.make_async_copy(sd_v, out_d.at[me.y], t_send.at[3, 1])
-    d_here.start()
-    for cp in send_b:
-        cp.wait_recv()
-    sb_v[...] = sums(zb_v, own_b[...])
-    b_cps = group_copies(0, lambda sl: sb_v.at[sl], out_b)
-    for cp in b_cps:
+        cp.wait()
+        strip_v[...] = strip_v[...] + layer.total(at)
+        cp = pltpu.make_async_copy(strip_v, layer_out.at[at], loc.at[0])
         cp.start()
-    for cp in send_o:
-        cp.wait_recv()
-    so_v[...] = sums(zo_v, do_v[me.g])
-    o_to = me.pair * per_pair + lax.div(me.g, 2)
-    o_half = lax.rem(me.g, 2)
-
-    def o_copy(y):
-        return remote(so_v, out_o.at[o_half], t_send.at[4, y], t_recv.at[4, o_half], (y, o_to))
-
-    o_here = pltpu.make_async_copy(so_v, out_o.at[o_half], t_send.at[4, 2])
-
-    def o_each(act, act_here):
-        for y in range(2):
-            mine = (y == me.y) & (o_to == me.f)
-
-            @pl.when(jnp.logical_not(mine))
-            def _():
-                act(o_copy(y))
-
-            @pl.when(mine)
-            def _():
-                act_here(o_here)
-
-    o_each(lambda cp: cp.start(), lambda cp: cp.start())
-    for cp in send_a:
-        cp.wait_recv()
-    sa_v[...] = sums(za_v, da_v[pl.ds(me.g * PLANE, PLANE)])
-    a_cps = group_copies(1, lambda sl: sa_v.at[sl], out_a)
-    for cp in a_cps:
-        cp.start()
+        cp.wait()
+
+    strips(length, result)
 
     group_wait(2, small_cps, out_small)
     d_cp.wait_send()
-    remote(out_d.at[1 - me.y], out_d.at[1 - me.y], t_send.at[3, 0], t_recv.at[3, 0], me.yn()).wait_recv()
+    remote(out_d.at[1 - me.y], out_d.at[1 - me.y], t_send.at[3, 0], t_recv.at[3, 0], me.yn).wait_recv()
     d_here.wait()
     group_wait(0, b_cps, out_b)
-    src_pair = lax.div(me.f, per_pair)
-    src_y, src_s = lax.div(src_pair, 4), lax.rem(src_pair, 2) * 2 + lax.rem(lax.div(src_pair, 2), 2)
+    src_y = jnp.where((me.g == 1) | (me.g == 2), 1, 0)
+    src_s = me.x * 2 + jnp.where(me.g >= 2, 1, 0)
     for h in range(2):
         src_f = (2 * lax.rem(me.f, per_pair) + h) * PLANE + src_s
 
         @pl.when(jnp.logical_not((src_y == me.y) & (src_f == me.f)))
         def _():
-            remote(out_o.at[h], out_o.at[h], t_send.at[4, 0], t_recv.at[4, h], me.sib()).wait_recv()
+            remote(out_o.at[h], out_o.at[h], t_send.at[4, 0], t_recv.at[4, h], me.sib).wait_recv()
 
     o_each(lambda cp: cp.wait_send(), lambda cp: cp.wait())
     group_wait(1, a_cps, out_a)
-    for cp in send_d + send_b + send_a + send_o:
-        cp.wait_send()
-    scatter.finish()
-
-
-def backward_call(cfg, branch_all, o_all, a_all, nrm_all, qkv_all, p_all, m_all, gated_all, dw_b, dw_d, tok, g_res, gains, ends, g_mid_gain, kern, mix):
+    for group in (sum_b, sum_a, sum_o):
+        group.finish()
+    scatter.finish_cores()
+    scatter.finish_chips()
+    layer.finish_chips()
+
+
+def backward_call(cfg, *args):
+    branch_all, o_all, a_all, tok = args[0], args[1], args[2], args[12]
     length, width = tok.shape
     planes, ff = cfg["planes"], cfg["ff"]
     n, r = a_all.shape[:2]
@@ -1369,40 +1617,129 @@
     taps = cfg["kq"] * length
     pad_rows = -(-SIDE // o_all.shape[1])
     piece = 2 * cfg["dh"] // planes
-    small = (2 * cfg["kq"] + 3, 16, 128)
+    small = (4, 16, 128)
     hbm, vmem, smem = pl.BlockSpec(memory_space=pl.ANY), pl.BlockSpec(memory_space=pltpu.VMEM), pl.BlockSpec(memory_space=pltpu.SMEM)
     sds = jax.ShapeDtypeStruct
     dma = pltpu.SemaphoreType.DMA
     rows = (GROUP, length)
+    others = planes - 1
     v16 = lambda *shape: pltpu.VMEM(shape, BF16)
     v32 = lambda *shape: pltpu.VMEM(shape, F32)
+    b_block, a_block, o_block = (PLANE - 1, r, 2 * ff), (PLANE, r, QKV), (1, piece, width)
     return pl.pallas_call(
         functools.partial(backward_kernel, cfg),
         out_shape=(
-            sds((length, width), F32), sds((GROUP, r, QKV), BF16), sds((GROUP, r, 2 * ff), BF16),
+            sds((length, width), F32), sds((length, width), F32), sds((GROUP, r, QKV), BF16), sds((GROUP, r, 2 * ff), BF16),
             sds((2, chunk, width), BF16), sds((2, piece, width), BF16), sds((GROUP,) + small, F32),
         ),
-        in_specs=[hbm] * 11 + [vmem] * 4 + [smem] * 2,
-        out_specs=(vmem,) + (hbm,) * 5,
+        in_specs=[hbm] * 14 + [vmem] * 4 + [smem] * 2,
+        out_specs=(vmem,) + (hbm,) * 6,
         scratch_shapes=[
             v16(*rows, width), v16(pad_rows, *o_all.shape[1:]), v16(n, r, QKV), v16(2, *rows, PLANE * r), v16(SLOTS, length, 3 * SIDE),
-            v16(SLOTS, 2, 2, length, length), v16(SLOTS, 2, length, length), v16(*rows, SIDE),
+            v16(SLOTS, 2, 2, length, length), v16(SLOTS, 2, length, length),
             v16(2, taps, length), v16(length, taps), v32(length + 8, length), v32(2, length, taps), v16(*rows, QKV),
-            v16(n, r, QKV), v16(planes, piece, width), v16(length, width), v32(8, SIDE), v32(8, width),
-            v16(planes - 1, PLANE, r, 2 * ff), v16(planes - 1, chunk, width), v16(planes - 1, PLANE, r, QKV), v16(planes - 1, piece, width),
-            v16(PLANE, r, 2 * ff), v16(chunk, width), v16(PLANE, r, QKV), v16(piece, width), v16(PLANE, r, 2 * ff), v16(chunk, width),
-            v32(*small), v32(planes - 1, *small),
-            *Scatter.scratch(length, width),
-            dma((5, planes - 1)), dma((5, planes - 1)), dma((5, GROUP)), dma((5, GROUP)), dma((8,)), dma((4, GROUP)),
+            v16(n, r, QKV), v16(planes, piece, width), v16(length, width), v32(8, SIDE), v32(8, width), v32(16, 128),
+            v16(others, *b_block), v16(others, *a_block), v16(others, *o_block), v16(*b_block), v16(*a_block), v16(*o_block),
+            v16(PLANE, r, 2 * ff), v16(*a_block), v16(*o_block), v16(*b_block), v32(64, width),
+            v32(*small), v32(others, *small),
+            *Scatter.scratch(length, width), *Scatter.scratch(length, width, cores=False),
+            dma((3, planes)), dma((3, planes)), dma((others,)), dma((others,)), dma((5, GROUP)), dma((5, GROUP)),
+            dma((9,)), dma((4, GROUP)),
         ],
         compiler_params=pltpu.CompilerParams(collective_id=3, has_side_effects=True, vmem_limit_bytes=54 * 2**20),
         name="attention_backward",
-    )(branch_all, o_all, a_all, nrm_all, qkv_all, p_all, m_all, gated_all, dw_b, dw_d, tok, g_res, gains, ends, g_mid_gain, kern, mix)
-
-
-def pair_order(blocks):
-    rest = blocks.shape[1:]
-    return jnp.swapaxes(blocks.reshape((2, 2, 2) + rest), 1, 2).reshape((GROUP,) + rest)
+    )(*args)
+
+
+def results_kernel(cfg, a_ref, b_ref, d_ref, o_ref, small_ref, qkv_ref, gate_ref, up_ref, down_ref, out_ref, taps_ref, vec_ref):
+    planes, ff = cfg["planes"], cfg["ff"]
+    rows, width = out_ref.shape
+    chunk = ff // planes
+    low = lanes(rows, 128) < 64
+
+    def slot(pair):
+        home, x = pair // 2, pair % 2
+        y, c = (0, 1, 1, 0)[home], (0, 0, 1, 1)[home]
+        return y * PLANE + x * 2 + c
+
+    def joined(even, odd, low):
+        o0, o1 = pltpu.roll(odd[0], 64, 1), pltpu.roll(odd[1], 64, 1)
+        return even[0], jnp.where(low, even[1], o0), jnp.where(low, o0, o1)
+
+    def tiles(pair, j):
+        t = lambda i: a_ref[slot(pair), :, i * 128 : (i + 1) * 128].astype(F32)
+        if j == 2:
+            return t(4), pltpu.roll(t(1), 64, 1)
+        return t(2 * j), t(2 * j + 1)
+
+    for j in range(3):
+        for two in range(GROUP // 2):
+            for i, t in enumerate(joined(tiles(2 * two, j), tiles(2 * two + 1, j), low)):
+                at = j * width + two * 384 + i * 128
+                qkv_ref[:, at : at + 128] = t
+    for z in range(planes):
+        for s in range(PLANE):
+            for y in range(2):
+                at = ((z * PLANE + s) * 2 + y) * chunk
+                src = b_ref.at[y * PLANE + s]
+                gate_ref[:, at : at + chunk] = src[:, z * chunk : (z + 1) * chunk].astype(F32)
+                up_ref[:, at : at + chunk] = src[:, ff + z * chunk : ff + (z + 1) * chunk].astype(F32)
+    down_ref[...] = d_ref[0].astype(F32)
+    out_ref[...] = o_ref[0].astype(F32)
+
+    @pl.when(pl.program_id(0) == 0)
+    def _():
+        base = 1
+        for pair in range(GROUP):
+            mixed = jnp.sum(small_ref[slot(pair), base], axis=-1, keepdims=True)
+            taps_ref[pair] = jnp.where(lanes(16, 128) == 127, mixed, small_ref[slot(pair), 0])
+        vec_ref[...] = jnp.zeros(vec_ref.shape, F32)
+        for k in range(2):
+            total = small_ref[0, base + 1 + k]
+            for s in range(1, GROUP):
+                total = total + small_ref[s, base + 1 + k]
+            for j in range(width // 128):
+                vec_ref[k : k + 1, j * 128 : (j + 1) * 128] = total[j : j + 1]
+        line = lambda pair: tuple(small_ref[slot(pair), base, 4 + j : 5 + j] for j in range(2))
+        for two in range(GROUP // 2):
+            for i, t in enumerate(joined(line(2 * two), line(2 * two + 1), lanes(1, 128) < 64)):
+                vec_ref[2:3, two * 384 + i * 128 : two * 384 + (i + 1) * 128] = t
+
+
+def results_call(cfg, out_a, out_b, out_d, out_o, small):
+    r = out_a.shape[1]
+    _, chunk, width = out_d.shape
+    half = r // 2
+    sds = jax.ShapeDtypeStruct
+    whole = lambda shape: pl.BlockSpec(shape, lambda i: (0,) * len(shape))
+    rows = lambda n, w: pl.BlockSpec((n, w), lambda i: (i, 0))
+    moved = 2 * (out_a.size + out_b.size + out_d.size + out_o.size) + 4 * (out_a.size + out_b.size + out_d.size + out_o.size)
+    return pl.pallas_call(
+        functools.partial(results_kernel, cfg),
+        grid=(2,),
+        out_shape=(
+            sds((r, 3 * width), F32), sds((r, n_cols(cfg)), F32), sds((r, n_cols(cfg)), F32), sds((2 * chunk, width), F32),
+            sds((r, width), F32), sds((GROUP, 16, 128), F32), sds((8, width), F32),
+        ),
+        in_specs=[
+            pl.BlockSpec((GROUP, half, out_a.shape[2]), lambda i: (0, i, 0)),
+            pl.BlockSpec((GROUP, half, out_b.shape[2]), lambda i: (0, i, 0)),
+            pl.BlockSpec((1, chunk, width), lambda i: (i, 0, 0)),
+            pl.BlockSpec((1, half, width), lambda i: (i, 0, 0)),
+            whole(small.shape),
+        ],
+        out_specs=(
+            rows(half, 3 * width), rows(half, n_cols(cfg)), rows(half, n_cols(cfg)), rows(chunk, width), rows(half, width),
+            whole((GROUP, 16, 128)), whole((8, width)),
+        ),
+        compiler_params=pltpu.CompilerParams(vmem_limit_bytes=40 * 2**20),
+        cost_estimate=pl.CostEstimate(flops=0, bytes_accessed=moved, transcendentals=0),
+        name="results",
+    )(out_a, out_b, out_d, out_o, small)
+
+
+def n_cols(cfg):
+    return cfg["ff"] * GROUP
 
 
 def fits(mesh, tokens, kernel, w_gate):
@@ -1410,7 +1747,7 @@
     width, length, heads, ff = tokens.shape[2], tokens.shape[1], kernel.shape[0], w_gate.shape[1]
     return (
         mesh.shape["rep"] == 2
-        and n % GROUP == 0
+        and n == 4 * PLANE
         and heads == 2 * GROUP
         and width == heads * 96
         and (width // n) % 32 == 0
@@ -1444,68 +1781,30 @@
     chunk = w_down.shape[0] // 2
     ff = planes * chunk
     cfg = dict(planes=planes, dh=dh, kq=kq, kk=kk, ff=ff)
-    y = lax.axis_index("rep")
     f = lax.axis_index("fsdp")
 
-    with jax.named_scope("slices_to_send"):
-        by_pair = lax.dynamic_index_in_dim(w_qkv.reshape(r, 3, 2, 2, 2, 2 * dh), y, 2, keepdims=False)
-        by_pair = by_pair.transpose(3, 2, 0, 1, 4).reshape(PLANE, r, 3, 2 * dh)
-        gains_at = jnp.stack([norm_in, norm_mid], axis=1)
-        gains_at = jnp.broadcast_to(jnp.pad(gains_at, ((0, 0), (0, 62)))[None], (PLANE, r, 64))
-        w_a = jnp.concatenate(
-            [by_pair[:, :, 0], by_pair[:, :, 2, 128:], by_pair[:, :, 1], gains_at, by_pair[:, :, 2, :128]], axis=-1
+    gain_cols = jnp.stack([norm_in, norm_mid, norm_heads], axis=1).astype(F32)
+    gain_cols = jnp.pad(gain_cols, ((0, 0), (0, 125)))
+    tok, ct = tokens[0], cotangent[0]
+    kern = kernel.reshape(-1)
+
+    (_, ct_all, a_all, b_all, d_all, o_all, nrm_all, qkv_all, p_all, m_all, gated_all, mid_all, resid, gains, ends) = (
+        forward_call(
+            cfg, tok, ct, w_qkv, w_gate, w_up, w_down, w_out, gain_cols, doc_lengths, pad_counts, kern, mixing
         )
-
-        def columns(w):
-            w = lax.dynamic_index_in_dim(w.reshape(r, planes, PLANE, 2, chunk), y, 3, keepdims=False)
-            return w.transpose(2, 0, 1, 3).reshape(PLANE, r, ff)
-
-        w_b = jnp.concatenate([columns(w_gate), columns(w_up)], axis=-1)
-        w_d = lax.dynamic_index_in_dim(w_down.reshape(2, chunk, width), y, 0, keepdims=False)
-        w_o = jnp.concatenate([w_out, jnp.pad(norm_heads[:, None], ((0, 0), (0, 127)))], axis=1)
-        places = jnp.arange(length, dtype=jnp.int32)
-        doc_ends = jnp.cumsum(doc_lengths[0])
-        own_end = jnp.min(jnp.where(doc_ends[None, :] > places[:, None], doc_ends[None, :], length), axis=1)
-        ends = jnp.where(places < length - pad_counts[0], own_end, places + 1).astype(F32)
-        meta = jnp.broadcast_to(ends[None], (8, length))
-    tok, ct = tokens[0], cotangent[0]
-    kern_flat = kernel.reshape(-1)
-
-    (_, ct_all, a_all, b_all, d_all, o_all, nrm_all, qkv_all, p_all, m_all, gated_all, mid_all, resid, gains, ends_all) = (
-        forward_call(cfg, tok, ct, w_a, w_b, w_d, w_o, meta, kern_flat, mixing)
-    )
-    layer_out, g_res, branch_all, dw_b, dw_d, g_mid_gain = feed_call(
-        cfg, mid_all, ct_all, b_all, d_all, resid, gains
-    )
-    g_tokens, out_a, out_b, out_d, out_o, small = backward_call(
-        cfg, branch_all, o_all, a_all, nrm_all, qkv_all, p_all, m_all, gated_all, dw_b.reshape(n, r, 2 * ff),
-        dw_d.reshape(planes, chunk, width), tok, g_res, gains, ends_all, g_mid_gain, kern_flat, mixing,
-    )
-
-    with jax.named_scope("results"):
-        q = out_a[:, :, 0 : 2 * dh]
-        k = out_a[:, :, SIDE : SIDE + 2 * dh]
-        v = jnp.concatenate([out_a[:, :, 2 * SIDE :], out_a[:, :, 2 * dh : SIDE]], axis=-1)
-        g_qkv = jnp.stack([pair_order(part) for part in (q, k, v)]).transpose(2, 0, 1, 3)
-        g_qkv = g_qkv.reshape(r, 3 * width).astype(F32)
-
-        def whole(part):
-            part = part.reshape(2, PLANE, r, planes, chunk).transpose(2, 3, 1, 0, 4)
-            return part.reshape(r, n * 2 * chunk).astype(F32)
-
-        g_gate, g_up = whole(out_b[:, :, :ff]), whole(out_b[:, :, ff:])
-        g_down = out_d.reshape(2 * chunk, width).astype(F32)
-        g_out = out_o.reshape(r, width).astype(F32)
-        g_kernel = pair_order(small[:, : 2 * kq, :kk].sum(-1)).reshape(heads, kq, kk)
-        base = 2 * kq
-        g_mixing = pair_order(small[:, base, 0:4].sum(-1)).reshape(heads, 2)
-
-        def own(line):
-            return lax.dynamic_slice_in_dim(line, f * r, r)
-
-        g_heads = own(pair_order(small[:, base, 4:6].reshape(GROUP, 256)[:, : 2 * dh]).reshape(width))
-        lines = small[:, base + 1 :, : width // 128].sum(0).reshape(2, width)
-        g_in, g_mid = own(lines[0]), own(lines[1])
+    )
+    g_res, branch_all, dw_b, sum_d, sum_first, out_red, g_mid_gain = feed_call(cfg, mid_all, ct_all, b_all, d_all, resid, gains)
+    g_tokens, layer_out, out_a, out_b, out_d, out_o, small = backward_call(
+        cfg, branch_all, o_all, a_all, nrm_all, qkv_all, p_all, m_all, gated_all, dw_b.reshape(n, r, 2 * ff), sum_d, sum_first, out_red,
+        tok, resid, g_res, gains, ends, g_mid_gain, kern, mixing,
+    )
+
+    g_qkv, g_gate, g_up, g_down, g_out, taps, vectors = results_call(cfg, out_a, out_b, out_d, out_o, small)
+    with jax.named_scope("small_results"):
+        g_kernel = taps[:, :kk, : 2 * kq].transpose(0, 2, 1).reshape(heads, kq, kk)
+        g_mixing = taps[:, 0:4, 127].reshape(heads, 2)
+        own = lax.dynamic_slice(vectors, (0, f * r), (3, r))
+        g_in, g_mid, g_heads = own[0], own[1], own[2]
     return (layer_out[None], g_tokens[None], g_in, g_qkv, g_kernel, g_mixing, g_heads, g_out, g_mid, g_gate, g_up, g_down)
 
 

time: 596 us -> 358 us (0.60); the launches traced: 587 us -> 357 us
  Pallas kernels: 518 us -> 338 us
  local copies, waits for them, and re-layouts: 55 us -> 17.1 us
  other arithmetic: 11.6 us -> 0.71 us
    pallas_call x1, Pallas kernels: 226 us -> 111 us  [backward_call(): pl.pallas_call(functools.partial(backward_kernel, cfg), out_shape=(sds((l...]
    pallas_call x1, Pallas kernels: 195 us -> 146 us  [forward_call(): pl.pallas_call(functools.partial(forward_kernel, cfg), out_shape=(sds(row...]
    convert_element_type x8 -> x0, local copies, waits for them, and re-layouts: 25.5 us -> none  [the longest x6 19.6 us: whole(): return part.reshape(r, n * 2 * chunk).astype(F32)]
    pallas_call x1, Pallas kernels: 96.7 us -> 77.3 us  [feed_call(): pl.pallas_call(functools.partial(feed_kernel, cfg), out_shape=(sds((lengt...]
    reshape x13 -> x2, local copies, waits for them, and re-layouts: 8.29 us -> 0.17 us  [the longest x1 0.17 us: per_device_group(): kern = kernel.reshape(-1)]
    unnamed x45 -> x42, local copies, waits for them, and re-layouts: 11.4 us -> 15.8 us
where the time goes in v2:
time: 358 us; the launch traced here: 357 us
  Pallas kernels  338 us (94%)
  local copies, waits for them, and re-layouts  17.1 us (5%)
    pallas_call x1, Pallas kernels, forward_call(): pl.pallas_call(functools.partial(forward_kernel, cfg), out_shape=(sds(row...  146 us
    pallas_call x1, Pallas kernels, backward_call(): pl.pallas_call(functools.partial(backward_kernel, cfg), out_shape=(sds((l...  111 us
    pallas_call x1, Pallas kernels, feed_call(): pl.pallas_call(functools.partial(feed_kernel, cfg), out_shape=(sds((lengt...  77.3 us
    unnamed x42, local copies, waits for them, and re-layouts  15.8 us

profile of v2, /device:TPU:0, one launch (start us, length us, event | category | flops | bytes accessed | tf_op | source)
XLA Modules:
  0.0 357.3 jit_solution(9833775036875981670)
XLA Ops:
  0.6 0.9 copy.42
  1.6 0.2 reshape.33.refs_10_.refs_18_
  1.7 0.0 copy-start.11
  1.7 0.8 copy.43.refs_11_.refs_19_
  2.5 0.0 copy-start.12
  2.5 0.7 pad_maximum_fusion
  3.2 0.1 copy.41
  4.0 0.0 copy-start
  4.0 1.1 copy-done
  5.1 0.0 copy-start.6
  5.1 1.0 copy-done.6
  6.1 0.0 copy-start.15
  6.1 0.7 copy-done.15
  6.7 146.4 %attention_forward.1 = (bf16[8,256,1536]{2,1,0:T(8,128)(2,1)}, bf16[8,256,1536]{2,1,0:T(8,128)(2,1)}, bf16[16,96,640]{2,1,0:T(8,128)(2,1)}, bf16[16,96,1024]{2,1...) custom-call(bf16[256,1536]{1,0:T(8,128)(2,1)S(1)} %bitcast.17, ...), custom_call_target="tpu_custom_call" | custom-call | tf_op jit(solution)/shard_map/attention_forward/pallas_call | solution.py:1085
  153.1 0.0 copy-done.11
  153.2 0.0 copy-done.12
  153.2 0.0 copy-start.4
  153.2 0.0 copy-start.10
  153.2 0.0 copy-start.13
  153.2 77.3 %feed_forward.1 = (f32[256,1536]{1,0:T(8,128)}, bf16[8,256,1536]{2,1,0:T(8,128)(2,1)}, bf16[1536,1024]{1,0:T(8,128)(2,1)}, bf16[128,1536]{1,0:T(8,128)(2,1)S(1)}...) custom-call(bf16[8,256,1536]{2,1,0:T(8,128)(2,1)} %get-tuple-element.47.refs_0_, ...), custom_call_target="tpu_custom_call" | custom-call | tf_op jit(solution)/shard_map/feed_forward/pallas_call | solution.py:1276
  230.5 0.0 copy-done.4
  230.5 0.0 copy-done.10
  230.6 0.0 copy-done.13
  230.6 0.0 copy-start.5
  230.6 0.7 copy-done.5
  231.3 0.0 copy-start.9
  231.3 0.7 copy-done.9
  232.0 0.0 copy-start.14
  232.0 0.6 copy-done.14
  232.6 110.7 %attention_backward.1 = (f32[256,1536]{1,0:T(8,128)}, f32[256,1536]{1,0:T(8,128)}, bf16[8,96,640]{2,1,0:T(8,128)(2,1)}, bf16[8,96,1024]{2,1,0:T(8,128)(2,1)}, bf...) custom-call(bf16[8,256,1536]{2,1,0:T(8,128)(2,1)} %get-tuple-element.53.refs_0_, ...), custom_call_target="tpu_custom_call" | custom-call | tf_op jit(solution)/shard_map/attention_backward/pallas_call | solution.py:1629
  343.3 0.0 copy-start.1
  343.3 1.4 copy-done.1
  344.7 1.2 copy-done.2
  345.9 1.1 copy-done.3
  347.0 1.0 copy-done.7
  348.0 0.9 copy-done.8
  348.9 3.7 %results.1 = (f32[96,4608]{1,0:T(8,128)}, f32[96,4096]{1,0:T(8,128)}, f32[96,4096]{1,0:T(8,128)}, f32[256,1536]{1,0:T(8,128)}, f32[96,1536]{1,0:T(8,128)}, /*ind...) custom-call(bf16[8,96,640]{2,1,0:T(8,128)(2,1)S(1)} %copy-done.2, bf16[8,96,1024]{2,1,0:T(8,128)(2,1)S(1)} %copy-done.1, ...), custom_call_target="tpu_custom_call" | custom-call | bytes 10911744 | tf_op jit(solution)/shard_map/results/pallas_call | solution.py:1717
  352.6 0.1 copy.45
  352.7 0.7 copy.46
  353.5 0.2 slice_reduce_fusion
  353.6 0.1 squeeze.21
  353.7 0.6 copy.47
  354.4 0.1 constant_dynamic-slice_fusion
  354.4 0.5 slice_bitcast_fusion.1
  355.0 0.0 copy-done.17
  355.0 1.1 copy.51
  356.1 0.0 copy-done.16
  356.1 1.1 copy.52
  (9 shorter events, 0.0 us)
Async XLA Ops:
  1.7 151.4 %copy-start.11 = (f32[1056]{0:T(1024)}, f32[1056]{0:T(1024)S(1)}, u32[]{:S(2)}) copy-start(f32[1056]{0:T(1024)S(1)} %reshape.33.refs_10_.refs_18_) | copy-start | bytes 12676
  2.5 150.7 %copy-start.12 = (f32[16,2]{1,0:T(8,128)}, f32[16,2]{1,0:T(8,128)S(1)}, u32[]{:S(2)}) copy-start(f32[16,2]{1,0:T(8,128)S(1)} %copy.43.refs_11_.refs_19_) | copy-start | bytes 388
  4.0 1.1 copy-start
  5.1 1.0 copy-start.6
  6.1 0.7 copy-start.15
  153.2 77.4 %copy-start.4 = (bf16[2,96,1536]{2,1,0:T(8,128)(2,1)}, bf16[2,96,1536]{2,1,0:T(8,128)(2,1)S(1)}, u32[]{:S(2)}) copy-start(bf16[2,96,1536]{2,1,0:T(8,128)(2,1)S(1)} %get-tuple-element.54.refs_1_) | copy-start | bytes 1769476
  153.2 77.4 %copy-start.10 = (f32[8,1536]{1,0:T(8,128)}, f32[8,1536]{1,0:T(8,128)S(1)}, u32[]{:S(2)}) copy-start(f32[8,1536]{1,0:T(8,128)S(1)} %get-tuple-element.52.refs_5_.refs_15_) | copy-start | bytes 147460
  153.2 77.4 %copy-start.13 = (f32[8,8,256]{2,1,0:T(8,128)}, f32[8,8,256]{2,1,0:T(8,128)S(1)}, u32[]{:S(2)}) copy-start(f32[8,8,256]{2,1,0:T(8,128)S(1)} %get-tuple-element.66.refs_16_) | copy-start | bytes 196612
  230.6 0.7 copy-start.5
  231.3 0.7 copy-start.9
  232.0 0.6 copy-start.14
  343.3 1.4 copy-start.1
  344.7 1.2 copy-start.2
  345.9 1.1 copy-start.3
  347.0 1.0 copy-start.7
  348.0 0.9 copy-start.8
  348.9 6.0 %copy-start.17 = (f32[256,1536]{1,0:T(8,128)S(1)}, f32[256,1536]{1,0:T(8,128)}, u32[]{:S(2)}) copy-start(f32[256,1536]{1,0:T(8,128)} %get-tuple-element.68) | copy-start | bytes 4718596
  352.6 3.5 copy-start.16

commit v3 on v2

--- a/solution.py
+++ b/solution.py
@@ -14,7 +14,6 @@
 PLANE = 4
 GROUP = 8
 SIDE = 256
-LAG = 3
 SLOTS = 2
 QKV = 640
 
@@ -187,7 +186,7 @@
         }[name]
         return remote(src, dst, self.send.at[i], self.recv.at[i], dev)
 
-    def push(self, i):
+    def push(self, i, turn=True):
         @pl.when(i == 1)
         def _():
             self._copy("da").start()
@@ -200,7 +199,8 @@
         @pl.when(i == 5)
         def _():
             self._copy("yb").start()
-            self.turn()
+            if turn:
+                self.turn()
 
     def ahead(self):
         self._copy("yb").start()
@@ -298,10 +298,12 @@
         direct.sort(key=lambda t: -abs(t - b))
         return [(t, (b, t) in self.by, i) for i, t in enumerate(direct)]
 
-    def _each(self, b, act):
+    def _each(self, b, act, target=None):
         @pl.when(self.me.g == b)
         def _():
             for t, through, i in self._plan(b):
+                if target not in (None, t):
+                    continue
                 if through:
                     z = self.me.planes
                     by = self.by[(b, t)]
@@ -309,9 +311,9 @@
                 else:
                     act(self._copy(b, t, self.blocks(t), i))
 
-    def start(self):
+    def start(self, targets=None):
         for b in range(self.me.planes):
-            self._each(b, lambda cp: cp.start())
+            self._each(b, lambda cp: cp.start(), None if targets is None else targets[b])
 
     def _combined(self, b, t):
         return self._copy(b, t, self.via, self.me.planes - 2)
@@ -405,9 +407,13 @@
     return (i >= j) & (i.astype(F32) < ends)
 
 
+def mix_at(mix_ref, pair, o, g):
+    return mix_ref[pl.ds(2 * pair + o, 1), g : g + 1]
+
+
 def mix_lanes(mix_ref, pair, g, dh):
     at = lanes(1, SIDE)
-    m0, m1 = mix_ref[2 * pair, g], mix_ref[2 * pair + 1, g]
+    m0, m1 = mix_at(mix_ref, pair, 0, g), mix_at(mix_ref, pair, 1, g)
     return jnp.where(at < dh, m0, jnp.where(at < 2 * dh, m1, 0.0))
 
 
@@ -423,7 +429,7 @@
     diff = (c - r) if flip else (r - c)
     acc = jnp.zeros((length, length), F32)
     for b in range(taps_k):
-        acc = jnp.where(diff == b - taps_k // 2, kern_ref[(head * taps_q + a) * taps_k + b], acc)
+        acc = jnp.where(diff == b - taps_k // 2, kern_ref[head, a : a + 1, b : b + 1], acc)
     return acc
 
 
@@ -711,12 +717,12 @@
 
 
 def forward_kernel(cfg, *refs):
-    (tok, ct, w_qkv, w_gate, w_up, w_down, w_o, gain_cols, docs, pads, kern, mix,
+    (tok, ct, w_qkv, w_gate, w_up, w_down, w_o, kern_in, mix_in, gain_rows, docs, pads,
      tok_all, ct_all, a_all, b_all, d_all, o_all, nrm_all, qkv_all, p_all, m_all, gated_all, mid_all, resid, gains, ends,
-     wq_v, w_a, w_b, meta,
+     kern, mix, wq_v, w_a, w_b, meta, gain_v, ct_v, down_v, own_o,
      x_v, wa_v, wo_v, t_v, cat_v, shift_v, qkv_v, p_v, m_v, gated_v, meta_v, mid_v, tok_v,
      out_v, red, diag, near, rs_send, rs_recv,
-     g_send, g_recv, g_loc, a_send, a_recv, ch_send, ch_recv, o_send, o_recv, meta_send, meta_recv, meet_sems, loc, pack, row_in, row_out) = refs
+     g_send, g_recv, g_loc, a_send, a_recv, ch_send, ch_recv, o_send, o_recv, meta_send, meta_recv, gain_send, gain_recv, meet_sems, loc, pack, row_in, row_out) = refs
     planes, dh, taps_q, taps_k = cfg["planes"], cfg["dh"], cfg["kq"], cfg["kk"]
     length, width = tok.shape
     per_pair = o_all.shape[0]
@@ -728,8 +734,15 @@
     wq_in.start()
     tok_in = pltpu.make_async_copy(tok, tok_v, loc.at[0])
     tok_in.start()
-    down_in = pltpu.make_async_copy(w_down.at[pl.ds(me.y * chunk, chunk)], d_all.at[me.g], loc.at[3])
+    taps_in = [pltpu.make_async_copy(kern_in, kern, loc.at[6]), pltpu.make_async_copy(mix_in, mix, loc.at[7])]
+    for cp in taps_in:
+        cp.start()
+    o_in = pltpu.make_async_copy(w_o, own_o, loc.at[4])
+    o_in.start()
+    down_in = pltpu.make_async_copy(w_down.at[pl.ds(me.y * chunk, chunk)], down_v, loc.at[3])
     down_in.start()
+    ct_in = pltpu.make_async_copy(ct, ct_v, loc.at[5])
+    ct_in.start()
 
     def columns(j, s, z):
         at = pl.multiple_of(z * (2 * PLANE * chunk) + s * (2 * chunk) + me.y * chunk, 128)
@@ -769,12 +782,19 @@
             q0,
             jnp.where(low, q1, pltpu.roll(v1, 64, 1)),
             k0,
-            jnp.where(low, k1, pltpu.roll(gain_cols[...], 64, 1)),
+            jnp.where(low, k1, 0.0),
             v0,
         )
         for i, t in enumerate(tiles):
             w_a[s, :, i * 128 : (i + 1) * 128] = t.astype(BF16)
 
+    down_in.wait()
+    down_out = pltpu.make_async_copy(down_v, d_all.at[me.g], loc.at[3])
+    down_out.start()
+    o_in.wait()
+    tok_in.wait()
+    for cp in taps_in:
+        cp.wait()
     me.greet()
 
     def first(src, dst_all, base):
@@ -806,14 +826,21 @@
         meta_sent.append(cp)
     meta_here = pltpu.make_async_copy(meta, meta_v.at[me.slot], meta_send.at[0])
     meta_here.start()
+    gain_here = pltpu.make_async_copy(gain_rows, gain_v.at[me.f], gain_send.at[0])
+    gain_here.start()
+    gain_sent = []
+    for d in range(1, PLANE):
+        to = lax.rem(me.s + d, PLANE)
+        gain_sent.append(remote(gain_rows, gain_v.at[me.f], gain_send.at[d], gain_recv.at[d], (me.y, me.g * PLANE + to)))
+        gain_sent[-1].start()
     sent_a, own_a = first(w_a, a_all, 0)
-    tokens = Gather(me, tok, tok_all, g_send.at[0], g_recv.at[0], g_loc.at[0])
+    tokens = Gather(me, tok_v, tok_all, g_send.at[0], g_recv.at[0], g_loc.at[0])
     tokens.start()
 
     o_y = jnp.where((me.g == 1) | (me.g == 2), 1, 0)
     o_c = jnp.where(me.g >= 2, 1, 0)
-    o_here = pltpu.make_async_copy(w_o, o_all.at[me.c], o_send.at[0])
-    o_sib = remote(w_o, o_all.at[me.c], o_send.at[0], o_recv.at[0], me.sib)
+    o_here = pltpu.make_async_copy(own_o, o_all.at[me.c], o_send.at[0])
+    o_sib = remote(own_o, o_all.at[me.c], o_send.at[0], o_recv.at[0], me.sib)
 
     @pl.when((o_y == me.y) & (o_c == me.c))
     def _():
@@ -823,29 +850,28 @@
     def _():
         o_sib.start()
 
-    def o_next(way):
-        return remote(o_all, o_all, o_send.at[1 + way], o_recv.at[1], me.plane_dev(me.g + 1 - 2 * way))
+    def o_copy(t, i):
+        return remote(o_all, o_all, o_send.at[i], o_recv.at[1], me.plane_dev(t))
+
+    o_way = ((2, 1), (2, 0), (1, 3), (1, 2))
 
     def o_each(act):
-        @pl.when((me.g >= me.home) & (me.g + 1 < planes))
-        def _():
-            act(o_next(0))
-
-        @pl.when((me.g <= me.home) & (me.g >= 1))
-        def _():
-            act(o_next(1))
-
-    apart = jnp.where(me.g > me.home, me.g - me.home, me.home - me.g)
-    inner = (me.g == 1) | (me.g == 2)
+        for home, (first_to, then_to) in enumerate(o_way):
+
+            @pl.when((me.g == home) & (me.home == home))
+            def _():
+                act(o_copy(first_to, 1))
+                act(o_copy(then_to, 2))
+
+    o_relays = ((me.home < 2) & (me.g == 2)) | ((me.home >= 2) & (me.g == 1))
 
     def o_from_home():
         o_here.wait()
         remote(o_all.at[1 - me.c], o_all.at[1 - me.c], o_send.at[0], o_recv.at[0], me.sib).wait_recv()
-        o_each(lambda cp: cp.start())
-
-    def o_pass_on():
-        o_next(0).wait_recv()
-        o_each(lambda cp: cp.start())
+
+    def o_relay():
+        o_copy(0, 1).wait_recv()
+        o_copy(jnp.where(me.home < 2, planes - 1, 0), 1).start()
 
     blocks4 = lambda ref: (lambda b: ref.at[pl.ds(b * PLANE, PLANE)])
     spread_a = Spread(me, blocks4(a_all), ch_send.at[0], ch_recv.at[0])
@@ -863,11 +889,20 @@
     shift_v[0:8] = jnp.zeros((8, taps_q * length), F32)
     wo_v[...] = jnp.zeros(wo_v.shape, BF16)
 
-    pl.when((apart == 0) & jnp.logical_not(inner))(o_from_home)
+    pl.when(me.g == me.home)(o_from_home)
+    o_each(lambda cp: cp.start())
+    gain_here.wait()
+    for d in range(1, PLANE):
+        fr = me.g * PLANE + lax.rem(me.s - d + PLANE, PLANE)
+        remote(gain_rows, gain_v.at[fr], gain_send.at[d], gain_recv.at[d], me.sib).wait_recv()
+    for d in range(1, planes):
+        to = lax.rem(me.g + d, planes)
+        part = gain_v.at[pl.ds(me.g * PLANE, PLANE)]
+        gain_sent.append(remote(part, part, gain_send.at[PLANE + d], gain_recv.at[PLANE + d], me.plane_dev(to)))
+        gain_sent[-1].start()
     first_wait(w_a, a_all, 0, own_a)
     spread_a.near()
-    pl.when((apart == 0) & inner)(o_from_home)
-    pl.when((apart == 1) & inner & (me.y == 0))(o_pass_on)
+    pl.when(o_relays)(o_relay)
 
     tokens.relay()
     for j in range(2):
@@ -875,13 +910,14 @@
             for z in range(planes):
                 columns(j, s, z).wait()
     sent_b, own_b = first(w_b, b_all, PLANE)
-    cots = Gather(me, ct, ct_all, g_send.at[1], g_recv.at[1], g_loc.at[1])
+    cots = Gather(me, ct_v, ct_all, g_send.at[1], g_recv.at[1], g_loc.at[1])
+    ct_in.wait()
     cots.start()
     spread_a.settle()
     meet(me, meet_sems.at[0])
     spread_a.rest()
 
-    down_in.wait()
+    down_out.wait()
 
     tokens.share()
     tokens.last()
@@ -889,33 +925,28 @@
     for row in range(GROUP):
         pltpu.make_async_copy(tok_all.at[row], x_v.at[row], row_in.at[row]).start()
     first_wait(w_b, b_all, PLANE, own_b)
-
-    spread_a.arrive()
-    wa_in = pltpu.make_async_copy(a_all, wa_v, loc.at[1])
-    wa_in.start()
-    pl.when((apart > 0) & inner & ((apart == 2) | (me.y == 1)))(o_pass_on)
-    spread_d.near()
-    spread_b.near()
-    wa_in.wait()
     for d in range(1, GROUP):
         fr = lax.rem(me.slot - d + GROUP, GROUP)
         remote(meta, meta_v.at[fr], meta_send.at[d], meta_recv.at[d], me.sib).wait_recv()
     meta_here.wait()
     ends[...] = meta_v[...]
-
-    gain_rows = jnp.transpose(wa_v[:, :, 384:512].reshape(width, 128).astype(F32))
+    for d in range(1, planes):
+        part = gain_v.at[pl.ds(lax.rem(me.g - d + planes, planes) * PLANE, PLANE)]
+        remote(part, part, gain_send.at[PLANE + d], gain_recv.at[PLANE + d], me.sib).wait_recv()
     gains[...] = jnp.zeros(gains.shape, F32)
-    gains[0:1] = gain_rows[64:65]
-    gains[1:2] = gain_rows[65:66]
-    heads_at = wa_v[pl.ds(me.pair * per_pair, per_pair), :, 384:512].reshape(2 * dh, 128).astype(F32)
-    heads_at = jnp.concatenate([heads_at, jnp.zeros((SIDE - 2 * dh, 128), F32)], axis=0)
-    gains[2:3, 0:SIDE] = jnp.transpose(heads_at)[66:67]
-
-    h0, h1 = head_lanes(length, dh)
-    scatter = Scatter(me, out_v, red, diag, near, rs_send, rs_recv)
-
-    def attention(i):
-        row, k = order(me, i)
+    lane = lanes(8, 128)
+    for k in range(planes):
+        v0, v1, v2, v3 = (gain_v[k * PLANE + j] for j in range(PLANE))
+        v1, v2, v3 = pltpu.roll(v1, 96, 1), pltpu.roll(v2, 64, 1), pltpu.roll(v3, 32, 1)
+        for j, t in enumerate((jnp.where(lane < 96, v0, v1), jnp.where(lane < 64, v1, v2), jnp.where(lane < 32, v2, v3))):
+            at = k * PLANE * w_o.shape[0] + j * 128
+            gains[0:2, at : at + 128] = t[0:2]
+    v0, v1 = gain_v[2 * me.pair], pltpu.roll(gain_v[2 * me.pair + 1], 96, 1)
+    gains[2:3, 0:128] = jnp.where(lane < 96, v0, v1)[2:3]
+    gains[2:3, 128:256] = jnp.where(lane < 64, v1, 0.0)[2:3]
+
+    def norms(i, carry):
+        row, _ = order(me, i)
         pltpu.make_async_copy(tok_all.at[row], x_v.at[row], row_in.at[row]).wait()
 
         def norm(at):
@@ -925,6 +956,27 @@
 
         strips(length, norm)
         pltpu.make_async_copy(x_v.at[row], nrm_all.at[row], row_out.at[0, row]).start()
+        return carry
+
+    lax.fori_loop(0, GROUP, norms, 0)
+    spread_a.arrive()
+    wa_in = pltpu.make_async_copy(a_all, wa_v, loc.at[1])
+    wa_in.start()
+    @pl.when((me.g != me.home) & jnp.logical_not(o_relays))
+    def _():
+        o_copy(0, 1).wait_recv()
+
+    wo_in = pltpu.make_async_copy(o_all, wo_v.at[pl.ds(0, per_pair)], loc.at[2])
+    wo_in.start()
+    spread_d.near()
+    spread_b.near()
+    wa_in.wait()
+    wo_in.wait()
+    h0, h1 = head_lanes(length, dh)
+    scatter = Scatter(me, out_v, red, diag, near, rs_send, rs_recv)
+
+    def attention(i):
+        row, k = order(me, i)
         acc = nn(x_v[row], wa_v[...].reshape(width, QKV))
         at = lanes(length, 128)
         q = jnp.where(h0 | h1, acc[:, 0:SIDE], 0.0)
@@ -969,8 +1021,6 @@
         pltpu.make_async_copy(gated_v.at[row], gated_all.at[row], row_out.at[4, row]).start()
         wo = wo_v[...].reshape(wo_v.shape[0] * wo_v.shape[1], width)
 
-    wo_in = pltpu.make_async_copy(o_all, wo_v.at[pl.ds(0, per_pair)], loc.at[2])
-
     def project(i):
         row, k = order(me, i)
         wo = wo_v[...].reshape(wo_v.shape[0] * wo_v.shape[1], width)
@@ -989,29 +1039,11 @@
     def one(i, carry):
         attention(i)
 
-        @pl.when(i == LAG)
-        def _():
-            wo_in.wait()
-
-            def late(j, carry):
-                project(j)
-                return carry
-
-            lax.fori_loop(0, LAG, late, 0)
-
-        @pl.when(i >= LAG)
-        def _():
-            project(i)
+        project(i)
 
         @pl.when(i == 1)
         def _():
             cots.relay()
-
-            @pl.when((apart > 0) & jnp.logical_not(inner))
-            def _():
-                o_next(0).wait_recv()
-
-            wo_in.start()
 
         @pl.when(i == 4)
         def _():
@@ -1021,15 +1053,9 @@
             spread_d.rest()
             spread_b.rest()
 
-        @pl.when(i == 5)
-        def _():
-            cots.share()
-            cots.last()
-
         return carry
 
     lax.fori_loop(0, GROUP, one, 0)
-    tok_in.wait()
     scatter.arrive()
 
     def middle(at):
@@ -1042,6 +1068,8 @@
     mids = Gather(me, mid_v, mid_all, g_send.at[2], g_recv.at[2], g_loc.at[2])
     mids.start()
     mids.relay()
+    cots.share()
+    cots.last()
     mids.share()
     mids.last()
     mids.finish()
@@ -1054,11 +1082,15 @@
         sp.finish()
     o_each(lambda cp: cp.wait_send())
 
+    @pl.when(o_relays)
+    def _():
+        o_copy(0, 1).wait_send()
+
     @pl.when((o_y == me.y) & (o_c != me.c))
     def _():
         o_sib.wait_send()
 
-    for cp in meta_sent + sent_a + sent_b:
+    for cp in meta_sent + gain_sent + sent_a + sent_b:
         cp.wait_send()
     for r in range(GROUP):
         pltpu.make_async_copy(x_v.at[r], nrm_all.at[r], row_out.at[0, r]).wait()
@@ -1068,7 +1100,7 @@
         pltpu.make_async_copy(gated_v.at[r], gated_all.at[r], row_out.at[4, r]).wait()
 
 
-def forward_call(cfg, tok, ct, w_qkv, w_gate, w_up, w_down, w_o, gain_cols, docs, pads, kern, mix):
+def forward_call(cfg, tok, ct, w_qkv, w_gate, w_up, w_down, w_o, kern, mix, gain_rows, docs, pads):
     length, width = tok.shape
     planes, ff, r = cfg["planes"], cfg["ff"], w_qkv.shape[0]
     n = planes * PLANE
@@ -1091,22 +1123,22 @@
             sds((GROUP, 2, 2, length, length), BF16), sds((GROUP, 2, length, length), BF16), sds(rows + (SIDE,), BF16),
             sds(rows + (width,), BF16), sds((length, width), F32), sds((8, width), F32), sds((GROUP, 8, length), F32),
         ),
-        in_specs=[hbm] * 7 + [vmem] + [smem] * 4,
+        in_specs=[hbm] * 9 + [vmem] + [smem] * 2,
         out_specs=(hbm,) * 12 + (vmem,) * 3,
         scratch_shapes=[
-            v16(*w_qkv.shape), v16(PLANE, r, QKV), v16(PLANE, r, 2 * ff), v32(8, length),
+            v32(*kern.shape), v32(*mix.shape), v16(*w_qkv.shape), v16(PLANE, r, QKV), v16(PLANE, r, 2 * ff), v32(8, length), v32(n, 8, 128), v16(length, width), v16(chunk, width), v16(*w_o.shape),
             v16(*rows, width), v16(n, r, QKV), v16(pad_rows, *w_o.shape),
             v16(2, 3 * length, taps), v16(length, 3 * length), v32(length + 8, taps),
             v16(*rows, 3 * SIDE), v16(GROUP, 2, 2, length, length), v16(GROUP, 2, length, length), v16(*rows, SIDE),
             v32(GROUP, 8, length), v16(length, width), v16(length, width),
             *Scatter.scratch(length, width),
             dma((3, Gather.SENDS)), dma((3, Gather.RECVS)), dma((3,)), dma((2 * PLANE,)), dma((2 * PLANE,)),
-            dma((3, planes)), dma((3, planes)), dma((3,)), dma((2,)), dma((GROUP,)), dma((GROUP,)), pltpu.SemaphoreType.REGULAR((2,)),
-            dma((4,)), dma((2, PLANE, planes)), dma((GROUP,)), dma((5, GROUP)),
+            dma((3, planes)), dma((3, planes)), dma((3,)), dma((2,)), dma((GROUP,)), dma((GROUP,)), dma((PLANE + planes,)), dma((PLANE + planes,)), pltpu.SemaphoreType.REGULAR((2,)),
+            dma((8,)), dma((2, PLANE, planes)), dma((GROUP,)), dma((5, GROUP)),
         ],
-        compiler_params=pltpu.CompilerParams(collective_id=1, has_side_effects=True, vmem_limit_bytes=52 * 2**20),
+        compiler_params=pltpu.CompilerParams(collective_id=1, has_side_effects=True, vmem_limit_bytes=60 * 2**20),
         name="attention_forward",
-    )(tok, ct, w_qkv, w_gate, w_up, w_down, w_o, gain_cols, docs, pads, kern, mix)
+    )(tok, ct, w_qkv, w_gate, w_up, w_down, w_o, kern, mix, gain_rows, docs, pads)
 
 
 def feed_kernel(cfg, *refs):
@@ -1130,7 +1162,7 @@
             pltpu.make_async_copy(ct_all.at[row], ct_v.at[row], row_in.at[1, row]),
         )
 
-    for i in range(GROUP):
+    for i in range(2):
         for cp in row_copies(order(me, i)[0]):
             cp.start()
     me.greet()
@@ -1142,6 +1174,9 @@
     sum_mid = Scatter(me, m_out, m_red, m_diag, m_near, m_send, m_recv)
     wb_in.wait()
     wd_in.wait()
+    for i in range(2, GROUP):
+        for cp in row_copies(order(me, i)[0]):
+            cp.start()
 
     def one(i, carry):
         row, k = order(me, i)
@@ -1161,22 +1196,33 @@
         gu_v[row, :, :ff] = g_gate
         gu_v[row, :, ff:] = g_up
         mid_part = nt(gu_v[row], wb)
-        out_part = nn(hidden, wd)
 
         @pl.when(lax.rem(i, 2) == 0)
         def _():
             sum_mid.put_sib(k, mid_part)
-            sum_out.put_sib(k, out_part)
 
         @pl.when(lax.rem(i, 2) == 1)
         def _():
             sum_mid.put_self(k, mid_part)
-            sum_out.put_self(k, out_part)
 
         sum_mid.push(i)
         return carry
 
     lax.fori_loop(0, GROUP, one, 0)
+
+    def output(i, carry):
+        row, k = order(me, i)
+        out_part = nn(hid_v[row], wd_v[...].reshape(ff, width))
+
+        @pl.when(lax.rem(i, 2) == 0)
+        def _():
+            sum_out.put_sib(k, out_part)
+
+        @pl.when(lax.rem(i, 2) == 1)
+        def _():
+            sum_out.put_self(k, out_part)
+
+        return carry
 
     tokens = GROUP * length
     tile = SIDE
@@ -1191,6 +1237,33 @@
     lax.fori_loop(0, ff // tile, down, 0)
     down_sum.start()
 
+    steps = width // tile
+
+    def tile_out(i):
+        slot = lax.rem(i, 2)
+        at = pl.ds(pl.multiple_of(i * tile, tile), tile)
+        return pltpu.make_async_copy(tile_v.at[slot], dw_b.at[at], out_sem.at[slot])
+
+    def gate_up(i, carry):
+        @pl.when(i >= 2)
+        def _():
+            tile_out(i - 2).wait()
+
+        at = pl.ds(pl.multiple_of(i * tile, tile), tile)
+        value = tn(mid_v[:, :, at].reshape(tokens, tile), gu_v[...].reshape(tokens, 2 * ff)).astype(BF16)
+        tile_v[lax.rem(i, 2)] = value
+        tile_out(i).start()
+        for z in range(first_v.shape[0]):
+            lo = z * PLANE * first_v.shape[1]
+
+            @pl.when(i == lo // tile)
+            def _():
+                first_v[z] = value[lo % tile : lo % tile + first_v.shape[1]]
+
+        return carry
+
+    lax.fori_loop(0, steps, gate_up, 0)
+    first_sum.start()
     g_mid_gain[...] = jnp.zeros(g_mid_gain.shape, F32)
     sum_mid.arrive()
 
@@ -1208,36 +1281,10 @@
     strips(length, middle)
     branch = Gather(me, ct_v.at[me.slot], branch_all, g_send, g_recv, g_loc.at[0])
     branch.start()
+
+    lax.fori_loop(0, GROUP, output, 0)
     red_out = pltpu.make_async_copy(o_red, out_red, out_sem.at[2])
     red_out.start()
-
-    steps = width // tile
-
-    def tile_out(i):
-        slot = lax.rem(i, 2)
-        at = pl.ds(pl.multiple_of(i * tile, tile), tile)
-        return pltpu.make_async_copy(tile_v.at[slot], dw_b.at[at], out_sem.at[slot])
-
-    def gate_up(i, carry):
-        @pl.when(i >= 2)
-        def _():
-            tile_out(i - 2).wait()
-
-        at = pl.ds(pl.multiple_of(i * tile, tile), tile)
-        value = tn(mid_v[:, :, at].reshape(tokens, tile), gu_v[...].reshape(tokens, 2 * ff)).astype(BF16)
-        tile_v[lax.rem(i, 2)] = value
-        tile_out(i).start()
-        for z in range(first_v.shape[0]):
-            lo = z * PLANE * first_v.shape[1]
-
-            @pl.when(i == lo // tile)
-            def _():
-                first_v[z] = value[lo % tile : lo % tile + first_v.shape[1]]
-
-        return carry
-
-    lax.fori_loop(0, steps, gate_up, 0)
-    first_sum.start()
     down_sum.combine(lambda t: dd_v.at[pl.ds(t, 1)])
     branch.relay()
     branch.share()
@@ -1296,10 +1343,10 @@
 
 def backward_kernel(cfg, *refs):
     (branch_all, o_all, a_all, nrm_all, qkv_all, p_all, m_all, gated_all, dw_b, sum_d, sum_first, out_red, tok,
-     resid, g_res, gains, ends, g_mid_gain, kern, mix,
+     resid, kern_in, mix_in, g_res, gains, ends, g_mid_gain,
      g_tokens, layer_out, out_a, out_b, out_d, out_o, out_small,
-     gb_v, wo_v, wa_v, nrm_v, qkv_v, p_v, m_v, t_v, cat_v, shift_v, corr_v, gq_v, da_v, do_v, tok_v, rows_v, line_v, taps_v,
-     zb_v, za_v, zo_v, via_b, via_a, via_o, sb_v, sa_v, so_v, far_b, strip_v, small_v, small_in,
+     kern, mix, gb_v, wo_v, wa_v, nrm_v, qkv_v, p_v, m_v, t_v, cat_v, shift_v, corr_v, gq_v, da_v, do_v, tok_v, rows_v, line_v, taps_v,
+     zb_v, za_v, zo_v, via_b, via_a, via_o, sb_v, sa_v, so_v, far_b, strip_v, sd_v, small_v, small_in,
      s_out, s_red, s_diag, s_near, rs_send, rs_recv,
      l_red, l_diag, l_near, l_send, l_recv,
      z_send, z_recv, small_send, small_recv, t_send, t_recv, loc, row_in) = refs
@@ -1315,15 +1362,20 @@
         for i, (src, dst) in enumerate(
             [(a_all, wa_v), (o_all, wo_v.at[pl.ds(0, per_pair)]), (tok, tok_v)]
             + [(dw_b.at[pl.ds(me.g * PLANE + 1, PLANE - 1)], sb_v.at[pl.ds(1, PLANE - 1)]), (sum_first, sb_v.at[0])]
-            + [(dw_b.at[pl.ds(far * PLANE + 1, PLANE - 1)], far_b), (out_red, l_red)]
+            + [(dw_b.at[pl.ds(far * PLANE + 1, PLANE - 1)], far_b), (out_red, l_red), (sum_d, sd_v)]
         )
     ]
 
     span = PLANE * r
 
-    def nrm_copy(j):
-        at = pl.ds(j * span, span)
-        return pltpu.make_async_copy(nrm_all.at[:, :, at], nrm_v.at[j % 2], loc.at[7 + j % 2])
+    turns = ((3, 2, 1, 0), (0, 2, 3, 1), (3, 1, 0, 2), (0, 1, 2, 3))
+
+    def turn_of(i):
+        return sum(jnp.where(me.g == b, turns[b][i], 0) for b in range(planes))
+
+    def nrm_copy(i):
+        at = pl.ds(pl.multiple_of(turn_of(i) * span, 128), span)
+        return pltpu.make_async_copy(nrm_all.at[:, :, at], nrm_v.at[i % 2], loc.at[8 + i % 2])
 
     def row_copies(i):
         row = order(me, i)[0]
@@ -1333,6 +1385,9 @@
             cps.append(pltpu.make_async_copy(src.at[row], dst.at[at], row_in.at[j + 1, i]))
         return cps
 
+    taps_in = [pltpu.make_async_copy(kern_in, kern, loc.at[10]), pltpu.make_async_copy(mix_in, mix, loc.at[11])]
+    for cp in taps_in:
+        cp.start()
     wo_v[...] = jnp.zeros(wo_v.shape, BF16)
     loads[1].start()
     loads[0].start()
@@ -1343,6 +1398,15 @@
         cp.start()
     for j in range(2):
         nrm_copy(j).start()
+    for cp in taps_in:
+        cp.wait()
+    for g in range(2):
+        for a in range(taps_q):
+            t_v[g, a * length : (a + 1) * length] = band(kern, 2 * me.pair + g, a, taps_q, taps_k, length, True).astype(BF16)
+    shift_v[length:] = jnp.zeros((8, length), F32)
+    corr_v[...] = jnp.zeros(corr_v.shape, F32)
+    rows_v[...] = jnp.zeros(rows_v.shape, F32)
+    small_v[...] = jnp.zeros(small_v.shape, F32)
     me.greet()
 
     blocks4 = lambda ref: (lambda b: ref.at[pl.ds(b * PLANE, PLANE)])
@@ -1356,24 +1420,21 @@
     sum_b.start()
     for group in (sum_b, sum_a, sum_o):
         group.clear()
-    d_cp = remote(sum_d, out_d.at[me.y], t_send.at[3, 0], t_recv.at[3, 0], me.yn)
-    d_cp.start()
-    d_here = pltpu.make_async_copy(sum_d, out_d.at[me.y], t_send.at[3, 1])
-    d_here.start()
-
-    for g in range(2):
-        for a in range(taps_q):
-            t_v[g, a * length : (a + 1) * length] = band(kern, 2 * me.pair + g, a, taps_q, taps_k, length, True).astype(BF16)
-    shift_v[length:] = jnp.zeros((8, length), F32)
-    corr_v[...] = jnp.zeros(corr_v.shape, F32)
-    rows_v[...] = jnp.zeros(rows_v.shape, F32)
-    small_v[...] = jnp.zeros(small_v.shape, F32)
     h0, h1 = head_lanes(length, dh)
     scatter = Scatter(me, s_out, s_red, s_diag, s_near, rs_send, rs_recv)
     layer = Scatter(me, None, l_red, l_diag, l_near, l_send, l_recv)
     loads[0].wait()
     loads[1].wait()
     loads[5].wait()
+    loads[6].wait()
+    layer.push(1)
+    layer.push(3)
+    layer.ahead()
+    loads[7].wait()
+    d_cp = remote(sd_v, out_d.at[me.y], t_send.at[3, 0], t_recv.at[3, 0], me.yn)
+    d_cp.start()
+    d_here = pltpu.make_async_copy(sd_v, out_d.at[me.y], t_send.at[3, 1])
+    d_here.start()
 
     def one(i, carry):
         row, k = order(me, i)
@@ -1400,7 +1461,7 @@
         g_k = jnp.zeros((length, SIDE), F32)
         g_v = jnp.zeros((length, SIDE), F32)
         for o in range(2):
-            mixed = mix[2 * me.pair + o, 0] * probs[0] + mix[2 * me.pair + o, 1] * probs[1]
+            mixed = mix_at(mix, me.pair, o, 0) * probs[0] + mix_at(mix, me.pair, o, 1) * probs[1]
             g_v = g_v + tn(mixed.astype(BF16), jnp.where(h0 if o == 0 else h1, g_att, 0.0).astype(BF16))
         for g in range(2):
             mine = h0 if g == 0 else h1
@@ -1419,23 +1480,16 @@
         mid_tile = g_q[:, 128:256] + pltpu.roll(g_v[:, 128:256], 64, 1)
         packed = jnp.concatenate([g_q[:, 0:128], mid_tile, g_k, g_v[:, 0:128]], axis=1).astype(BF16)
         gq_v[row] = packed
-        part = nt(packed, wa_v[...].reshape(width, QKV))
-
-        @pl.when(lax.rem(i, 2) == 0)
-        def _():
-            scatter.put_sib(k, part)
-
-        @pl.when(lax.rem(i, 2) == 1)
-        def _():
-            scatter.put_self(k, part)
-
-        scatter.push(i)
 
         @pl.when(i + SLOTS < GROUP)
         def _():
             for cp in row_copies(i + SLOTS):
                 cp.start()
 
+        @pl.when(i == 4)
+        def _():
+            layer.turn()
+
         @pl.when(i == 5)
         def _():
             sum_b.combine(lambda t: far_b)
@@ -1443,11 +1497,8 @@
         return carry
 
     lax.fori_loop(0, GROUP, one, 0)
-    for i in (2, 3, 4, 6):
+    for i in (2, 3, 4):
         loads[i].wait()
-    for i in (1, 3):
-        layer.push(i)
-    layer.ahead()
     gated_in = [
         pltpu.make_async_copy(gated_all.at[i], p_v.at[i // 4, i // 2 % 2, i % 2], row_in.at[0, i]) for i in range(GROUP)
     ]
@@ -1455,19 +1506,64 @@
         cp.start()
 
     tokens = GROUP * length
-    for j in range(planes):
-        nrm_copy(j).wait()
-        value = tn(nrm_v[j % 2].reshape(tokens, span), gq_v[...].reshape(tokens, QKV))
-        da_v[j * PLANE : (j + 1) * PLANE] = value.astype(BF16).reshape(PLANE, r, QKV)
-        if j + 2 < planes:
-            nrm_copy(j + 2).start()
-    sum_a.start()
     for cp in gated_in:
         cp.wait()
     value = tn(p_v[...].reshape(tokens, SIDE), gb_v[...].reshape(tokens, width))
     do_v[...] = value[0 : 2 * dh].astype(BF16).reshape(do_v.shape)
 
     sum_o.start()
+    for i in range(planes):
+        nrm_copy(i).wait()
+        value = tn(nrm_v[i % 2].reshape(tokens, span), gq_v[...].reshape(tokens, QKV))
+        da_v[pl.ds(turn_of(i) * PLANE, PLANE)] = value.astype(BF16).reshape(PLANE, r, QKV)
+        sum_a.start([turns[b][i] for b in range(planes)])
+        if i + 2 < planes:
+            nrm_copy(i + 2).start()
+    def to_slot(d):
+        to = lax.rem(me.slot + d, GROUP)
+        return lax.div(to, PLANE), lax.rem(to, PLANE)
+
+    def group_copies(kind, src_of, landing):
+        cps = []
+        for d in range(1, GROUP):
+            y, sl = to_slot(d)
+            cps.append(remote(src_of(sl), landing.at[me.slot], t_send.at[kind, d], t_recv.at[kind, d], (y, me.g * PLANE + sl)))
+        cps.append(pltpu.make_async_copy(src_of(me.s), landing.at[me.slot], t_send.at[kind, 0]))
+        for cp in cps:
+            cp.start()
+        return cps
+
+    def group_wait(kind, cps, landing):
+        for d in range(1, GROUP):
+            fr = lax.rem(me.slot - d + GROUP, GROUP)
+            remote(landing.at[fr], landing.at[fr], t_send.at[kind, d], t_recv.at[kind, d], me.sib).wait_recv()
+        for cp in cps[:-1]:
+            cp.wait_send()
+        cps[-1].wait()
+
+    def back_through(i, carry):
+        row, k = order(me, i)
+        part = nt(gq_v[row], wa_v[...].reshape(width, QKV))
+
+        @pl.when(lax.rem(i, 2) == 0)
+        def _():
+            scatter.put_sib(k, part)
+
+        @pl.when(lax.rem(i, 2) == 1)
+        def _():
+            scatter.put_self(k, part)
+
+        scatter.push(i, turn=False)
+        return carry
+
+    lax.fori_loop(0, GROUP, back_through, 0)
+    scatter.turn()
+    sum_b.total(sb_v.at[pl.ds(1, PLANE - 1)], sb_v.at[pl.ds(1, PLANE - 1)])
+    b_cps = group_copies(0, lambda sl: sb_v.at[sl], out_b)
+
+    sum_o.combine(lambda t: do_v.at[pl.ds(t, 1)])
+    sum_a.combine(lambda t: da_v.at[pl.ds(t * PLANE, PLANE)])
+
     def taps(at, carry):
         g, a = lax.div(at, taps_q), lax.rem(at, taps_q)
         lanes_at = pl.ds(pl.multiple_of(a * length, length), length)
@@ -1491,6 +1587,19 @@
     for j in range(2):
         small_v[base, 4 + j : 5 + j] = rows_v[0:1, j * 128 : (j + 1) * 128]
 
+    layer.arrive()
+
+    def result(at):
+        cp = pltpu.make_async_copy(resid.at[at], strip_v, loc.at[0])
+        cp.start()
+        cp.wait()
+        strip_v[...] = strip_v[...] + layer.total(at)
+        cp = pltpu.make_async_copy(strip_v, layer_out.at[at], loc.at[0])
+        cp.start()
+        cp.wait()
+
+    strips(length, result)
+
     scatter.arrive()
 
     def middle(at):
@@ -1511,38 +1620,6 @@
     for cp in send_s:
         cp.start()
 
-    def to_slot(d):
-        to = lax.rem(me.slot + d, GROUP)
-        return lax.div(to, PLANE), lax.rem(to, PLANE)
-
-    def group_copies(kind, src_of, landing):
-        cps = []
-        for d in range(1, GROUP):
-            y, sl = to_slot(d)
-            cps.append(remote(src_of(sl), landing.at[me.slot], t_send.at[kind, d], t_recv.at[kind, d], (y, me.g * PLANE + sl)))
-        cps.append(pltpu.make_async_copy(src_of(me.s), landing.at[me.slot], t_send.at[kind, 0]))
-        for cp in cps:
-            cp.start()
-        return cps
-
-    def group_wait(kind, cps, landing):
-        for d in range(1, GROUP):
-            fr = lax.rem(me.slot - d + GROUP, GROUP)
-            remote(landing.at[fr], landing.at[fr], t_send.at[kind, d], t_recv.at[kind, d], me.sib).wait_recv()
-        for cp in cps[:-1]:
-            cp.wait_send()
-        cps[-1].wait()
-
-    layer.turn()
-    sum_b.total(sb_v.at[pl.ds(1, PLANE - 1)], sb_v.at[pl.ds(1, PLANE - 1)])
-    b_cps = group_copies(0, lambda sl: sb_v.at[sl], out_b)
-
-    sum_a.combine(lambda t: da_v.at[pl.ds(t * PLANE, PLANE)])
-
-    sum_o.combine(lambda t: do_v.at[pl.ds(t, 1)])
-    sum_a.total(sa_v, da_v.at[pl.ds(me.g * PLANE, PLANE)])
-    a_cps = group_copies(1, lambda sl: sa_v.at[sl], out_a)
-
     sum_o.total(so_v, do_v.at[pl.ds(me.g, 1)])
     o_to = me.pair * per_pair + lax.div(me.g, 2)
     o_half = lax.rem(me.g, 2)
@@ -1565,25 +1642,15 @@
                 act_here(o_here)
 
     o_each(lambda cp: cp.start(), lambda cp: cp.start())
+    sum_a.total(sa_v, da_v.at[pl.ds(me.g * PLANE, PLANE)])
+    a_cps = group_copies(1, lambda sl: sa_v.at[sl], out_a)
+
     for cp in send_s:
         cp.wait_recv()
     for cp in send_s:
         cp.wait_send()
     small_v[...] = small_v[...] + sum(small_in[d] for d in range(planes - 1))
     small_cps = group_copies(2, lambda sl: small_v, out_small)
-
-    layer.arrive()
-
-    def result(at):
-        cp = pltpu.make_async_copy(resid.at[at], strip_v, loc.at[0])
-        cp.start()
-        cp.wait()
-        strip_v[...] = strip_v[...] + layer.total(at)
-        cp = pltpu.make_async_copy(strip_v, layer_out.at[at], loc.at[0])
-        cp.start()
-        cp.wait()
-
-    strips(length, result)
 
     group_wait(2, small_cps, out_small)
     d_cp.wait_send()
@@ -1632,26 +1699,27 @@
             sds((length, width), F32), sds((length, width), F32), sds((GROUP, r, QKV), BF16), sds((GROUP, r, 2 * ff), BF16),
             sds((2, chunk, width), BF16), sds((2, piece, width), BF16), sds((GROUP,) + small, F32),
         ),
-        in_specs=[hbm] * 14 + [vmem] * 4 + [smem] * 2,
+        in_specs=[hbm] * 16 + [vmem] * 4,
         out_specs=(vmem,) + (hbm,) * 6,
         scratch_shapes=[
-            v16(*rows, width), v16(pad_rows, *o_all.shape[1:]), v16(n, r, QKV), v16(2, *rows, PLANE * r), v16(SLOTS, length, 3 * SIDE),
+            v32(*args[14].shape), v32(*args[15].shape), v16(*rows, width), v16(pad_rows, *o_all.shape[1:]), v16(n, r, QKV), v16(2, *rows, PLANE * r), v16(SLOTS, length, 3 * SIDE),
             v16(SLOTS, 2, 2, length, length), v16(SLOTS, 2, length, length),
             v16(2, taps, length), v16(length, taps), v32(length + 8, length), v32(2, length, taps), v16(*rows, QKV),
             v16(n, r, QKV), v16(planes, piece, width), v16(length, width), v32(8, SIDE), v32(8, width), v32(16, 128),
             v16(others, *b_block), v16(others, *a_block), v16(others, *o_block), v16(*b_block), v16(*a_block), v16(*o_block),
-            v16(PLANE, r, 2 * ff), v16(*a_block), v16(*o_block), v16(*b_block), v32(64, width),
+            v16(PLANE, r, 2 * ff), v16(*a_block), v16(*o_block), v16(*b_block), v32(64, width), v16(chunk, width),
             v32(*small), v32(others, *small),
             *Scatter.scratch(length, width), *Scatter.scratch(length, width, cores=False),
             dma((3, planes)), dma((3, planes)), dma((others,)), dma((others,)), dma((5, GROUP)), dma((5, GROUP)),
-            dma((9,)), dma((4, GROUP)),
+            dma((12,)), dma((4, GROUP)),
         ],
         compiler_params=pltpu.CompilerParams(collective_id=3, has_side_effects=True, vmem_limit_bytes=54 * 2**20),
         name="attention_backward",
     )(*args)
 
 
-def results_kernel(cfg, a_ref, b_ref, d_ref, o_ref, small_ref, qkv_ref, gate_ref, up_ref, down_ref, out_ref, taps_ref, vec_ref):
+def results_kernel(cfg, a_ref, b_ref, d_ref, o_ref, small_ref, g_tok, layer, qkv_ref, gate_ref, up_ref, down_ref, out_ref,
+                   taps_ref, mix_ref, in_ref, mid_ref, heads_ref, tok_ref, layer_ref, vec_v):
     planes, ff = cfg["planes"], cfg["ff"]
     rows, width = out_ref.shape
     chunk = ff // planes
@@ -1687,26 +1755,38 @@
     down_ref[...] = d_ref[0].astype(F32)
     out_ref[...] = o_ref[0].astype(F32)
 
+    tok_ref[...] = g_tok[...]
+    layer_ref[...] = layer[...]
+
     @pl.when(pl.program_id(0) == 0)
     def _():
         base = 1
         for pair in range(GROUP):
+            taps = jnp.transpose(jnp.concatenate([small_ref[slot(pair), 0], jnp.zeros((112, 128), F32)], axis=0))
+            for g in range(2):
+                taps_ref[2 * pair + g] = taps[g * cfg["kq"] : (g + 1) * cfg["kq"], 0 : cfg["kk"]]
             mixed = jnp.sum(small_ref[slot(pair), base], axis=-1, keepdims=True)
-            taps_ref[pair] = jnp.where(lanes(16, 128) == 127, mixed, small_ref[slot(pair), 0])
-        vec_ref[...] = jnp.zeros(vec_ref.shape, F32)
+            for o in range(2):
+                for g in range(2):
+                    mix_ref[2 * pair + o : 2 * pair + o + 1, g : g + 1] = mixed[2 * o + g : 2 * o + g + 1]
+        vec_v[...] = jnp.zeros(vec_v.shape, F32)
         for k in range(2):
             total = small_ref[0, base + 1 + k]
             for s in range(1, GROUP):
                 total = total + small_ref[s, base + 1 + k]
             for j in range(width // 128):
-                vec_ref[k : k + 1, j * 128 : (j + 1) * 128] = total[j : j + 1]
+                vec_v[k : k + 1, j * 128 : (j + 1) * 128] = total[j : j + 1]
         line = lambda pair: tuple(small_ref[slot(pair), base, 4 + j : 5 + j] for j in range(2))
         for two in range(GROUP // 2):
             for i, t in enumerate(joined(line(2 * two), line(2 * two + 1), lanes(1, 128) < 64)):
-                vec_ref[2:3, two * 384 + i * 128 : two * 384 + (i + 1) * 128] = t
-
-
-def results_call(cfg, out_a, out_b, out_d, out_o, small):
+                vec_v[2:3, two * 384 + i * 128 : two * 384 + (i + 1) * 128] = t
+        own = in_ref.shape[1]
+        mine = pltpu.roll(vec_v[...], lax.rem(width - lax.axis_index("fsdp") * own, width), 1)
+        for k, ref in enumerate((in_ref, mid_ref, heads_ref)):
+            ref[...] = mine[k : k + 1, 0:own]
+
+
+def results_call(cfg, out_a, out_b, out_d, out_o, small, g_tokens, layer_out):
     r = out_a.shape[1]
     _, chunk, width = out_d.shape
     half = r // 2
@@ -1719,7 +1799,8 @@
         grid=(2,),
         out_shape=(
             sds((r, 3 * width), F32), sds((r, n_cols(cfg)), F32), sds((r, n_cols(cfg)), F32), sds((2 * chunk, width), F32),
-            sds((r, width), F32), sds((GROUP, 16, 128), F32), sds((8, width), F32),
+            sds((r, width), F32), sds((2 * GROUP, cfg["kq"], cfg["kk"]), F32), sds((2 * GROUP, 2), F32),
+            sds((1, r), F32), sds((1, r), F32), sds((1, r), F32), sds(g_tokens.shape, F32), sds(g_tokens.shape, F32),
         ),
         in_specs=[
             pl.BlockSpec((GROUP, half, out_a.shape[2]), lambda i: (0, i, 0)),
@@ -1727,15 +1808,19 @@
             pl.BlockSpec((1, chunk, width), lambda i: (i, 0, 0)),
             pl.BlockSpec((1, half, width), lambda i: (i, 0, 0)),
             whole(small.shape),
+            rows(g_tokens.shape[0] // 2, width),
+            rows(g_tokens.shape[0] // 2, width),
         ],
+        scratch_shapes=[pltpu.VMEM((8, width), F32)],
         out_specs=(
             rows(half, 3 * width), rows(half, n_cols(cfg)), rows(half, n_cols(cfg)), rows(chunk, width), rows(half, width),
-            whole((GROUP, 16, 128)), whole((8, width)),
+            whole((2 * GROUP, cfg["kq"], cfg["kk"])), whole((2 * GROUP, 2)),
+            whole((1, r)), whole((1, r)), whole((1, r)), rows(g_tokens.shape[0] // 2, width), rows(g_tokens.shape[0] // 2, width),
         ),
-        compiler_params=pltpu.CompilerParams(vmem_limit_bytes=40 * 2**20),
+        compiler_params=pltpu.CompilerParams(vmem_limit_bytes=60 * 2**20),
         cost_estimate=pl.CostEstimate(flops=0, bytes_accessed=moved, transcendentals=0),
         name="results",
-    )(out_a, out_b, out_d, out_o, small)
+    )(out_a, out_b, out_d, out_o, small, g_tokens, layer_out)
 
 
 def n_cols(cfg):
@@ -1781,31 +1866,38 @@
     chunk = w_down.shape[0] // 2
     ff = planes * chunk
     cfg = dict(planes=planes, dh=dh, kq=kq, kk=kk, ff=ff)
-    f = lax.axis_index("fsdp")
-
-    gain_cols = jnp.stack([norm_in, norm_mid, norm_heads], axis=1).astype(F32)
-    gain_cols = jnp.pad(gain_cols, ((0, 0), (0, 125)))
+
+    gain_rows = jnp.pad(jnp.stack([norm_in, norm_mid, norm_heads]).astype(F32), ((0, 5), (0, 128 - r)))
     tok, ct = tokens[0], cotangent[0]
-    kern = kernel.reshape(-1)
 
     (_, ct_all, a_all, b_all, d_all, o_all, nrm_all, qkv_all, p_all, m_all, gated_all, mid_all, resid, gains, ends) = (
         forward_call(
-            cfg, tok, ct, w_qkv, w_gate, w_up, w_down, w_out, gain_cols, doc_lengths, pad_counts, kern, mixing
+            cfg, tok, ct, w_qkv, w_gate, w_up, w_down, w_out, kernel, mixing, gain_rows, doc_lengths, pad_counts
         )
     )
     g_res, branch_all, dw_b, sum_d, sum_first, out_red, g_mid_gain = feed_call(cfg, mid_all, ct_all, b_all, d_all, resid, gains)
     g_tokens, layer_out, out_a, out_b, out_d, out_o, small = backward_call(
         cfg, branch_all, o_all, a_all, nrm_all, qkv_all, p_all, m_all, gated_all, dw_b.reshape(n, r, 2 * ff), sum_d, sum_first, out_red,
-        tok, resid, g_res, gains, ends, g_mid_gain, kern, mixing,
-    )
-
-    g_qkv, g_gate, g_up, g_down, g_out, taps, vectors = results_call(cfg, out_a, out_b, out_d, out_o, small)
-    with jax.named_scope("small_results"):
-        g_kernel = taps[:, :kk, : 2 * kq].transpose(0, 2, 1).reshape(heads, kq, kk)
-        g_mixing = taps[:, 0:4, 127].reshape(heads, 2)
-        own = lax.dynamic_slice(vectors, (0, f * r), (3, r))
-        g_in, g_mid, g_heads = own[0], own[1], own[2]
-    return (layer_out[None], g_tokens[None], g_in, g_qkv, g_kernel, g_mixing, g_heads, g_out, g_mid, g_gate, g_up, g_down)
+        tok, resid, kernel, mixing, g_res, gains, ends, g_mid_gain,
+    )
+
+    g_qkv, g_gate, g_up, g_down, g_out, g_kernel, g_mixing, g_in, g_mid, g_heads, g_tokens, layer_out = results_call(
+        cfg, out_a, out_b, out_d, out_o, small, g_tokens, layer_out
+    )
+    return (
+        layer_out[None],
+        g_tokens[None],
+        g_in[0],
+        g_qkv,
+        g_kernel,
+        g_mixing,
+        g_heads[0],
+        g_out,
+        g_mid[0],
+        g_gate,
+        g_up,
+        g_down,
+    )
 
 
 def solution(mesh):

time: 358 us -> 345 us (0.964)
  local copies, waits for them, and re-layouts: 17.1 us -> 8.62 us
  Pallas kernels: 338 us -> 333 us
    unnamed x42 -> x12, local copies, waits for them, and re-layouts: 15.8 us -> 8.62 us
    pallas_call x1, Pallas kernels: 77.3 us -> 72 us  [feed_call(): pl.pallas_call(functools.partial(feed_kernel, cfg), out_shape=(sds((lengt...]
where the time goes in v3:
time: 345 us; the launch traced here: 344 us
  Pallas kernels  333 us (97%)
  local copies, waits for them, and re-layouts  8.62 us (2%)
    pallas_call x1, Pallas kernels, forward_call(): pl.pallas_call(functools.partial(forward_kernel, cfg), out_shape=(sds(row...  143 us
    pallas_call x1, Pallas kernels, backward_call(): pl.pallas_call(functools.partial(backward_kernel, cfg), out_shape=(sds((l...  111 us
    pallas_call x1, Pallas kernels, feed_call(): pl.pallas_call(functools.partial(feed_kernel, cfg), out_shape=(sds((lengt...  72 us
    unnamed x12, local copies, waits for them, and re-layouts  8.62 us

profile of v3, /device:TPU:0, one launch (start us, length us, event | category | flops | bytes accessed | tf_op | source)
XLA Modules:
  0.0 344.0 jit_solution(9716592228117391942)
XLA Ops:
  1.3 1.3 fusion.9.refs_9_
  2.6 1.4 copy.27.refs_8_.refs_15_
  3.9 1.5 copy.26.refs_7_.refs_14_
  5.5 143.4 %attention_forward.1 = (bf16[8,256,1536]{2,1,0:T(8,128)(2,1)}, bf16[8,256,1536]{2,1,0:T(8,128)(2,1)}, bf16[16,96,640]{2,1,0:T(8,128)(2,1)}, bf16[16,96,1024]{2,1...) custom-call(bf16[256,1536]{1,0:T(8,128)(2,1)} %bitcast.12, ...), custom_call_target="tpu_custom_call" | custom-call | tf_op jit(solution)/shard_map/attention_forward/pallas_call | solution.py:1117
  148.9 0.0 copy-start.2
  148.9 0.8 copy-done.2
  149.7 72.0 %feed_forward.1 = (f32[256,1536]{1,0:T(8,128)}, bf16[8,256,1536]{2,1,0:T(8,128)(2,1)}, bf16[1536,1024]{1,0:T(8,128)(2,1)}, bf16[128,1536]{1,0:T(8,128)(2,1)S(1)}...) custom-call(bf16[8,256,1536]{2,1,0:T(8,128)(2,1)} %get-tuple-element.52.refs_0_, ...), custom_call_target="tpu_custom_call" | custom-call | tf_op jit(solution)/shard_map/feed_forward/pallas_call | solution.py:1323
  221.8 0.0 copy-start
  221.8 0.7 copy-done
  222.5 0.0 copy-start.1
  222.5 0.7 copy-done.1
  223.2 0.0 copy-start.3
  223.2 0.6 copy-done.3
  223.8 110.5 %attention_backward.1 = (f32[256,1536]{1,0:T(8,128)}, f32[256,1536]{1,0:T(8,128)}, bf16[8,96,640]{2,1,0:T(8,128)(2,1)}, bf16[8,96,1024]{2,1,0:T(8,128)(2,1)}, bf...) custom-call(bf16[8,256,1536]{2,1,0:T(8,128)(2,1)} %get-tuple-element.58.refs_0_, ...), custom_call_target="tpu_custom_call" | custom-call | tf_op jit(solution)/shard_map/attention_backward/pallas_call | solution.py:1696
  334.4 6.7 %results.1 = (f32[96,4608]{1,0:T(8,128)}, f32[96,4096]{1,0:T(8,128)}, f32[96,4096]{1,0:T(8,128)}, f32[256,1536]{1,0:T(8,128)}, f32[96,1536]{1,0:T(8,128)}, /*ind...) custom-call(bf16[8,96,640]{2,1,0:T(8,128)(2,1)} %get-tuple-element.7, ...), custom_call_target="tpu_custom_call" | custom-call | bytes 10911744 | tf_op jit(solution)/shard_map/results/pallas_call | solution.py:1797
  341.0 1.3 copy.31
  342.4 1.6 copy.30
Async XLA Ops:
  148.9 0.8 copy-start.2
  221.8 0.7 copy-start
  222.5 0.7 copy-start.1
  223.2 0.6 copy-start.3

commit v4 on v3

--- a/solution.py
+++ b/solution.py
@@ -14,6 +14,7 @@
 PLANE = 4
 GROUP = 8
 SIDE = 256
+FIRST = 1
 SLOTS = 2
 QKV = 640
 
@@ -298,11 +299,11 @@
         direct.sort(key=lambda t: -abs(t - b))
         return [(t, (b, t) in self.by, i) for i, t in enumerate(direct)]
 
-    def _each(self, b, act, target=None):
+    def _each(self, b, act, ways=(True, False)):
         @pl.when(self.me.g == b)
         def _():
             for t, through, i in self._plan(b):
-                if target not in (None, t):
+                if through not in ways:
                     continue
                 if through:
                     z = self.me.planes
@@ -311,9 +312,9 @@
                 else:
                     act(self._copy(b, t, self.blocks(t), i))
 
-    def start(self, targets=None):
+    def start(self, ways=(True, False)):
         for b in range(self.me.planes):
-            self._each(b, lambda cp: cp.start(), None if targets is None else targets[b])
+            self._each(b, lambda cp: cp.start(), ways)
 
     def _combined(self, b, t):
         return self._copy(b, t, self.via, self.me.planes - 2)
@@ -407,14 +408,18 @@
     return (i >= j) & (i.astype(F32) < ends)
 
 
-def mix_at(mix_ref, pair, o, g):
-    return mix_ref[pl.ds(2 * pair + o, 1), g : g + 1]
-
-
-def mix_lanes(mix_ref, pair, g, dh):
+def of_head(value, head):
+    at = lax.broadcasted_iota(jnp.int32, value.shape, value.ndim - 1)
+    return jnp.sum(jnp.where(at == head, value, 0.0), axis=-1, keepdims=True)
+
+
+def pair_mixing(mix_ref, pair):
+    return [[of_head(mix_ref[g : g + 1], 2 * pair + o) for g in range(2)] for o in range(2)]
+
+
+def mix_lanes(mixing, g, dh):
     at = lanes(1, SIDE)
-    m0, m1 = mix_at(mix_ref, pair, 0, g), mix_at(mix_ref, pair, 1, g)
-    return jnp.where(at < dh, m0, jnp.where(at < 2 * dh, m1, 0.0))
+    return jnp.where(at < dh, mixing[0][g], jnp.where(at < 2 * dh, mixing[1][g], 0.0))
 
 
 def head_stats(value, dh, h0, h1):
@@ -423,14 +428,17 @@
     return jnp.where(h0, m0, jnp.where(h1, m1, 0.0))
 
 
-def band(kern_ref, head, a, taps_q, taps_k, length, flip):
+def bands(kern_ref, head, length, flip):
+    taps_k, taps_q, _ = kern_ref.shape
     r = lax.broadcasted_iota(jnp.int32, (length, length), 0)
     c = lax.broadcasted_iota(jnp.int32, (length, length), 1)
     diff = (c - r) if flip else (r - c)
-    acc = jnp.zeros((length, length), F32)
-    for b in range(taps_k):
-        acc = jnp.where(diff == b - taps_k // 2, kern_ref[head, a : a + 1, b : b + 1], acc)
-    return acc
+    taps = [of_head(kern_ref[b], head) for b in range(taps_k)]
+    for a in range(taps_q):
+        acc = jnp.zeros((length, length), F32)
+        for b in range(taps_k):
+            acc = jnp.where(diff == b - taps_k // 2, taps[b][a : a + 1], acc)
+        yield a, acc
 
 
 def rms_norm(values_in, scaling):
@@ -879,8 +887,7 @@
     spread_d = Spread(me, lambda b: d_all.at[b], ch_send.at[2], ch_recv.at[2])
 
     for g in range(2):
-        for a in range(taps_q):
-            t = band(kern, 2 * me.pair + g, a, taps_q, taps_k, length, False)
+        for a, t in bands(kern, 2 * me.pair + g, length, False):
             high = t.astype(BF16)
             at = slice(a * length, (a + 1) * length)
             t_v[g, 0:length, at] = high
@@ -974,6 +981,8 @@
     wo_in.wait()
     h0, h1 = head_lanes(length, dh)
     scatter = Scatter(me, out_v, red, diag, near, rs_send, rs_recv)
+
+    mixing = pair_mixing(mix, me.pair)
 
     def attention(i):
         row, k = order(me, i)
@@ -1010,7 +1019,7 @@
             low = (probs - high.astype(F32)).astype(BF16)
             p_v[row, g, 0] = high
             p_v[row, g, 1] = low
-            attended = attended + (nn(high, v) + nn(low, v)) * mix_lanes(mix, me.pair, g, dh)
+            attended = attended + (nn(high, v) + nn(low, v)) * mix_lanes(mixing, g, dh)
         pltpu.make_async_copy(m_v.at[row], m_all.at[row], row_out.at[2, row]).start()
         pltpu.make_async_copy(p_v.at[row], p_all.at[row], row_out.at[3, row]).start()
         centred = attended - head_stats(attended, dh, h0, h1)
@@ -1169,7 +1178,7 @@
     sum_out = Scatter(me, o_out, o_red, None, None, o_send, o_recv)
     down_sum = Collect(me, lambda b: dd_v.at[pl.ds(b, 1)], zd_v, via_v, z_send.at[0], z_recv.at[0])
     down_sum.clear()
-    first_sum = Collect(me, lambda b: first_v.at[pl.ds(b, 1)], zf_v, via_f, z_send.at[1], z_recv.at[1])
+    first_sum = Collect(me, lambda b: first_v.at[b], zf_v, via_f, z_send.at[1], z_recv.at[1])
     first_sum.clear()
     sum_mid = Scatter(me, m_out, m_red, m_diag, m_near, m_send, m_recv)
     wb_in.wait()
@@ -1189,12 +1198,9 @@
         g_hidden = nt(ct_v[row], wd)
         sig = jax.nn.sigmoid(gate)
         silu = gate * sig
-        hidden = (silu * up).astype(BF16)
-        hid_v[row] = hidden
-        g_gate = (g_hidden * up * sig * (1.0 + gate * (1.0 - sig))).astype(BF16)
-        g_up = (g_hidden * silu).astype(BF16)
-        gu_v[row, :, :ff] = g_gate
-        gu_v[row, :, ff:] = g_up
+        hid_v[row] = (silu * up).astype(BF16)
+        gu_v[row, :, :ff] = (g_hidden * up * sig * (1.0 + gate * (1.0 - sig))).astype(BF16)
+        gu_v[row, :, ff:] = (g_hidden * silu).astype(BF16)
         mid_part = nt(gu_v[row], wb)
 
         @pl.when(lax.rem(i, 2) == 0)
@@ -1207,8 +1213,6 @@
 
         sum_mid.push(i)
         return carry
-
-    lax.fori_loop(0, GROUP, one, 0)
 
     def output(i, carry):
         row, k = order(me, i)
@@ -1223,6 +1227,8 @@
             sum_out.put_self(k, out_part)
 
         return carry
+
+    lax.fori_loop(0, GROUP, one, 0)
 
     tokens = GROUP * length
     tile = SIDE
@@ -1253,12 +1259,16 @@
         value = tn(mid_v[:, :, at].reshape(tokens, tile), gu_v[...].reshape(tokens, 2 * ff)).astype(BF16)
         tile_v[lax.rem(i, 2)] = value
         tile_out(i).start()
+        r = first_v.shape[2]
         for z in range(first_v.shape[0]):
-            lo = z * PLANE * first_v.shape[1]
-
-            @pl.when(i == lo // tile)
-            def _():
-                first_v[z] = value[lo % tile : lo % tile + first_v.shape[1]]
+            for q in range(FIRST):
+                lo = (z * PLANE + q) * r
+                for tile_at in range(lo // tile, (lo + r - 1) // tile + 1):
+                    begin, end = max(lo, tile_at * tile), min(lo + r, (tile_at + 1) * tile)
+
+                    @pl.when(i == tile_at)
+                    def _():
+                        first_v[z, q, begin - lo : end - lo] = value[begin - tile_at * tile : end - tile_at * tile]
 
         return carry
 
@@ -1287,14 +1297,14 @@
     red_out.start()
     down_sum.combine(lambda t: dd_v.at[pl.ds(t, 1)])
     branch.relay()
+    first_sum.combine(lambda t: first_v.at[t])
     branch.share()
-    first_sum.combine(lambda t: first_v.at[pl.ds(t, 1)])
     branch.last()
     down_sum.total(sd_v, dd_v.at[pl.ds(me.g, 1)])
     sd_out = pltpu.make_async_copy(sd_v.at[0], sum_d, out_sem.at[3])
     sd_out.start()
-    first_sum.total(sf_v, first_v.at[pl.ds(me.g, 1)])
-    sf_out = pltpu.make_async_copy(sf_v.at[0], sum_first, out_sem.at[4])
+    first_sum.total(sf_v, first_v.at[me.g])
+    sf_out = pltpu.make_async_copy(sf_v, sum_first, out_sem.at[4])
     sf_out.start()
     branch.finish()
     sum_mid.finish_cores()
@@ -1324,14 +1334,14 @@
         functools.partial(feed_kernel, cfg),
         out_shape=(
             sds((length, width), F32), sds(rows + (width,), BF16),
-            sds((width, 2 * ff), BF16), sds((chunk, width), BF16), sds((r, 2 * ff), BF16), sds((4, length, width), BF16), sds((8, width), F32),
+            sds((width, 2 * ff), BF16), sds((chunk, width), BF16), sds((FIRST, r, 2 * ff), BF16), sds((4, length, width), BF16), sds((8, width), F32),
         ),
         in_specs=[hbm] * 4 + [vmem] * 2,
         out_specs=(vmem, hbm, hbm, hbm, hbm, hbm, vmem),
         scratch_shapes=[
             v16(*rows, width), v16(*rows, width), v16(*w_b.shape), v16(*w_d.shape), v16(*rows, ff), v16(*rows, 2 * ff),
             v16(2, SIDE, 2 * ff), v16(others + 1, chunk, width), v16(others, 1, chunk, width), v16(1, chunk, width), v16(1, chunk, width),
-            v16(others + 1, r, 2 * ff), v16(others, 1, r, 2 * ff), v16(1, r, 2 * ff), v16(1, r, 2 * ff),
+            v16(others + 1, FIRST, r, 2 * ff), v16(others, FIRST, r, 2 * ff), v16(FIRST, r, 2 * ff), v16(FIRST, r, 2 * ff),
             *Scatter.scratch(length, width, chips=False), *Scatter.scratch(length, width),
             dma((Gather.SENDS,)), dma((Gather.RECVS,)), dma((1,)), dma((2, others + 1)), dma((2, others + 1)),
             dma((2,)), dma((2, GROUP)), dma((5,)),
@@ -1344,12 +1354,12 @@
 def backward_kernel(cfg, *refs):
     (branch_all, o_all, a_all, nrm_all, qkv_all, p_all, m_all, gated_all, dw_b, sum_d, sum_first, out_red, tok,
      resid, kern_in, mix_in, g_res, gains, ends, g_mid_gain,
-     g_tokens, layer_out, out_a, out_b, out_d, out_o, out_small,
-     kern, mix, gb_v, wo_v, wa_v, nrm_v, qkv_v, p_v, m_v, t_v, cat_v, shift_v, corr_v, gq_v, da_v, do_v, tok_v, rows_v, line_v, taps_v,
-     zb_v, za_v, zo_v, via_b, via_a, via_o, sb_v, sa_v, so_v, far_b, strip_v, sd_v, small_v, small_in,
+     g_tokens, layer_out, out_a, out_c, out_b, out_d, out_o, out_small, out_line,
+     kern, mix, gb_v, wo_v, wa_v, nrm_v, qkv_v, p_v, m_v, t_v, cat_v, shift_v, corr_v, gq_v, da_v, dc_v, do_v, tok_v, rows_v, line_v, taps_v,
+     zb_v, za_v, zc_v, zo_v, via_b, via_a, via_c, via_o, sb_v, sa_v, sc_v, so_v, far_b, strip_v, sd_v, small_v, small_in, last_v, last_in,
      s_out, s_red, s_diag, s_near, rs_send, rs_recv,
      l_red, l_diag, l_near, l_send, l_recv,
-     z_send, z_recv, small_send, small_recv, t_send, t_recv, loc, row_in) = refs
+     z_send, z_recv, small_send, small_recv, line_send, line_recv, t_send, t_recv, loc, row_in) = refs
     planes, dh, taps_q, taps_k = cfg["planes"], cfg["dh"], cfg["kq"], cfg["kk"]
     length, width = tok.shape
     scale = dh ** (-0.5)
@@ -1361,8 +1371,8 @@
         pltpu.make_async_copy(src, dst, loc.at[i])
         for i, (src, dst) in enumerate(
             [(a_all, wa_v), (o_all, wo_v.at[pl.ds(0, per_pair)]), (tok, tok_v)]
-            + [(dw_b.at[pl.ds(me.g * PLANE + 1, PLANE - 1)], sb_v.at[pl.ds(1, PLANE - 1)]), (sum_first, sb_v.at[0])]
-            + [(dw_b.at[pl.ds(far * PLANE + 1, PLANE - 1)], far_b), (out_red, l_red), (sum_d, sd_v)]
+            + [(dw_b.at[pl.ds(me.g * PLANE + FIRST, PLANE - FIRST)], sb_v.at[pl.ds(FIRST, PLANE - FIRST)]), (sum_first, sb_v.at[pl.ds(0, FIRST)])]
+            + [(dw_b.at[pl.ds(far * PLANE + FIRST, PLANE - FIRST)], far_b), (out_red, l_red), (sum_d, sd_v)]
         )
     ]
 
@@ -1373,9 +1383,9 @@
     def turn_of(i):
         return sum(jnp.where(me.g == b, turns[b][i], 0) for b in range(planes))
 
-    def nrm_copy(i):
-        at = pl.ds(pl.multiple_of(turn_of(i) * span, 128), span)
-        return pltpu.make_async_copy(nrm_all.at[:, :, at], nrm_v.at[i % 2], loc.at[8 + i % 2])
+    def nrm_copy(m):
+        at = pl.ds(pl.multiple_of(turn_of(m % planes) * span, 128), span)
+        return pltpu.make_async_copy(nrm_all.at[:, :, at], nrm_v.at[m % 2], loc.at[8 + m % 2])
 
     def row_copies(i):
         row = order(me, i)[0]
@@ -1401,8 +1411,8 @@
     for cp in taps_in:
         cp.wait()
     for g in range(2):
-        for a in range(taps_q):
-            t_v[g, a * length : (a + 1) * length] = band(kern, 2 * me.pair + g, a, taps_q, taps_k, length, True).astype(BF16)
+        for a, t in bands(kern, 2 * me.pair + g, length, True):
+            t_v[g, a * length : (a + 1) * length] = t.astype(BF16)
     shift_v[length:] = jnp.zeros((8, length), F32)
     corr_v[...] = jnp.zeros(corr_v.shape, F32)
     rows_v[...] = jnp.zeros(rows_v.shape, F32)
@@ -1410,19 +1420,51 @@
     me.greet()
 
     blocks4 = lambda ref: (lambda b: ref.at[pl.ds(b * PLANE, PLANE)])
-    sum_b = Collect(me, lambda b: dw_b.at[pl.ds(b * PLANE + 1, PLANE - 1)], zb_v, via_b, z_send.at[0], z_recv.at[0])
+    sum_b = Collect(me, lambda b: dw_b.at[pl.ds(b * PLANE + FIRST, PLANE - FIRST)], zb_v, via_b, z_send.at[0], z_recv.at[0])
     sum_a = Collect(me, blocks4(da_v), za_v, via_a, z_send.at[1], z_recv.at[1])
+    sum_c = Collect(me, blocks4(dc_v), zc_v, via_c, z_send.at[3], z_recv.at[3])
     sum_o = Collect(me, lambda b: do_v.at[pl.ds(b, 1)], zo_v, via_o, z_send.at[2], z_recv.at[2])
     send_s = []
     for d in range(1, planes):
         to = lax.rem(me.g + d, planes)
         send_s.append(remote(small_v, small_in.at[d - 1], small_send.at[d - 1], small_recv.at[d - 1], me.plane_dev(to)))
+    send_l = []
+    for d in range(1, planes):
+        to = lax.rem(me.g + d, planes)
+        send_l.append(remote(last_v, last_in.at[d - 1], line_send.at[d - 1], line_recv.at[d - 1], me.plane_dev(to)))
     sum_b.start()
-    for group in (sum_b, sum_a, sum_o):
+    for group in (sum_b, sum_a, sum_c, sum_o):
         group.clear()
     h0, h1 = head_lanes(length, dh)
     scatter = Scatter(me, s_out, s_red, s_diag, s_near, rs_send, rs_recv)
     layer = Scatter(me, None, l_red, l_diag, l_near, l_send, l_recv)
+    def to_slot(d):
+        to = lax.rem(me.slot + d, GROUP)
+        return lax.div(to, PLANE), lax.rem(to, PLANE)
+
+    def group_copies(kind, src_of, landing, places=None):
+        def one_of(d):
+            y, sl = to_slot(d)
+            return remote(src_of(sl), landing.at[me.slot], t_send.at[kind, d], t_recv.at[kind, d], (y, me.g * PLANE + sl))
+
+        own = pltpu.make_async_copy(src_of(me.s), landing.at[me.slot], t_send.at[kind, 0])
+        cps = [one_of(d) for d in range(1, GROUP)] + [own]
+        for d, cp in enumerate(cps, 1):
+            if places is None:
+                cp.start()
+            else:
+                sl = to_slot(d % GROUP)[1]
+                pl.when((sl >= places[0]) & (sl < places[1]))(cp.start)
+        return cps
+
+    def group_wait(kind, cps, landing):
+        for d in range(1, GROUP):
+            fr = lax.rem(me.slot - d + GROUP, GROUP)
+            remote(landing.at[fr], landing.at[fr], t_send.at[kind, d], t_recv.at[kind, d], me.sib).wait_recv()
+        for cp in cps[:-1]:
+            cp.wait_send()
+        cps[-1].wait()
+
     loads[0].wait()
     loads[1].wait()
     loads[5].wait()
@@ -1430,11 +1472,15 @@
     layer.push(1)
     layer.push(3)
     layer.ahead()
+    loads[4].wait()
+    group_copies(0, lambda sl: sb_v.at[sl], out_b, (0, FIRST))
     loads[7].wait()
     d_cp = remote(sd_v, out_d.at[me.y], t_send.at[3, 0], t_recv.at[3, 0], me.yn)
     d_cp.start()
     d_here = pltpu.make_async_copy(sd_v, out_d.at[me.y], t_send.at[3, 1])
     d_here.start()
+
+    mixing = pair_mixing(mix, me.pair)
 
     def one(i, carry):
         row, k = order(me, i)
@@ -1445,7 +1491,7 @@
         q, kk, v = qkv_v[at, :, 0:SIDE], qkv_v[at, :, SIDE : 2 * SIDE], qkv_v[at, :, 2 * SIDE : 3 * SIDE]
         parts = [nn(p_v[at, g, 0], v) + nn(p_v[at, g, 1], v) for g in range(2)]
         probs = [p_v[at, g, 0].astype(F32) + p_v[at, g, 1].astype(F32) for g in range(2)]
-        lane_mix = [mix_lanes(mix, me.pair, g, dh) for g in range(2)]
+        lane_mix = [mix_lanes(mixing, g, dh) for g in range(2)]
         attended = parts[0] * lane_mix[0] + parts[1] * lane_mix[1]
         centred = jnp.where(h0 | h1, attended - head_stats(attended, dh, h0, h1), 0.0)
         inv = lax.rsqrt(head_stats(centred * centred, dh, h0, h1) + 1e-5)
@@ -1461,7 +1507,7 @@
         g_k = jnp.zeros((length, SIDE), F32)
         g_v = jnp.zeros((length, SIDE), F32)
         for o in range(2):
-            mixed = mix_at(mix, me.pair, o, 0) * probs[0] + mix_at(mix, me.pair, o, 1) * probs[1]
+            mixed = mixing[o][0] * probs[0] + mixing[o][1] * probs[1]
             g_v = g_v + tn(mixed.astype(BF16), jnp.where(h0 if o == 0 else h1, g_att, 0.0).astype(BF16))
         for g in range(2):
             mine = h0 if g == 0 else h1
@@ -1480,6 +1526,17 @@
         mid_tile = g_q[:, 128:256] + pltpu.roll(g_v[:, 128:256], 64, 1)
         packed = jnp.concatenate([g_q[:, 0:128], mid_tile, g_k, g_v[:, 0:128]], axis=1).astype(BF16)
         gq_v[row] = packed
+        part = nt(packed, wa_v[...].reshape(width, QKV))
+
+        @pl.when(lax.rem(i, 2) == 0)
+        def _():
+            scatter.put_sib(k, part)
+
+        @pl.when(lax.rem(i, 2) == 1)
+        def _():
+            scatter.put_self(k, part)
+
+        scatter.push(i, turn=False)
 
         @pl.when(i + SLOTS < GROUP)
         def _():
@@ -1497,72 +1554,13 @@
         return carry
 
     lax.fori_loop(0, GROUP, one, 0)
-    for i in (2, 3, 4):
+    for i in (2, 3):
         loads[i].wait()
     gated_in = [
         pltpu.make_async_copy(gated_all.at[i], p_v.at[i // 4, i // 2 % 2, i % 2], row_in.at[0, i]) for i in range(GROUP)
     ]
     for cp in gated_in:
         cp.start()
-
-    tokens = GROUP * length
-    for cp in gated_in:
-        cp.wait()
-    value = tn(p_v[...].reshape(tokens, SIDE), gb_v[...].reshape(tokens, width))
-    do_v[...] = value[0 : 2 * dh].astype(BF16).reshape(do_v.shape)
-
-    sum_o.start()
-    for i in range(planes):
-        nrm_copy(i).wait()
-        value = tn(nrm_v[i % 2].reshape(tokens, span), gq_v[...].reshape(tokens, QKV))
-        da_v[pl.ds(turn_of(i) * PLANE, PLANE)] = value.astype(BF16).reshape(PLANE, r, QKV)
-        sum_a.start([turns[b][i] for b in range(planes)])
-        if i + 2 < planes:
-            nrm_copy(i + 2).start()
-    def to_slot(d):
-        to = lax.rem(me.slot + d, GROUP)
-        return lax.div(to, PLANE), lax.rem(to, PLANE)
-
-    def group_copies(kind, src_of, landing):
-        cps = []
-        for d in range(1, GROUP):
-            y, sl = to_slot(d)
-            cps.append(remote(src_of(sl), landing.at[me.slot], t_send.at[kind, d], t_recv.at[kind, d], (y, me.g * PLANE + sl)))
-        cps.append(pltpu.make_async_copy(src_of(me.s), landing.at[me.slot], t_send.at[kind, 0]))
-        for cp in cps:
-            cp.start()
-        return cps
-
-    def group_wait(kind, cps, landing):
-        for d in range(1, GROUP):
-            fr = lax.rem(me.slot - d + GROUP, GROUP)
-            remote(landing.at[fr], landing.at[fr], t_send.at[kind, d], t_recv.at[kind, d], me.sib).wait_recv()
-        for cp in cps[:-1]:
-            cp.wait_send()
-        cps[-1].wait()
-
-    def back_through(i, carry):
-        row, k = order(me, i)
-        part = nt(gq_v[row], wa_v[...].reshape(width, QKV))
-
-        @pl.when(lax.rem(i, 2) == 0)
-        def _():
-            scatter.put_sib(k, part)
-
-        @pl.when(lax.rem(i, 2) == 1)
-        def _():
-            scatter.put_self(k, part)
-
-        scatter.push(i, turn=False)
-        return carry
-
-    lax.fori_loop(0, GROUP, back_through, 0)
-    scatter.turn()
-    sum_b.total(sb_v.at[pl.ds(1, PLANE - 1)], sb_v.at[pl.ds(1, PLANE - 1)])
-    b_cps = group_copies(0, lambda sl: sb_v.at[sl], out_b)
-
-    sum_o.combine(lambda t: do_v.at[pl.ds(t, 1)])
-    sum_a.combine(lambda t: da_v.at[pl.ds(t * PLANE, PLANE)])
 
     def taps(at, carry):
         g, a = lax.div(at, taps_q), lax.rem(at, taps_q)
@@ -1573,7 +1571,7 @@
             line = jnp.sum(jnp.where(diff == b - taps_k // 2, e, 0.0), axis=0, keepdims=True)
             taps_v[b : b + 1] = line[:, 0:128] + line[:, 128:256]
         each = jnp.sum(taps_v[...], axis=-1, keepdims=True)
-        small_v[0] = jnp.where(lanes(16, 128) == at, each, small_v[0])
+        small_v[0] = jnp.where(lanes(16, 128) == a * 2 * GROUP + 2 * me.pair + g, each, small_v[0])
         return carry
 
     taps_v[...] = jnp.zeros(taps_v.shape, F32)
@@ -1587,6 +1585,46 @@
     for j in range(2):
         small_v[base, 4 + j : 5 + j] = rows_v[0:1, j * 128 : (j + 1) * 128]
 
+    for j in range(width // 128):
+        small_v[2, j : j + 1] = g_mid_gain[0:1, j * 128 : (j + 1) * 128]
+    for cp in send_s:
+        cp.start()
+
+    tokens = GROUP * length
+    for cp in gated_in:
+        cp.wait()
+    value = tn(p_v[...].reshape(tokens, SIDE), gb_v[...].reshape(tokens, width))
+    do_v[...] = value[0 : 2 * dh].astype(BF16).reshape(do_v.shape)
+
+    sum_o.start()
+    for m in range(2 * planes):
+        i, first_part = m % planes, m < planes
+        nrm_copy(m).wait()
+        at = slice(0, SIDE) if first_part else slice(SIDE, QKV)
+        value = tn(nrm_v[m % 2].reshape(tokens, span), gq_v[:, :, at].reshape(tokens, at.stop - at.start))
+        terms = da_v if first_part else dc_v
+        terms[pl.ds(turn_of(i) * PLANE, PLANE)] = value.astype(BF16).reshape((PLANE,) + terms.shape[1:])
+        if m + 2 < 2 * planes:
+            nrm_copy(m + 2).start()
+    for way in (True, False):
+        sum_a.start((way,))
+        sum_c.start((way,))
+    scatter.turn()
+    sum_b.total(sb_v.at[pl.ds(FIRST, PLANE - FIRST)], sb_v.at[pl.ds(FIRST, PLANE - FIRST)])
+    b_cps = group_copies(0, lambda sl: sb_v.at[sl], out_b, (FIRST, PLANE))
+
+    for cp in send_s:
+        cp.wait_recv()
+    for cp in send_s:
+        cp.wait_send()
+    small_v[...] = small_v[...] + sum(small_in[d] for d in range(planes - 1))
+    small_cps = group_copies(2, lambda sl: small_v, out_small)
+
+    sum_o.combine(lambda t: do_v.at[pl.ds(t, 1)])
+    sum_a.combine(lambda t: da_v.at[pl.ds(t * PLANE, PLANE)])
+
+    sum_c.combine(lambda t: dc_v.at[pl.ds(t * PLANE, PLANE)])
+
     layer.arrive()
 
     def result(at):
@@ -1614,10 +1652,10 @@
     line_v[...] = jnp.zeros(line_v.shape, F32)
     strips(length, middle)
     line = line_v[0:1]
+    last_v[...] = jnp.zeros(last_v.shape, F32)
     for j in range(width // 128):
-        small_v[base + 1, j : j + 1] = line[:, j * 128 : (j + 1) * 128]
-        small_v[base + 2, j : j + 1] = g_mid_gain[0:1, j * 128 : (j + 1) * 128]
-    for cp in send_s:
+        last_v[j : j + 1] = line[:, j * 128 : (j + 1) * 128]
+    for cp in send_l:
         cp.start()
 
     sum_o.total(so_v, do_v.at[pl.ds(me.g, 1)])
@@ -1645,12 +1683,15 @@
     sum_a.total(sa_v, da_v.at[pl.ds(me.g * PLANE, PLANE)])
     a_cps = group_copies(1, lambda sl: sa_v.at[sl], out_a)
 
-    for cp in send_s:
+    sum_c.total(sc_v, dc_v.at[pl.ds(me.g * PLANE, PLANE)])
+    c_cps = group_copies(5, lambda sl: sc_v.at[sl], out_c)
+
+    for cp in send_l:
         cp.wait_recv()
-    for cp in send_s:
+    for cp in send_l:
         cp.wait_send()
-    small_v[...] = small_v[...] + sum(small_in[d] for d in range(planes - 1))
-    small_cps = group_copies(2, lambda sl: small_v, out_small)
+    last_v[...] = last_v[...] + sum(last_in[d] for d in range(planes - 1))
+    line_cps = group_copies(6, lambda sl: last_v, out_line)
 
     group_wait(2, small_cps, out_small)
     d_cp.wait_send()
@@ -1668,7 +1709,9 @@
 
     o_each(lambda cp: cp.wait_send(), lambda cp: cp.wait())
     group_wait(1, a_cps, out_a)
-    for group in (sum_b, sum_a, sum_o):
+    group_wait(5, c_cps, out_c)
+    group_wait(6, line_cps, out_line)
+    for group in (sum_b, sum_a, sum_c, sum_o):
         group.finish()
     scatter.finish_cores()
     scatter.finish_chips()
@@ -1684,7 +1727,7 @@
     taps = cfg["kq"] * length
     pad_rows = -(-SIDE // o_all.shape[1])
     piece = 2 * cfg["dh"] // planes
-    small = (4, 16, 128)
+    small = (3, 16, 128)
     hbm, vmem, smem = pl.BlockSpec(memory_space=pl.ANY), pl.BlockSpec(memory_space=pltpu.VMEM), pl.BlockSpec(memory_space=pltpu.SMEM)
     sds = jax.ShapeDtypeStruct
     dma = pltpu.SemaphoreType.DMA
@@ -1692,25 +1735,28 @@
     others = planes - 1
     v16 = lambda *shape: pltpu.VMEM(shape, BF16)
     v32 = lambda *shape: pltpu.VMEM(shape, F32)
-    b_block, a_block, o_block = (PLANE - 1, r, 2 * ff), (PLANE, r, QKV), (1, piece, width)
+    b_block, o_block = (PLANE - FIRST, r, 2 * ff), (1, piece, width)
+    a_block, c_block = (PLANE, r, SIDE), (PLANE, r, QKV - SIDE)
     return pl.pallas_call(
         functools.partial(backward_kernel, cfg),
         out_shape=(
-            sds((length, width), F32), sds((length, width), F32), sds((GROUP, r, QKV), BF16), sds((GROUP, r, 2 * ff), BF16),
-            sds((2, chunk, width), BF16), sds((2, piece, width), BF16), sds((GROUP,) + small, F32),
+            sds((length, width), F32), sds((length, width), F32), sds((GROUP, r, SIDE), BF16), sds((GROUP, r, QKV - SIDE), BF16),
+            sds((GROUP, r, 2 * ff), BF16),
+            sds((2, chunk, width), BF16), sds((2, piece, width), BF16), sds((GROUP,) + small, F32), sds((GROUP, 16, 128), F32),
         ),
         in_specs=[hbm] * 16 + [vmem] * 4,
-        out_specs=(vmem,) + (hbm,) * 6,
+        out_specs=(vmem,) + (hbm,) * 8,
         scratch_shapes=[
             v32(*args[14].shape), v32(*args[15].shape), v16(*rows, width), v16(pad_rows, *o_all.shape[1:]), v16(n, r, QKV), v16(2, *rows, PLANE * r), v16(SLOTS, length, 3 * SIDE),
             v16(SLOTS, 2, 2, length, length), v16(SLOTS, 2, length, length),
             v16(2, taps, length), v16(length, taps), v32(length + 8, length), v32(2, length, taps), v16(*rows, QKV),
-            v16(n, r, QKV), v16(planes, piece, width), v16(length, width), v32(8, SIDE), v32(8, width), v32(16, 128),
-            v16(others, *b_block), v16(others, *a_block), v16(others, *o_block), v16(*b_block), v16(*a_block), v16(*o_block),
-            v16(PLANE, r, 2 * ff), v16(*a_block), v16(*o_block), v16(*b_block), v32(64, width), v16(chunk, width),
-            v32(*small), v32(others, *small),
+            v16(n, r, SIDE), v16(n, r, QKV - SIDE), v16(planes, piece, width), v16(length, width), v32(8, SIDE), v32(8, width), v32(16, 128),
+            v16(others, *b_block), v16(others, *a_block), v16(others, *c_block), v16(others, *o_block),
+            v16(*b_block), v16(*a_block), v16(*c_block), v16(*o_block),
+            v16(PLANE, r, 2 * ff), v16(*a_block), v16(*c_block), v16(*o_block), v16(*b_block), v32(64, width), v16(chunk, width),
+            v32(*small), v32(others, *small), v32(16, 128), v32(others, 16, 128),
             *Scatter.scratch(length, width), *Scatter.scratch(length, width, cores=False),
-            dma((3, planes)), dma((3, planes)), dma((others,)), dma((others,)), dma((5, GROUP)), dma((5, GROUP)),
+            dma((4, planes)), dma((4, planes)), dma((others,)), dma((others,)), dma((others,)), dma((others,)), dma((7, GROUP)), dma((7, GROUP)),
             dma((12,)), dma((4, GROUP)),
         ],
         compiler_params=pltpu.CompilerParams(collective_id=3, has_side_effects=True, vmem_limit_bytes=54 * 2**20),
@@ -1718,7 +1764,7 @@
     )(*args)
 
 
-def results_kernel(cfg, a_ref, b_ref, d_ref, o_ref, small_ref, g_tok, layer, qkv_ref, gate_ref, up_ref, down_ref, out_ref,
+def results_kernel(cfg, a_ref, c_ref, b_ref, d_ref, o_ref, small_ref, line_ref, g_tok, layer, qkv_ref, gate_ref, up_ref, down_ref, out_ref,
                    taps_ref, mix_ref, in_ref, mid_ref, heads_ref, tok_ref, layer_ref, vec_v):
     planes, ff = cfg["planes"], cfg["ff"]
     rows, width = out_ref.shape
@@ -1735,7 +1781,10 @@
         return even[0], jnp.where(low, even[1], o0), jnp.where(low, o0, o1)
 
     def tiles(pair, j):
-        t = lambda i: a_ref[slot(pair), :, i * 128 : (i + 1) * 128].astype(F32)
+        def t(i):
+            ref, i = (a_ref, i) if i < 2 else (c_ref, i - 2)
+            return ref[slot(pair), :, i * 128 : (i + 1) * 128].astype(F32)
+
         if j == 2:
             return t(4), pltpu.roll(t(1), 64, 1)
         return t(2 * j), t(2 * j + 1)
@@ -1761,19 +1810,26 @@
     @pl.when(pl.program_id(0) == 0)
     def _():
         base = 1
-        for pair in range(GROUP):
-            taps = jnp.transpose(jnp.concatenate([small_ref[slot(pair), 0], jnp.zeros((112, 128), F32)], axis=0))
-            for g in range(2):
-                taps_ref[2 * pair + g] = taps[g * cfg["kq"] : (g + 1) * cfg["kq"], 0 : cfg["kk"]]
-            mixed = jnp.sum(small_ref[slot(pair), base], axis=-1, keepdims=True)
-            for o in range(2):
-                for g in range(2):
-                    mix_ref[2 * pair + o : 2 * pair + o + 1, g : g + 1] = mixed[2 * o + g : 2 * o + g + 1]
+        heads = 2 * GROUP
+        taps = small_ref[0, 0]
+        for s in range(1, GROUP):
+            taps = taps + small_ref[s, 0]
+        for k in range(cfg["kk"]):
+            for q in range(cfg["kq"]):
+                taps_ref[k, q : q + 1] = taps[k : k + 1, q * heads : (q + 1) * heads]
+        mixed = [jnp.sum(small_ref[slot(pair), base], axis=-1, keepdims=True) for pair in range(GROUP)]
+        for g in range(2):
+            line = jnp.zeros((1, heads), F32)
+            for pair in range(GROUP):
+                for o in range(2):
+                    k = 2 * o + g
+                    line = jnp.where(lanes(1, heads) == 2 * pair + o, mixed[pair][k : k + 1], line)
+            mix_ref[g : g + 1] = line
         vec_v[...] = jnp.zeros(vec_v.shape, F32)
-        for k in range(2):
-            total = small_ref[0, base + 1 + k]
+        for k, part in enumerate((lambda s: line_ref[s], lambda s: small_ref[s, base + 1])):
+            total = part(0)
             for s in range(1, GROUP):
-                total = total + small_ref[s, base + 1 + k]
+                total = total + part(s)
             for j in range(width // 128):
                 vec_v[k : k + 1, j * 128 : (j + 1) * 128] = total[j : j + 1]
         line = lambda pair: tuple(small_ref[slot(pair), base, 4 + j : 5 + j] for j in range(2))
@@ -1786,41 +1842,43 @@
             ref[...] = mine[k : k + 1, 0:own]
 
 
-def results_call(cfg, out_a, out_b, out_d, out_o, small, g_tokens, layer_out):
+def results_call(cfg, out_a, out_c, out_b, out_d, out_o, small, line, g_tokens, layer_out):
     r = out_a.shape[1]
     _, chunk, width = out_d.shape
     half = r // 2
     sds = jax.ShapeDtypeStruct
     whole = lambda shape: pl.BlockSpec(shape, lambda i: (0,) * len(shape))
     rows = lambda n, w: pl.BlockSpec((n, w), lambda i: (i, 0))
-    moved = 2 * (out_a.size + out_b.size + out_d.size + out_o.size) + 4 * (out_a.size + out_b.size + out_d.size + out_o.size)
+    moved = 6 * (out_a.size + out_c.size + out_b.size + out_d.size + out_o.size) + 16 * g_tokens.size
     return pl.pallas_call(
         functools.partial(results_kernel, cfg),
         grid=(2,),
         out_shape=(
             sds((r, 3 * width), F32), sds((r, n_cols(cfg)), F32), sds((r, n_cols(cfg)), F32), sds((2 * chunk, width), F32),
-            sds((r, width), F32), sds((2 * GROUP, cfg["kq"], cfg["kk"]), F32), sds((2 * GROUP, 2), F32),
+            sds((r, width), F32), sds((cfg["kk"], cfg["kq"], 2 * GROUP), F32), sds((2, 2 * GROUP), F32),
             sds((1, r), F32), sds((1, r), F32), sds((1, r), F32), sds(g_tokens.shape, F32), sds(g_tokens.shape, F32),
         ),
         in_specs=[
             pl.BlockSpec((GROUP, half, out_a.shape[2]), lambda i: (0, i, 0)),
+            pl.BlockSpec((GROUP, half, out_c.shape[2]), lambda i: (0, i, 0)),
             pl.BlockSpec((GROUP, half, out_b.shape[2]), lambda i: (0, i, 0)),
             pl.BlockSpec((1, chunk, width), lambda i: (i, 0, 0)),
             pl.BlockSpec((1, half, width), lambda i: (i, 0, 0)),
             whole(small.shape),
+            whole(line.shape),
             rows(g_tokens.shape[0] // 2, width),
             rows(g_tokens.shape[0] // 2, width),
         ],
         scratch_shapes=[pltpu.VMEM((8, width), F32)],
         out_specs=(
             rows(half, 3 * width), rows(half, n_cols(cfg)), rows(half, n_cols(cfg)), rows(chunk, width), rows(half, width),
-            whole((2 * GROUP, cfg["kq"], cfg["kk"])), whole((2 * GROUP, 2)),
+            whole((cfg["kk"], cfg["kq"], 2 * GROUP)), whole((2, 2 * GROUP)),
             whole((1, r)), whole((1, r)), whole((1, r)), rows(g_tokens.shape[0] // 2, width), rows(g_tokens.shape[0] // 2, width),
         ),
         compiler_params=pltpu.CompilerParams(vmem_limit_bytes=60 * 2**20),
         cost_estimate=pl.CostEstimate(flops=0, bytes_accessed=moved, transcendentals=0),
         name="results",
-    )(out_a, out_b, out_d, out_o, small, g_tokens, layer_out)
+    )(out_a, out_c, out_b, out_d, out_o, small, line, g_tokens, layer_out)
 
 
 def n_cols(cfg):
@@ -1869,28 +1927,29 @@
 
     gain_rows = jnp.pad(jnp.stack([norm_in, norm_mid, norm_heads]).astype(F32), ((0, 5), (0, 128 - r)))
     tok, ct = tokens[0], cotangent[0]
+    kern, mix = kernel.transpose(2, 1, 0), mixing.T
 
     (_, ct_all, a_all, b_all, d_all, o_all, nrm_all, qkv_all, p_all, m_all, gated_all, mid_all, resid, gains, ends) = (
         forward_call(
-            cfg, tok, ct, w_qkv, w_gate, w_up, w_down, w_out, kernel, mixing, gain_rows, doc_lengths, pad_counts
+            cfg, tok, ct, w_qkv, w_gate, w_up, w_down, w_out, kern, mix, gain_rows, doc_lengths, pad_counts
         )
     )
     g_res, branch_all, dw_b, sum_d, sum_first, out_red, g_mid_gain = feed_call(cfg, mid_all, ct_all, b_all, d_all, resid, gains)
-    g_tokens, layer_out, out_a, out_b, out_d, out_o, small = backward_call(
+    g_tokens, layer_out, out_a, out_c, out_b, out_d, out_o, small, line = backward_call(
         cfg, branch_all, o_all, a_all, nrm_all, qkv_all, p_all, m_all, gated_all, dw_b.reshape(n, r, 2 * ff), sum_d, sum_first, out_red,
-        tok, resid, kernel, mixing, g_res, gains, ends, g_mid_gain,
+        tok, resid, kern, mix, g_res, gains, ends, g_mid_gain,
     )
 
     g_qkv, g_gate, g_up, g_down, g_out, g_kernel, g_mixing, g_in, g_mid, g_heads, g_tokens, layer_out = results_call(
-        cfg, out_a, out_b, out_d, out_o, small, g_tokens, layer_out
+        cfg, out_a, out_c, out_b, out_d, out_o, small, line, g_tokens, layer_out
     )
     return (
         layer_out[None],
         g_tokens[None],
         g_in[0],
         g_qkv,
-        g_kernel,
-        g_mixing,
+        g_kernel.transpose(2, 1, 0),
+        g_mixing.T,
         g_heads[0],
         g_out,
         g_mid[0],

time: 345 us -> 336 us (0.974)
  local copies, waits for them, and re-layouts: 8.62 us -> 2.83 us
    unnamed x12 -> x8, local copies, waits for them, and re-layouts: 8.62 us -> 2.83 us
where the time goes in v4:
time: 336 us
  Pallas kernels  330 us (98%)
    pallas_call x1, Pallas kernels, forward_call(): pl.pallas_call(functools.partial(forward_kernel, cfg), out_shape=(sds(row...  143 us
    pallas_call x1, Pallas kernels, backward_call(): pl.pallas_call(functools.partial(backward_kernel, cfg), out_shape=(sds((l...  108 us
    pallas_call x1, Pallas kernels, feed_call(): pl.pallas_call(functools.partial(feed_kernel, cfg), out_shape=(sds((lengt...  72 us

profile of v4, /device:TPU:0, one launch (start us, length us, event | category | flops | bytes accessed | tf_op | source)
XLA Modules:
  0.0 335.9 jit_solution(9165689596612805035)
XLA Ops:
  1.3 1.3 fusion.9.refs_9_
  2.6 143.4 %attention_forward.1 = (bf16[8,256,1536]{2,1,0:T(8,128)(2,1)}, bf16[8,256,1536]{2,1,0:T(8,128)(2,1)}, bf16[16,96,640]{2,1,0:T(8,128)(2,1)}, bf16[16,96,1024]{2,1...) custom-call(bf16[256,1536]{1,0:T(8,128)(2,1)} %bitcast.16, ...), custom_call_target="tpu_custom_call" | custom-call | tf_op jit(solution)/shard_map/attention_forward/pallas_call | solution.py:1126
  146.0 0.0 copy-start.2
  146.0 0.8 copy-done.2
  146.8 72.0 %feed_forward.1 = (f32[256,1536]{1,0:T(8,128)}, bf16[8,256,1536]{2,1,0:T(8,128)(2,1)}, bf16[1536,1024]{1,0:T(8,128)(2,1)}, bf16[128,1536]{1,0:T(8,128)(2,1)S(1)}...) custom-call(bf16[8,256,1536]{2,1,0:T(8,128)(2,1)} %get-tuple-element.54.refs_0_, ...), custom_call_target="tpu_custom_call" | custom-call | tf_op jit(solution)/shard_map/feed_forward/pallas_call | solution.py:1333
  218.9 0.0 copy-start
  218.9 0.7 copy-done
  219.6 0.0 copy-start.1
  219.6 0.7 copy-done.1
  220.3 0.0 copy-start.3
  220.3 0.6 copy-done.3
  220.9 108.1 %attention_backward.1 = (f32[256,1536]{1,0:T(8,128)}, f32[256,1536]{1,0:T(8,128)}, bf16[8,96,256]{2,1,0:T(8,128)(2,1)}, bf16[8,96,384]{2,1,0:T(8,128)(2,1)}, bf1...) custom-call(bf16[8,256,1536]{2,1,0:T(8,128)(2,1)} %get-tuple-element, ...), custom_call_target="tpu_custom_call" | custom-call | tf_op jit(solution)/shard_map/attention_backward/pallas_call | solution.py:1740
  329.1 6.6 %results.1 = (f32[96,4608]{1,0:T(8,128)}, f32[96,4096]{1,0:T(8,128)}, f32[96,4096]{1,0:T(8,128)}, f32[256,1536]{1,0:T(8,128)}, f32[96,1536]{1,0:T(8,128)}, /*ind...) custom-call(bf16[8,96,256]{2,1,0:T(8,128)(2,1)} %get-tuple-element.7, ...), custom_call_target="tpu_custom_call" | custom-call | bytes 17203200 | tf_op jit(solution)/shard_map/results/pallas_call | solution.py:1853
Async XLA Ops:
  146.0 0.8 copy-start.2
  218.9 0.7 copy-start
  219.6 0.7 copy-start.1
  220.3 0.6 copy-start.3

commit v5 on v4

--- a/solution.py
+++ b/solution.py
@@ -47,14 +47,16 @@
         c = self.c + dc - 2 * dc * self.c
         return y * 4 + x * 2 + c
 
-    def greet(self):
+    def hail(self):
         sem = pltpu.get_barrier_semaphore()
         n = self.planes * PLANE
         for d in range(1, n):
             pl.semaphore_signal(sem, inc=1, device_id=(self.y, lax.rem(self.f + d, n)), device_id_type=MESH)
         for s in range(PLANE):
             pl.semaphore_signal(sem, inc=1, device_id=(1 - self.y, self.g * PLANE + s), device_id_type=MESH)
-        pl.semaphore_wait(sem, n - 1 + PLANE)
+
+    def await_all(self):
+        pl.semaphore_wait(pltpu.get_barrier_semaphore(), self.planes * PLANE - 1 + PLANE)
 
 
 def meet(me, sem):
@@ -726,8 +728,8 @@
 
 def forward_kernel(cfg, *refs):
     (tok, ct, w_qkv, w_gate, w_up, w_down, w_o, kern_in, mix_in, gain_rows, docs, pads,
-     tok_all, ct_all, a_all, b_all, d_all, o_all, nrm_all, qkv_all, p_all, m_all, gated_all, mid_all, resid, gains, ends,
-     kern, mix, wq_v, w_a, w_b, meta, gain_v, ct_v, down_v, own_o,
+     tok_all, ct_all, a_all, b_all, d_all, o_all, nrm_all, qkv_all, p_all, m_all, gated_all, mid_all, resid, ends,
+     gains, kern, mix, wq_v, w_a, w_b, meta, gain_v, ct_v, down_v, own_o,
      x_v, wa_v, wo_v, t_v, cat_v, shift_v, qkv_v, p_v, m_v, gated_v, meta_v, mid_v, tok_v,
      out_v, red, diag, near, rs_send, rs_recv,
      g_send, g_recv, g_loc, a_send, a_recv, ch_send, ch_recv, o_send, o_recv, meta_send, meta_recv, gain_send, gain_recv, meet_sems, loc, pack, row_in, row_out) = refs
@@ -737,6 +739,8 @@
     scale = dh ** (-0.5)
     ff, chunk = cfg["ff"], cfg["ff"] // planes
     me = Place(planes)
+
+    me.hail()
 
     wq_in = pltpu.make_async_copy(w_qkv, wq_v, loc.at[1])
     wq_in.start()
@@ -803,7 +807,7 @@
     tok_in.wait()
     for cp in taps_in:
         cp.wait()
-    me.greet()
+    me.await_all()
 
     def first(src, dst_all, base):
         cps = []
@@ -951,6 +955,8 @@
     v0, v1 = gain_v[2 * me.pair], pltpu.roll(gain_v[2 * me.pair + 1], 96, 1)
     gains[2:3, 0:128] = jnp.where(lane < 96, v0, v1)[2:3]
     gains[2:3, 128:256] = jnp.where(lane < 64, v1, 0.0)[2:3]
+
+    resid[length:] = gains[...]
 
     def norms(i, carry):
         row, _ = order(me, i)
@@ -1130,12 +1136,12 @@
             sds((n, r, QKV), BF16), sds((n, r, 2 * ff), BF16), sds((planes, chunk, width), BF16),
             sds((per_pair,) + w_o.shape, BF16), sds(rows + (width,), BF16), sds(rows + (3 * SIDE,), BF16),
             sds((GROUP, 2, 2, length, length), BF16), sds((GROUP, 2, length, length), BF16), sds(rows + (SIDE,), BF16),
-            sds(rows + (width,), BF16), sds((length, width), F32), sds((8, width), F32), sds((GROUP, 8, length), F32),
+            sds(rows + (width,), BF16), sds((length + 8, width), F32), sds((GROUP, 8, length), F32),
         ),
         in_specs=[hbm] * 9 + [vmem] + [smem] * 2,
-        out_specs=(hbm,) * 12 + (vmem,) * 3,
+        out_specs=(hbm,) * 12 + (vmem,) * 2,
         scratch_shapes=[
-            v32(*kern.shape), v32(*mix.shape), v16(*w_qkv.shape), v16(PLANE, r, QKV), v16(PLANE, r, 2 * ff), v32(8, length), v32(n, 8, 128), v16(length, width), v16(chunk, width), v16(*w_o.shape),
+            v32(8, width), v32(*kern.shape), v32(*mix.shape), v16(*w_qkv.shape), v16(PLANE, r, QKV), v16(PLANE, r, 2 * ff), v32(8, length), v32(n, 8, 128), v16(length, width), v16(chunk, width), v16(*w_o.shape),
             v16(*rows, width), v16(n, r, QKV), v16(pad_rows, *w_o.shape),
             v16(2, 3 * length, taps), v16(length, 3 * length), v32(length + 8, taps),
             v16(*rows, 3 * SIDE), v16(GROUP, 2, 2, length, length), v16(GROUP, 2, length, length), v16(*rows, SIDE),
@@ -1151,15 +1157,17 @@
 
 
 def feed_kernel(cfg, *refs):
-    (mid_all, ct_all, w_b, w_d, resid, gains,
-     g_res, branch_all, dw_b, sum_d, sum_first, out_red, g_mid_gain,
-     mid_v, ct_v, wb_v, wd_v, hid_v, gu_v, tile_v, dd_v, zd_v, via_v, sd_v, first_v, zf_v, via_f, sf_v,
+    (mid_all, ct_all, w_b, w_d, resid,
+     g_res, branch_all, dw_b, out_red,
+     mid_v, ct_v, wb_v, wd_v, hid_v, gu_v, tile_v, dd_v, zd_v, via_v, sd_v, first_v, zf_v, via_f, sf_v, flat_v,
      o_out, o_red, o_send, o_recv,
      m_out, m_red, m_diag, m_near, m_send, m_recv,
      g_send, g_recv, g_loc, z_send, z_recv, loc, row_in, out_sem) = refs
-    length, width = resid.shape
+    length, width = ct_all.shape[1:]
     ff = cfg["ff"]
+    gain = slice(length + 1, length + 2)
     me = Place(cfg["planes"])
+    me.hail()
     wb_in = pltpu.make_async_copy(w_b, wb_v, loc.at[0])
     wb_in.start()
     wd_in = pltpu.make_async_copy(w_d, wd_v, loc.at[1])
@@ -1174,7 +1182,7 @@
     for i in range(2):
         for cp in row_copies(order(me, i)[0]):
             cp.start()
-    me.greet()
+    me.await_all()
     sum_out = Scatter(me, o_out, o_red, None, None, o_send, o_recv)
     down_sum = Collect(me, lambda b: dd_v.at[pl.ds(b, 1)], zd_v, via_v, z_send.at[0], z_recv.at[0])
     down_sum.clear()
@@ -1274,15 +1282,15 @@
 
     lax.fori_loop(0, steps, gate_up, 0)
     first_sum.start()
-    g_mid_gain[...] = jnp.zeros(g_mid_gain.shape, F32)
+    g_res[length:] = jnp.zeros((8, width), F32)
     sum_mid.arrive()
 
     def middle(at):
         g_mid = sum_mid.total(at)
         res = resid[at]
         s = lax.rsqrt(jnp.mean(res * res, axis=-1, keepdims=True) + 1e-6)
-        g_mid_gain[0:1] = g_mid_gain[0:1] + jnp.sum(g_mid * res * s, axis=0, keepdims=True)
-        pulled = g_mid * gains[1:2]
+        g_res[length : length + 1] = g_res[length : length + 1] + jnp.sum(g_mid * res * s, axis=0, keepdims=True)
+        pulled = g_mid * resid[gain]
         back = ct_v[me.slot, at].astype(F32) + s * pulled
         back = back - res * (s * s * s * jnp.mean(pulled * res, axis=-1, keepdims=True))
         g_res[at] = back
@@ -1293,7 +1301,7 @@
     branch.start()
 
     lax.fori_loop(0, GROUP, output, 0)
-    red_out = pltpu.make_async_copy(o_red, out_red, out_sem.at[2])
+    red_out = pltpu.make_async_copy(o_red, out_red.at[pl.ds(0, 4)], out_sem.at[2])
     red_out.start()
     down_sum.combine(lambda t: dd_v.at[pl.ds(t, 1)])
     branch.relay()
@@ -1301,10 +1309,15 @@
     branch.share()
     branch.last()
     down_sum.total(sd_v, dd_v.at[pl.ds(me.g, 1)])
-    sd_out = pltpu.make_async_copy(sd_v.at[0], sum_d, out_sem.at[3])
+    sd_out = pltpu.make_async_copy(sd_v.at[0], out_red.at[4, pl.ds(0, sd_v.shape[1])], out_sem.at[3])
     sd_out.start()
     first_sum.total(sf_v, first_v.at[me.g])
-    sf_out = pltpu.make_async_copy(sf_v, sum_first, out_sem.at[4])
+    flat_v[...] = sf_v[...].reshape(flat_v.shape)
+    r = sf_v.shape[1]
+    own_rows = pl.ds(pl.multiple_of(me.g * (PLANE * r), 16), FIRST * r)
+    tile_out(steps - 2).wait()
+    tile_out(steps - 1).wait()
+    sf_out = pltpu.make_async_copy(flat_v, dw_b.at[own_rows], out_sem.at[4])
     sf_out.start()
     branch.finish()
     sum_mid.finish_cores()
@@ -1312,15 +1325,13 @@
     sum_out.finish_cores()
     down_sum.finish()
     first_sum.finish()
-    tile_out(steps - 2).wait()
-    tile_out(steps - 1).wait()
     red_out.wait()
     sd_out.wait()
     sf_out.wait()
 
 
-def feed_call(cfg, mid_all, ct_all, w_b, w_d, resid, gains):
-    length, width = resid.shape
+def feed_call(cfg, mid_all, ct_all, w_b, w_d, resid):
+    length, width = ct_all.shape[1:]
     ff = cfg["ff"]
     hbm, vmem = pl.BlockSpec(memory_space=pl.ANY), pl.BlockSpec(memory_space=pltpu.VMEM)
     sds = jax.ShapeDtypeStruct
@@ -1333,29 +1344,29 @@
     return pl.pallas_call(
         functools.partial(feed_kernel, cfg),
         out_shape=(
-            sds((length, width), F32), sds(rows + (width,), BF16),
-            sds((width, 2 * ff), BF16), sds((chunk, width), BF16), sds((FIRST, r, 2 * ff), BF16), sds((4, length, width), BF16), sds((8, width), F32),
+            sds((length + 8, width), F32), sds(rows + (width,), BF16),
+            sds((width, 2 * ff), BF16), sds((5, length, width), BF16),
         ),
-        in_specs=[hbm] * 4 + [vmem] * 2,
-        out_specs=(vmem, hbm, hbm, hbm, hbm, hbm, vmem),
+        in_specs=[hbm] * 4 + [vmem],
+        out_specs=(vmem, hbm, hbm, hbm),
         scratch_shapes=[
             v16(*rows, width), v16(*rows, width), v16(*w_b.shape), v16(*w_d.shape), v16(*rows, ff), v16(*rows, 2 * ff),
             v16(2, SIDE, 2 * ff), v16(others + 1, chunk, width), v16(others, 1, chunk, width), v16(1, chunk, width), v16(1, chunk, width),
-            v16(others + 1, FIRST, r, 2 * ff), v16(others, FIRST, r, 2 * ff), v16(FIRST, r, 2 * ff), v16(FIRST, r, 2 * ff),
+            v16(others + 1, FIRST, r, 2 * ff), v16(others, FIRST, r, 2 * ff), v16(FIRST, r, 2 * ff), v16(FIRST, r, 2 * ff), v16(FIRST * r, 2 * ff),
             *Scatter.scratch(length, width, chips=False), *Scatter.scratch(length, width),
             dma((Gather.SENDS,)), dma((Gather.RECVS,)), dma((1,)), dma((2, others + 1)), dma((2, others + 1)),
             dma((2,)), dma((2, GROUP)), dma((5,)),
         ],
         compiler_params=pltpu.CompilerParams(collective_id=2, has_side_effects=True, vmem_limit_bytes=52 * 2**20),
         name="feed_forward",
-    )(mid_all, ct_all, w_b, w_d, resid, gains)
+    )(mid_all, ct_all, w_b, w_d, resid)
 
 
 def backward_kernel(cfg, *refs):
-    (branch_all, o_all, a_all, nrm_all, qkv_all, p_all, m_all, gated_all, dw_b, sum_d, sum_first, out_red, tok,
-     resid, kern_in, mix_in, g_res, gains, ends, g_mid_gain,
+    (branch_all, o_all, a_all, nrm_all, qkv_all, p_all, m_all, gated_all, dw_b, out_red, tok,
+     resid, kern_in, mix_in, g_res, ends,
      g_tokens, layer_out, out_a, out_c, out_b, out_d, out_o, out_small, out_line,
-     kern, mix, gb_v, wo_v, wa_v, nrm_v, qkv_v, p_v, m_v, t_v, cat_v, shift_v, corr_v, gq_v, da_v, dc_v, do_v, tok_v, rows_v, line_v, taps_v,
+     gains, kern, mix, gb_v, wo_v, wa_v, nrm_v, qkv_v, p_v, m_v, t_v, cat_v, shift_v, corr_v, gq_v, da_v, dc_v, do_v, tok_v, rows_v, line_v, taps_v,
      zb_v, za_v, zc_v, zo_v, via_b, via_a, via_c, via_o, sb_v, sa_v, sc_v, so_v, far_b, strip_v, sd_v, small_v, small_in, last_v, last_in,
      s_out, s_red, s_diag, s_near, rs_send, rs_recv,
      l_red, l_diag, l_near, l_send, l_recv,
@@ -1371,8 +1382,8 @@
         pltpu.make_async_copy(src, dst, loc.at[i])
         for i, (src, dst) in enumerate(
             [(a_all, wa_v), (o_all, wo_v.at[pl.ds(0, per_pair)]), (tok, tok_v)]
-            + [(dw_b.at[pl.ds(me.g * PLANE + FIRST, PLANE - FIRST)], sb_v.at[pl.ds(FIRST, PLANE - FIRST)]), (sum_first, sb_v.at[pl.ds(0, FIRST)])]
-            + [(dw_b.at[pl.ds(far * PLANE + FIRST, PLANE - FIRST)], far_b), (out_red, l_red), (sum_d, sd_v)]
+            + [(dw_b.at[pl.ds(me.g * PLANE, PLANE)], sb_v), (resid.at[pl.ds(length, 8)], gains)]
+            + [(dw_b.at[pl.ds(far * PLANE + FIRST, PLANE - FIRST)], far_b), (out_red.at[pl.ds(0, 4)], l_red), (out_red.at[4, pl.ds(0, sd_v.shape[0])], sd_v)]
         )
     ]
 
@@ -1395,6 +1406,7 @@
             cps.append(pltpu.make_async_copy(src.at[row], dst.at[at], row_in.at[j + 1, i]))
         return cps
 
+    me.hail()
     taps_in = [pltpu.make_async_copy(kern_in, kern, loc.at[10]), pltpu.make_async_copy(mix_in, mix, loc.at[11])]
     for cp in taps_in:
         cp.start()
@@ -1417,7 +1429,7 @@
     corr_v[...] = jnp.zeros(corr_v.shape, F32)
     rows_v[...] = jnp.zeros(rows_v.shape, F32)
     small_v[...] = jnp.zeros(small_v.shape, F32)
-    me.greet()
+    me.await_all()
 
     blocks4 = lambda ref: (lambda b: ref.at[pl.ds(b * PLANE, PLANE)])
     sum_b = Collect(me, lambda b: dw_b.at[pl.ds(b * PLANE + FIRST, PLANE - FIRST)], zb_v, via_b, z_send.at[0], z_recv.at[0])
@@ -1472,6 +1484,7 @@
     layer.push(1)
     layer.push(3)
     layer.ahead()
+    loads[3].wait()
     loads[4].wait()
     group_copies(0, lambda sl: sb_v.at[sl], out_b, (0, FIRST))
     loads[7].wait()
@@ -1554,8 +1567,7 @@
         return carry
 
     lax.fori_loop(0, GROUP, one, 0)
-    for i in (2, 3):
-        loads[i].wait()
+    loads[2].wait()
     gated_in = [
         pltpu.make_async_copy(gated_all.at[i], p_v.at[i // 4, i // 2 % 2, i % 2], row_in.at[0, i]) for i in range(GROUP)
     ]
@@ -1586,7 +1598,7 @@
         small_v[base, 4 + j : 5 + j] = rows_v[0:1, j * 128 : (j + 1) * 128]
 
     for j in range(width // 128):
-        small_v[2, j : j + 1] = g_mid_gain[0:1, j * 128 : (j + 1) * 128]
+        small_v[2, j : j + 1] = g_res[length : length + 1, j * 128 : (j + 1) * 128]
     for cp in send_s:
         cp.start()
 
@@ -1719,7 +1731,7 @@
 
 
 def backward_call(cfg, *args):
-    branch_all, o_all, a_all, tok = args[0], args[1], args[2], args[12]
+    branch_all, o_all, a_all, tok = args[0], args[1], args[2], args[10]
     length, width = tok.shape
     planes, ff = cfg["planes"], cfg["ff"]
     n, r = a_all.shape[:2]
@@ -1744,10 +1756,10 @@
             sds((GROUP, r, 2 * ff), BF16),
             sds((2, chunk, width), BF16), sds((2, piece, width), BF16), sds((GROUP,) + small, F32), sds((GROUP, 16, 128), F32),
         ),
-        in_specs=[hbm] * 16 + [vmem] * 4,
+        in_specs=[hbm] * 14 + [vmem] * 2,
         out_specs=(vmem,) + (hbm,) * 8,
         scratch_shapes=[
-            v32(*args[14].shape), v32(*args[15].shape), v16(*rows, width), v16(pad_rows, *o_all.shape[1:]), v16(n, r, QKV), v16(2, *rows, PLANE * r), v16(SLOTS, length, 3 * SIDE),
+            v32(8, width), v32(*args[12].shape), v32(*args[13].shape), v16(*rows, width), v16(pad_rows, *o_all.shape[1:]), v16(n, r, QKV), v16(2, *rows, PLANE * r), v16(SLOTS, length, 3 * SIDE),
             v16(SLOTS, 2, 2, length, length), v16(SLOTS, 2, length, length),
             v16(2, taps, length), v16(length, taps), v32(length + 8, length), v32(2, length, taps), v16(*rows, QKV),
             v16(n, r, SIDE), v16(n, r, QKV - SIDE), v16(planes, piece, width), v16(length, width), v32(8, SIDE), v32(8, width), v32(16, 128),
@@ -1846,34 +1858,38 @@
     r = out_a.shape[1]
     _, chunk, width = out_d.shape
     half = r // 2
+    step = 16
+    steps = r // step
+    quarter = g_tokens.shape[0] // 4
     sds = jax.ShapeDtypeStruct
     whole = lambda shape: pl.BlockSpec(shape, lambda i: (0,) * len(shape))
     rows = lambda n, w: pl.BlockSpec((n, w), lambda i: (i, 0))
+    few = lambda n, w, count: pl.BlockSpec((n, w), lambda i: (jnp.minimum(i, count - 1), 0))
     moved = 6 * (out_a.size + out_c.size + out_b.size + out_d.size + out_o.size) + 16 * g_tokens.size
     return pl.pallas_call(
         functools.partial(results_kernel, cfg),
-        grid=(2,),
+        grid=(steps,),
         out_shape=(
             sds((r, 3 * width), F32), sds((r, n_cols(cfg)), F32), sds((r, n_cols(cfg)), F32), sds((2 * chunk, width), F32),
             sds((r, width), F32), sds((cfg["kk"], cfg["kq"], 2 * GROUP), F32), sds((2, 2 * GROUP), F32),
             sds((1, r), F32), sds((1, r), F32), sds((1, r), F32), sds(g_tokens.shape, F32), sds(g_tokens.shape, F32),
         ),
         in_specs=[
-            pl.BlockSpec((GROUP, half, out_a.shape[2]), lambda i: (0, i, 0)),
-            pl.BlockSpec((GROUP, half, out_c.shape[2]), lambda i: (0, i, 0)),
-            pl.BlockSpec((GROUP, half, out_b.shape[2]), lambda i: (0, i, 0)),
-            pl.BlockSpec((1, chunk, width), lambda i: (i, 0, 0)),
-            pl.BlockSpec((1, half, width), lambda i: (i, 0, 0)),
+            pl.BlockSpec((GROUP, step, out_a.shape[2]), lambda i: (0, i, 0)),
+            pl.BlockSpec((GROUP, step, out_c.shape[2]), lambda i: (0, i, 0)),
+            pl.BlockSpec((GROUP, step, out_b.shape[2]), lambda i: (0, i, 0)),
+            pl.BlockSpec((1, chunk, width), lambda i: (jnp.minimum(i, 1), 0, 0)),
+            pl.BlockSpec((1, step, width), lambda i: (lax.div(i, half // step), lax.rem(i, half // step), 0)),
             whole(small.shape),
             whole(line.shape),
-            rows(g_tokens.shape[0] // 2, width),
-            rows(g_tokens.shape[0] // 2, width),
+            few(quarter, width, 4),
+            few(quarter, width, 4),
         ],
         scratch_shapes=[pltpu.VMEM((8, width), F32)],
         out_specs=(
-            rows(half, 3 * width), rows(half, n_cols(cfg)), rows(half, n_cols(cfg)), rows(chunk, width), rows(half, width),
+            rows(step, 3 * width), rows(step, n_cols(cfg)), rows(step, n_cols(cfg)), few(chunk, width, 2), rows(step, width),
             whole((cfg["kk"], cfg["kq"], 2 * GROUP)), whole((2, 2 * GROUP)),
-            whole((1, r)), whole((1, r)), whole((1, r)), rows(g_tokens.shape[0] // 2, width), rows(g_tokens.shape[0] // 2, width),
+            whole((1, r)), whole((1, r)), whole((1, r)), few(quarter, width, 4), few(quarter, width, 4),
         ),
         compiler_params=pltpu.CompilerParams(vmem_limit_bytes=60 * 2**20),
         cost_estimate=pl.CostEstimate(flops=0, bytes_accessed=moved, transcendentals=0),
@@ -1929,15 +1945,15 @@
     tok, ct = tokens[0], cotangent[0]
     kern, mix = kernel.transpose(2, 1, 0), mixing.T
 
-    (_, ct_all, a_all, b_all, d_all, o_all, nrm_all, qkv_all, p_all, m_all, gated_all, mid_all, resid, gains, ends) = (
+    (_, ct_all, a_all, b_all, d_all, o_all, nrm_all, qkv_all, p_all, m_all, gated_all, mid_all, resid, ends) = (
         forward_call(
             cfg, tok, ct, w_qkv, w_gate, w_up, w_down, w_out, kern, mix, gain_rows, doc_lengths, pad_counts
         )
     )
-    g_res, branch_all, dw_b, sum_d, sum_first, out_red, g_mid_gain = feed_call(cfg, mid_all, ct_all, b_all, d_all, resid, gains)
+    g_res, branch_all, dw_b, out_red = feed_call(cfg, mid_all, ct_all, b_all, d_all, resid)
     g_tokens, layer_out, out_a, out_c, out_b, out_d, out_o, small, line = backward_call(
-        cfg, branch_all, o_all, a_all, nrm_all, qkv_all, p_all, m_all, gated_all, dw_b.reshape(n, r, 2 * ff), sum_d, sum_first, out_red,
-        tok, resid, kern, mix, g_res, gains, ends, g_mid_gain,
+        cfg, branch_all, o_all, a_all, nrm_all, qkv_all, p_all, m_all, gated_all, dw_b.reshape(n, r, 2 * ff), out_red,
+        tok, resid, kern, mix, g_res, ends,
     )
 
     g_qkv, g_gate, g_up, g_down, g_out, g_kernel, g_mixing, g_in, g_mid, g_heads, g_tokens, layer_out = results_call(

time: 336 us -> 333 us (level)
  no operation moved by 1% of the time
where the time goes in v5:
time: 333 us; the launch traced here: 332 us
  Pallas kernels  328 us (98%)
    pallas_call x1, Pallas kernels, forward_call(): pl.pallas_call(functools.partial(forward_kernel, cfg), out_shape=(sds(row...  141 us
    pallas_call x1, Pallas kernels, backward_call(): pl.pallas_call(functools.partial(backward_kernel, cfg), out_shape=(sds((l...  106 us
    pallas_call x1, Pallas kernels, feed_call(): pl.pallas_call(functools.partial(feed_kernel, cfg), out_shape=(sds((lengt...  72.4 us
    pallas_call x1, Pallas kernels, results_call(): pl.pallas_call(functools.partial(results_kernel, cfg), grid=(steps,), out...  8.57 us

profile of v5, /device:TPU:0, one launch (start us, length us, event | category | flops | bytes accessed | tf_op | source)
XLA Modules:
  0.0 332.4 jit_solution(11363482610896182949)
XLA Ops:
  1.3 1.3 fusion.9.refs_9_
  2.6 141.4 %attention_forward.1 = (bf16[8,256,1536]{2,1,0:T(8,128)(2,1)}, bf16[8,256,1536]{2,1,0:T(8,128)(2,1)}, bf16[16,96,640]{2,1,0:T(8,128)(2,1)}, bf16[16,96,1024]{2,1...) custom-call(bf16[256,1536]{1,0:T(8,128)(2,1)} %bitcast.16, ...), custom_call_target="tpu_custom_call" | custom-call | tf_op jit(solution)/shard_map/attention_forward/pallas_call | solution.py:1132
  144.0 0.0 copy-start
  144.0 1.4 copy-done
  145.4 72.4 %feed_forward.1 = (f32[264,1536]{1,0:T(8,128)}, bf16[8,256,1536]{2,1,0:T(8,128)(2,1)}, bf16[1536,1024]{1,0:T(8,128)(2,1)}, bf16[5,256,1536]{2,1,0:T(8,128)(2,1)}) custom-call(bf16[8,256,1536]{2,1,0:T(8,128)(2,1)} %get-tuple-element.50.refs_0_, bf16[8,256,1536]{2,1,0:T(8,128)(2,1)} %get-tuple-element.51.refs_1_, ...), custom_call_target="tpu_custom_call" | custom-call | tf_op jit(solution)/shard_map/feed_forward/pallas_call | solution.py:1344
  217.8 105.8 %attention_backward.1 = (f32[256,1536]{1,0:T(8,128)}, f32[256,1536]{1,0:T(8,128)}, bf16[8,96,256]{2,1,0:T(8,128)(2,1)}, bf16[8,96,384]{2,1,0:T(8,128)(2,1)}, bf1...) custom-call(bf16[8,256,1536]{2,1,0:T(8,128)(2,1)} %get-tuple-element, ...), custom_call_target="tpu_custom_call" | custom-call | tf_op jit(solution)/shard_map/attention_backward/pallas_call | solution.py:1752
  323.6 8.6 %results.1 = (f32[96,4608]{1,0:T(8,128)}, f32[96,4096]{1,0:T(8,128)}, f32[96,4096]{1,0:T(8,128)}, f32[256,1536]{1,0:T(8,128)}, f32[96,1536]{1,0:T(8,128)}, /*ind...) custom-call(bf16[8,96,256]{2,1,0:T(8,128)(2,1)} %get-tuple-element.6, ...), custom_call_target="tpu_custom_call" | custom-call | bytes 17203200 | tf_op jit(solution)/shard_map/results/pallas_call | solution.py:1869
Async XLA Ops:
  144.0 1.4 copy-start

commit v6 on v5

--- a/solution.py
+++ b/solution.py
@@ -1357,7 +1357,7 @@
             dma((Gather.SENDS,)), dma((Gather.RECVS,)), dma((1,)), dma((2, others + 1)), dma((2, others + 1)),
             dma((2,)), dma((2, GROUP)), dma((5,)),
         ],
-        compiler_params=pltpu.CompilerParams(collective_id=2, has_side_effects=True, vmem_limit_bytes=52 * 2**20),
+        compiler_params=pltpu.CompilerParams(collective_id=2, has_side_effects=True, vmem_limit_bytes=63 * 2**20),
         name="feed_forward",
     )(mid_all, ct_all, w_b, w_d, resid)
 
@@ -1858,38 +1858,34 @@
     r = out_a.shape[1]
     _, chunk, width = out_d.shape
     half = r // 2
-    step = 16
-    steps = r // step
-    quarter = g_tokens.shape[0] // 4
     sds = jax.ShapeDtypeStruct
     whole = lambda shape: pl.BlockSpec(shape, lambda i: (0,) * len(shape))
     rows = lambda n, w: pl.BlockSpec((n, w), lambda i: (i, 0))
-    few = lambda n, w, count: pl.BlockSpec((n, w), lambda i: (jnp.minimum(i, count - 1), 0))
     moved = 6 * (out_a.size + out_c.size + out_b.size + out_d.size + out_o.size) + 16 * g_tokens.size
     return pl.pallas_call(
         functools.partial(results_kernel, cfg),
-        grid=(steps,),
+        grid=(2,),
         out_shape=(
             sds((r, 3 * width), F32), sds((r, n_cols(cfg)), F32), sds((r, n_cols(cfg)), F32), sds((2 * chunk, width), F32),
             sds((r, width), F32), sds((cfg["kk"], cfg["kq"], 2 * GROUP), F32), sds((2, 2 * GROUP), F32),
             sds((1, r), F32), sds((1, r), F32), sds((1, r), F32), sds(g_tokens.shape, F32), sds(g_tokens.shape, F32),
         ),
         in_specs=[
-            pl.BlockSpec((GROUP, step, out_a.shape[2]), lambda i: (0, i, 0)),
-            pl.BlockSpec((GROUP, step, out_c.shape[2]), lambda i: (0, i, 0)),
-            pl.BlockSpec((GROUP, step, out_b.shape[2]), lambda i: (0, i, 0)),
-            pl.BlockSpec((1, chunk, width), lambda i: (jnp.minimum(i, 1), 0, 0)),
-            pl.BlockSpec((1, step, width), lambda i: (lax.div(i, half // step), lax.rem(i, half // step), 0)),
+            pl.BlockSpec((GROUP, half, out_a.shape[2]), lambda i: (0, i, 0)),
+            pl.BlockSpec((GROUP, half, out_c.shape[2]), lambda i: (0, i, 0)),
+            pl.BlockSpec((GROUP, half, out_b.shape[2]), lambda i: (0, i, 0)),
+            pl.BlockSpec((1, chunk, width), lambda i: (i, 0, 0)),
+            pl.BlockSpec((1, half, width), lambda i: (i, 0, 0)),
             whole(small.shape),
             whole(line.shape),
-            few(quarter, width, 4),
-            few(quarter, width, 4),
+            rows(g_tokens.shape[0] // 2, width),
+            rows(g_tokens.shape[0] // 2, width),
         ],
         scratch_shapes=[pltpu.VMEM((8, width), F32)],
         out_specs=(
-            rows(step, 3 * width), rows(step, n_cols(cfg)), rows(step, n_cols(cfg)), few(chunk, width, 2), rows(step, width),
+            rows(half, 3 * width), rows(half, n_cols(cfg)), rows(half, n_cols(cfg)), rows(chunk, width), rows(half, width),
             whole((cfg["kk"], cfg["kq"], 2 * GROUP)), whole((2, 2 * GROUP)),
-            whole((1, r)), whole((1, r)), whole((1, r)), few(quarter, width, 4), few(quarter, width, 4),
+            whole((1, r)), whole((1, r)), whole((1, r)), rows(g_tokens.shape[0] // 2, width), rows(g_tokens.shape[0] // 2, width),
         ),
         compiler_params=pltpu.CompilerParams(vmem_limit_bytes=60 * 2**20),
         cost_estimate=pl.CostEstimate(flops=0, bytes_accessed=moved, transcendentals=0),

time: 333 us -> 330 us (level)
  no operation moved by 1% of the time
where the time goes in v6:
time: 330 us; the launch traced here: 329 us
  Pallas kernels  327 us (99%)
    pallas_call x1, Pallas kernels, forward_call(): pl.pallas_call(functools.partial(forward_kernel, cfg), out_shape=(sds(row...  141 us
    pallas_call x1, Pallas kernels, backward_call(): pl.pallas_call(functools.partial(backward_kernel, cfg), out_shape=(sds((l...  106 us
    pallas_call x1, Pallas kernels, feed_call(): pl.pallas_call(functools.partial(feed_kernel, cfg), out_shape=(sds((lengt...  72.4 us
    pallas_call x1, Pallas kernels, results_call(): pl.pallas_call(functools.partial(results_kernel, cfg), grid=(2,), out_sha...  6.64 us

profile of v6, /device:TPU:0, one launch (start us, length us, event | category | flops | bytes accessed | tf_op | source)
XLA Modules:
  0.0 329.3 jit_solution(5884921188638172619)
XLA Ops:
  1.3 1.3 fusion.9.refs_9_
  2.6 141.4 %attention_forward.1 = (bf16[8,256,1536]{2,1,0:T(8,128)(2,1)}, bf16[8,256,1536]{2,1,0:T(8,128)(2,1)}, bf16[16,96,640]{2,1,0:T(8,128)(2,1)}, bf16[16,96,1024]{2,1...) custom-call(bf16[256,1536]{1,0:T(8,128)(2,1)} %bitcast.16, ...), custom_call_target="tpu_custom_call" | custom-call | tf_op jit(solution)/shard_map/attention_forward/pallas_call | solution.py:1132
  144.0 72.4 %feed_forward.1 = (f32[264,1536]{1,0:T(8,128)}, bf16[8,256,1536]{2,1,0:T(8,128)(2,1)}, bf16[1536,1024]{1,0:T(8,128)(2,1)}, bf16[5,256,1536]{2,1,0:T(8,128)(2,1)}) custom-call(bf16[8,256,1536]{2,1,0:T(8,128)(2,1)} %get-tuple-element.50.refs_0_, bf16[8,256,1536]{2,1,0:T(8,128)(2,1)} %get-tuple-element.51.refs_1_, ...), custom_call_target="tpu_custom_call" | custom-call | tf_op jit(solution)/shard_map/feed_forward/pallas_call | solution.py:1344
  216.4 106.1 %attention_backward.1 = (f32[256,1536]{1,0:T(8,128)}, f32[256,1536]{1,0:T(8,128)}, bf16[8,96,256]{2,1,0:T(8,128)(2,1)}, bf16[8,96,384]{2,1,0:T(8,128)(2,1)}, bf1...) custom-call(bf16[8,256,1536]{2,1,0:T(8,128)(2,1)} %get-tuple-element, ...), custom_call_target="tpu_custom_call" | custom-call | tf_op jit(solution)/shard_map/attention_backward/pallas_call | solution.py:1752
  322.5 6.6 %results.1 = (f32[96,4608]{1,0:T(8,128)}, f32[96,4096]{1,0:T(8,128)}, f32[96,4096]{1,0:T(8,128)}, f32[256,1536]{1,0:T(8,128)}, f32[96,1536]{1,0:T(8,128)}, /*ind...) custom-call(bf16[8,96,256]{2,1,0:T(8,128)(2,1)} %get-tuple-element.6, ...), custom_call_target="tpu_custom_call" | custom-call | bytes 17203200 | tf_op jit(solution)/shard_map/results/pallas_call | solution.py:1865

commit v7 on v6

--- a/solution.py
+++ b/solution.py
@@ -1060,7 +1060,7 @@
         def _():
             cots.relay()
 
-        @pl.when(i == 4)
+        @pl.when(i == 5)
         def _():
             spread_d.settle()
             spread_b.settle()
@@ -1574,6 +1574,13 @@
     for cp in gated_in:
         cp.start()
 
+    tokens = GROUP * length
+    for cp in gated_in:
+        cp.wait()
+    value = tn(p_v[...].reshape(tokens, SIDE), gb_v[...].reshape(tokens, width))
+    do_v[...] = value[0 : 2 * dh].astype(BF16).reshape(do_v.shape)
+
+    sum_o.start()
     def taps(at, carry):
         g, a = lax.div(at, taps_q), lax.rem(at, taps_q)
         lanes_at = pl.ds(pl.multiple_of(a * length, length), length)
@@ -1602,25 +1609,18 @@
     for cp in send_s:
         cp.start()
 
-    tokens = GROUP * length
-    for cp in gated_in:
-        cp.wait()
-    value = tn(p_v[...].reshape(tokens, SIDE), gb_v[...].reshape(tokens, width))
-    do_v[...] = value[0 : 2 * dh].astype(BF16).reshape(do_v.shape)
-
-    sum_o.start()
     for m in range(2 * planes):
-        i, first_part = m % planes, m < planes
+        i, narrow = m % planes, m >= planes
         nrm_copy(m).wait()
-        at = slice(0, SIDE) if first_part else slice(SIDE, QKV)
+        at = slice(0, SIDE) if narrow else slice(SIDE, QKV)
         value = tn(nrm_v[m % 2].reshape(tokens, span), gq_v[:, :, at].reshape(tokens, at.stop - at.start))
-        terms = da_v if first_part else dc_v
+        terms = da_v if narrow else dc_v
         terms[pl.ds(turn_of(i) * PLANE, PLANE)] = value.astype(BF16).reshape((PLANE,) + terms.shape[1:])
         if m + 2 < 2 * planes:
             nrm_copy(m + 2).start()
     for way in (True, False):
+        sum_c.start((way,))
         sum_a.start((way,))
-        sum_c.start((way,))
     scatter.turn()
     sum_b.total(sb_v.at[pl.ds(FIRST, PLANE - FIRST)], sb_v.at[pl.ds(FIRST, PLANE - FIRST)])
     b_cps = group_copies(0, lambda sl: sb_v.at[sl], out_b, (FIRST, PLANE))
@@ -1633,9 +1633,9 @@
     small_cps = group_copies(2, lambda sl: small_v, out_small)
 
     sum_o.combine(lambda t: do_v.at[pl.ds(t, 1)])
+    sum_c.combine(lambda t: dc_v.at[pl.ds(t * PLANE, PLANE)])
+
     sum_a.combine(lambda t: da_v.at[pl.ds(t * PLANE, PLANE)])
-
-    sum_c.combine(lambda t: dc_v.at[pl.ds(t * PLANE, PLANE)])
 
     layer.arrive()
 
@@ -1692,11 +1692,11 @@
                 act_here(o_here)
 
     o_each(lambda cp: cp.start(), lambda cp: cp.start())
+    sum_c.total(sc_v, dc_v.at[pl.ds(me.g * PLANE, PLANE)])
+    c_cps = group_copies(5, lambda sl: sc_v.at[sl], out_c)
+
     sum_a.total(sa_v, da_v.at[pl.ds(me.g * PLANE, PLANE)])
     a_cps = group_copies(1, lambda sl: sa_v.at[sl], out_a)
-
-    sum_c.total(sc_v, dc_v.at[pl.ds(me.g * PLANE, PLANE)])
-    c_cps = group_copies(5, lambda sl: sc_v.at[sl], out_c)
 
     for cp in send_l:
         cp.wait_recv()
@@ -1720,8 +1720,8 @@
             remote(out_o.at[h], out_o.at[h], t_send.at[4, 0], t_recv.at[4, h], me.sib).wait_recv()
 
     o_each(lambda cp: cp.wait_send(), lambda cp: cp.wait())
+    group_wait(5, c_cps, out_c)
     group_wait(1, a_cps, out_a)
-    group_wait(5, c_cps, out_c)
     group_wait(6, line_cps, out_line)
     for group in (sum_b, sum_a, sum_c, sum_o):
         group.finish()

time: 330 us -> 329 us (level)
  no operation moved by 1% of the time
where the time goes in v7:
time: 329 us; the launch traced here: 328 us
  Pallas kernels  325 us (99%)
    pallas_call x1, Pallas kernels, forward_call(): pl.pallas_call(functools.partial(forward_kernel, cfg), out_shape=(sds(row...  141 us
    pallas_call x1, Pallas kernels, backward_call(): pl.pallas_call(functools.partial(backward_kernel, cfg), out_shape=(sds((l...  105 us
    pallas_call x1, Pallas kernels, feed_call(): pl.pallas_call(functools.partial(feed_kernel, cfg), out_shape=(sds((lengt...  72.4 us
    pallas_call x1, Pallas kernels, results_call(): pl.pallas_call(functools.partial(results_kernel, cfg), grid=(2,), out_sha...  6.64 us

profile of v7, /device:TPU:0, one launch (start us, length us, event | category | flops | bytes accessed | tf_op | source)
XLA Modules:
  0.0 328.2 jit_solution(7035124707039559570)
XLA Ops:
  1.3 1.3 fusion.9.refs_9_
  2.6 141.4 %attention_forward.1 = (bf16[8,256,1536]{2,1,0:T(8,128)(2,1)}, bf16[8,256,1536]{2,1,0:T(8,128)(2,1)}, bf16[16,96,640]{2,1,0:T(8,128)(2,1)}, bf16[16,96,1024]{2,1...) custom-call(bf16[256,1536]{1,0:T(8,128)(2,1)} %bitcast.16, ...), custom_call_target="tpu_custom_call" | custom-call | tf_op jit(solution)/shard_map/attention_forward/pallas_call | solution.py:1132
  144.0 72.4 %feed_forward.1 = (f32[264,1536]{1,0:T(8,128)}, bf16[8,256,1536]{2,1,0:T(8,128)(2,1)}, bf16[1536,1024]{1,0:T(8,128)(2,1)}, bf16[5,256,1536]{2,1,0:T(8,128)(2,1)}) custom-call(bf16[8,256,1536]{2,1,0:T(8,128)(2,1)} %get-tuple-element.50.refs_0_, bf16[8,256,1536]{2,1,0:T(8,128)(2,1)} %get-tuple-element.51.refs_1_, ...), custom_call_target="tpu_custom_call" | custom-call | tf_op jit(solution)/shard_map/feed_forward/pallas_call | solution.py:1344
  216.4 105.0 %attention_backward.1 = (f32[256,1536]{1,0:T(8,128)}, f32[256,1536]{1,0:T(8,128)}, bf16[8,96,256]{2,1,0:T(8,128)(2,1)}, bf16[8,96,384]{2,1,0:T(8,128)(2,1)}, bf1...) custom-call(bf16[8,256,1536]{2,1,0:T(8,128)(2,1)} %get-tuple-element, ...), custom_call_target="tpu_custom_call" | custom-call | tf_op jit(solution)/shard_map/attention_backward/pallas_call | solution.py:1752
  321.4 6.6 %results.1 = (f32[96,4608]{1,0:T(8,128)}, f32[96,4096]{1,0:T(8,128)}, f32[96,4096]{1,0:T(8,128)}, f32[256,1536]{1,0:T(8,128)}, f32[96,1536]{1,0:T(8,128)}, /*ind...) custom-call(bf16[8,96,256]{2,1,0:T(8,128)(2,1)} %get-tuple-element.6, ...), custom_call_target="tpu_custom_call" | custom-call | bytes 17203200 | tf_op jit(solution)/shard_map/results/pallas_call | solution.py:1865

commit v8 on v7

--- a/solution.py
+++ b/solution.py
@@ -1300,11 +1300,12 @@
     branch = Gather(me, ct_v.at[me.slot], branch_all, g_send, g_recv, g_loc.at[0])
     branch.start()
 
-    lax.fori_loop(0, GROUP, output, 0)
+    down_sum.combine(lambda t: dd_v.at[pl.ds(t, 1)])
+    lax.fori_loop(0, GROUP // 2, output, 0)
+    branch.relay()
+    lax.fori_loop(GROUP // 2, GROUP, output, 0)
     red_out = pltpu.make_async_copy(o_red, out_red.at[pl.ds(0, 4)], out_sem.at[2])
     red_out.start()
-    down_sum.combine(lambda t: dd_v.at[pl.ds(t, 1)])
-    branch.relay()
     first_sum.combine(lambda t: first_v.at[t])
     branch.share()
     branch.last()

time: 329 us -> 329 us (level)
  no operation moved by 1% of the time
where the time goes in v8:
time: 329 us; the launch traced here: 328 us
  Pallas kernels  325 us (99%)
    pallas_call x1, Pallas kernels, forward_call(): pl.pallas_call(functools.partial(forward_kernel, cfg), out_shape=(sds(row...  141 us
    pallas_call x1, Pallas kernels, backward_call(): pl.pallas_call(functools.partial(backward_kernel, cfg), out_shape=(sds((l...  105 us
    pallas_call x1, Pallas kernels, feed_call(): pl.pallas_call(functools.partial(feed_kernel, cfg), out_shape=(sds((lengt...  72.4 us
    pallas_call x1, Pallas kernels, results_call(): pl.pallas_call(functools.partial(results_kernel, cfg), grid=(2,), out_sha...  6.64 us

profile of v8, /device:TPU:0, one launch (start us, length us, event | category | flops | bytes accessed | tf_op | source)
XLA Modules:
  0.0 328.2 jit_solution(9018197422176327869)
XLA Ops:
  1.3 1.3 fusion.9.refs_9_
  2.6 141.4 %attention_forward.1 = (bf16[8,256,1536]{2,1,0:T(8,128)(2,1)}, bf16[8,256,1536]{2,1,0:T(8,128)(2,1)}, bf16[16,96,640]{2,1,0:T(8,128)(2,1)}, bf16[16,96,1024]{2,1...) custom-call(bf16[256,1536]{1,0:T(8,128)(2,1)} %bitcast.16, ...), custom_call_target="tpu_custom_call" | custom-call | tf_op jit(solution)/shard_map/attention_forward/pallas_call | solution.py:1132
  144.0 72.4 %feed_forward.1 = (f32[264,1536]{1,0:T(8,128)}, bf16[8,256,1536]{2,1,0:T(8,128)(2,1)}, bf16[1536,1024]{1,0:T(8,128)(2,1)}, bf16[5,256,1536]{2,1,0:T(8,128)(2,1)}) custom-call(bf16[8,256,1536]{2,1,0:T(8,128)(2,1)} %get-tuple-element.50.refs_0_, bf16[8,256,1536]{2,1,0:T(8,128)(2,1)} %get-tuple-element.51.refs_1_, ...), custom_call_target="tpu_custom_call" | custom-call | tf_op jit(solution)/shard_map/feed_forward/pallas_call | solution.py:1345
  216.4 105.0 %attention_backward.1 = (f32[256,1536]{1,0:T(8,128)}, f32[256,1536]{1,0:T(8,128)}, bf16[8,96,256]{2,1,0:T(8,128)(2,1)}, bf16[8,96,384]{2,1,0:T(8,128)(2,1)}, bf1...) custom-call(bf16[8,256,1536]{2,1,0:T(8,128)(2,1)} %get-tuple-element, ...), custom_call_target="tpu_custom_call" | custom-call | tf_op jit(solution)/shard_map/attention_backward/pallas_call | solution.py:1753
  321.4 6.6 %results.1 = (f32[96,4608]{1,0:T(8,128)}, f32[96,4096]{1,0:T(8,128)}, f32[96,4096]{1,0:T(8,128)}, f32[256,1536]{1,0:T(8,128)}, f32[96,1536]{1,0:T(8,128)}, /*ind...) custom-call(bf16[8,96,256]{2,1,0:T(8,128)(2,1)} %get-tuple-element.6, ...), custom_call_target="tpu_custom_call" | custom-call | bytes 17203200 | tf_op jit(solution)/shard_map/results/pallas_call | solution.py:1866
